TPU v7x, 32 devices: a whole 2x2x4 slice. The times are simulated.
32 devices in a mesh: seq: 8 (over z, y), tp: 4 (over x, core).
Axes of the slice: x: 2, y: 2, z: 4, core: 2. Of those that a mesh axis runs over, the one named last changes fastest.
Arguments:
- tokens: bfloat16 [4, 4096, 1024], P(None, 'seq'), may hold values from -6 to 6
- lengths: int32 [4], replicated, may hold values from 1024 to 4096, as said below
- gain_mix: float32 [1024], replicated, may hold values from 0.25 to 1.75
- w_in: bfloat16 [1024, 3, 1024], P(None, None, 'tp'), may hold values from -0.1875 to 0.1875
- conv_weight: float32 [3, 1024], P(None, 'tp'), may hold values from -3.5 to 3.5
- w_out: bfloat16 [1024, 1024], P('tp'), may hold values from -0.1875 to 0.1875
- gain_ffn: float32 [1024], replicated, may hold values from 0.25 to 1.75
- w_gate: bfloat16 [1024, 4608], P(None, 'tp'), may hold values from -0.1875 to 0.1875
- w_up: bfloat16 [1024, 4608], P(None, 'tp'), may hold values from -0.1875 to 0.1875
- w_down: bfloat16 [4608, 1024], P('tp'), may hold values from -0.125 to 0.125
- cotangent: bfloat16 [4, 4096, 1024], P(None, 'seq'), may hold values from -6 to 6
Outputs:
- block_out: bfloat16 [4, 4096, 1024], P(None, 'seq')
- grad_tokens: float32 [4, 4096, 1024], P(None, 'seq')
- grad_gain_mix: float32 [1024], replicated
- grad_w_in: float32 [1024, 3, 1024], P(None, None, 'tp')
- grad_conv: float32 [3, 1024], P(None, 'tp')
- grad_w_out: float32 [1024, 1024], P('tp')
- grad_gain_ffn: float32 [1024], replicated
- grad_w_gate: float32 [1024, 4608], P(None, 'tp')
- grad_w_up: float32 [1024, 4608], P(None, 'tp')
- grad_w_down: float32 [4608, 1024], P('tp')
Inputs may be any that keep to these rules, and one draw needn't show every extreme that they name: Each slot holds one sequence in its first lengths[s] positions, the rest is padding; in every draw one slot is full, 4096 tokens.
All inputs are finite; a program needn't handle non-finite values.
Results may differ from a plain program's by a relative error of at most 0.0092.
Values sent between devices are 32-bit elements; how exact they have to be, the bound alone decides.
A program may use at most 192 MiB of HBM per device.

v0:
```python
import jax
import jax.numpy as jnp
from jax import lax
from jax.sharding import PartitionSpec as P

NORM_EPS = 1e-05


def from_behind(block, axis, distance):
    devices = range(lax.axis_size(axis))
    route = [(i - distance, i) for i in devices if i - distance in devices]
    return lax.ppermute(block, axis, route)


def rms_scale(values):
    return lax.rsqrt(jnp.mean(values * values, axis=-1, keepdims=True) + NORM_EPS)


def contract_rows(left, right):
    return lax.dot_general(
        left, right, (((0,), (0,)), ((), ())), preferred_element_type=jnp.float32
    )


def contract_cols(left, right):
    return lax.dot_general(
        left, right, (((1,), (1,)), ((), ())), preferred_element_type=jnp.float32
    )


def per_device(
    tokens, lengths, gain_mix, w_in, conv_weight, w_out, gain_ffn, w_gate, w_up, w_down, cotangent
):
    slot_count, local_len, model_width = tokens.shape
    local_chans = w_in.shape[2]
    row_count = slot_count * local_len
    first_pos = lax.axis_index("seq") * local_len
    positions = first_pos + jnp.arange(local_len, dtype=jnp.int32)
    valid_mask = (positions[None, :] < lengths[:, None]).astype(jnp.float32)[:, :, None]
    valid_rows = valid_mask.reshape(row_count, 1)
    inputs_f = tokens.astype(jnp.float32).reshape(row_count, model_width)
    scale_mix = rms_scale(inputs_f)
    unit_mix = inputs_f * scale_mix
    normed_in = (gain_mix * unit_mix).astype(jnp.bfloat16)
    w_in_flat = w_in.reshape(model_width, 3 * local_chans)
    projected = jnp.dot(normed_in, w_in_flat, preferred_element_type=jnp.float32)
    in_gate = projected[:, :local_chans]
    out_gate = projected[:, local_chans : 2 * local_chans]
    conv_value = projected[:, 2 * local_chans :]
    gated_seq = (valid_rows * in_gate * conv_value).reshape(slot_count, local_len, local_chans)
    carried = from_behind(gated_seq[:, local_len - 2 :, :], "seq", 1)
    padded_seq = jnp.concatenate([carried, gated_seq], axis=1)
    conv_sum = (
        conv_weight[0] * padded_seq[:, 0:local_len]
        + conv_weight[1] * padded_seq[:, 1 : local_len + 1]
        + conv_weight[2] * padded_seq[:, 2 : local_len + 2]
    ).reshape(row_count, local_chans)
    mixed_seq = (out_gate * conv_sum).astype(jnp.bfloat16)
    mixer_part = jnp.dot(mixed_seq, w_out, preferred_element_type=jnp.float32)
    mixer_out = lax.psum(mixer_part, "tp")
    hidden_res = inputs_f + mixer_out
    scale_ffn = rms_scale(hidden_res)
    unit_ffn = hidden_res * scale_ffn
    normed_mid = (gain_ffn * unit_ffn).astype(jnp.bfloat16)
    gate_proj = jnp.dot(normed_mid, w_gate, preferred_element_type=jnp.float32)
    up_proj = jnp.dot(normed_mid, w_up, preferred_element_type=jnp.float32)
    sigmoid_gate = jax.nn.sigmoid(gate_proj)
    silu_gate = gate_proj * sigmoid_gate
    activated = (silu_gate * up_proj).astype(jnp.bfloat16)
    ffn_part = jnp.dot(activated, w_down, preferred_element_type=jnp.float32)
    ffn_out = lax.psum(ffn_part, "tp")
    block_out = (
        (valid_rows * (hidden_res + ffn_out))
        .astype(jnp.bfloat16)
        .reshape(slot_count, local_len, model_width)
    )
    grad_out = valid_rows * cotangent.astype(jnp.float32).reshape(row_count, model_width)
    grad_ffn = grad_out.astype(jnp.bfloat16)
    grad_act = contract_cols(grad_ffn, w_down)
    grad_w_down = contract_rows(activated, grad_ffn)
    silu_slope = sigmoid_gate * (1.0 + gate_proj * (1.0 - sigmoid_gate))
    grad_gate = (grad_act * up_proj * silu_slope).astype(jnp.bfloat16)
    grad_up = (grad_act * silu_gate).astype(jnp.bfloat16)
    grad_w_gate = contract_rows(normed_mid, grad_gate)
    grad_w_up = contract_rows(normed_mid, grad_up)
    mid_part = contract_cols(grad_gate, w_gate) + contract_cols(grad_up, w_up)
    grad_mid = lax.psum(mid_part, "tp")
    grad_gain_ffn = jnp.sum(grad_mid * unit_ffn, axis=0)
    scaled_mid = gain_ffn * grad_mid
    grad_hidden = grad_out + scale_ffn * (
        scaled_mid - unit_ffn * jnp.mean(scaled_mid * unit_ffn, axis=-1, keepdims=True)
    )
    ffn_totals = (grad_gain_ffn, grad_w_gate, grad_w_up, grad_w_down)
    grad_mixer = grad_hidden.astype(jnp.bfloat16)
    grad_w_out = contract_rows(mixed_seq, grad_mixer)
    grad_mixed = contract_cols(grad_mixer, w_out)
    grad_out_gate = grad_mixed * conv_sum
    grad_conv_in = (grad_mixed * out_gate).reshape(slot_count, local_len, local_chans)
    next_grad = from_behind(grad_conv_in[:, :2, :], "seq", -1)
    extended = jnp.concatenate([grad_conv_in, next_grad], axis=1)
    grad_gated = (
        conv_weight[2] * extended[:, 0:local_len]
        + conv_weight[1] * extended[:, 1 : local_len + 1]
        + conv_weight[0] * extended[:, 2 : local_len + 2]
    ).reshape(row_count, local_chans)
    grad_conv = jnp.stack(
        [
            jnp.sum(grad_conv_in * padded_seq[:, tap : tap + local_len], axis=(0, 1))
            for tap in range(3)
        ],
        axis=0,
    )
    grad_in_gate = grad_gated * valid_rows * conv_value
    grad_value = grad_gated * valid_rows * in_gate
    grad_proj = jnp.concatenate([grad_in_gate, grad_out_gate, grad_value], axis=1).astype(
        jnp.bfloat16
    )
    grad_w_in = contract_rows(normed_in, grad_proj).reshape(model_width, 3, local_chans)
    in_part = contract_cols(grad_proj, w_in_flat)
    grad_in = lax.psum(in_part, "tp")
    grad_gain_mix = jnp.sum(grad_in * unit_mix, axis=0)
    scaled_in = gain_mix * grad_in
    grad_tokens = grad_hidden + scale_mix * (
        scaled_in - unit_mix * jnp.mean(scaled_in * unit_mix, axis=-1, keepdims=True)
    )
    grad_tokens = grad_tokens.reshape(slot_count, local_len, model_width)
    summed_all = lax.psum(
        (
            grad_gain_mix,
            grad_w_in,
            grad_conv,
            grad_w_out,
            ffn_totals[0],
            ffn_totals[1],
            ffn_totals[2],
            ffn_totals[3],
        ),
        "seq",
    )
    (
        total_gain_mix,
        total_w_in,
        total_conv,
        total_w_out,
        total_gain_ffn,
        total_w_gate,
        total_w_up,
        total_w_down,
    ) = summed_all
    return (
        block_out,
        grad_tokens,
        total_gain_mix,
        total_w_in,
        total_conv,
        total_w_out,
        total_gain_ffn,
        total_w_gate,
        total_w_up,
        total_w_down,
    )


def solution(mesh):
    placed = (
        P(None, "seq", None),
        P(),
        P(),
        P(None, None, "tp"),
        P(None, "tp"),
        P("tp", None),
        P(),
        P(None, "tp"),
        P(None, "tp"),
        P("tp", None),
        P(None, "seq", None),
    )
    return jax.shard_map(
        per_device,
        mesh=mesh,
        in_specs=placed,
        out_specs=(
            P(None, "seq", None),
            P(None, "seq", None),
            P(),
            P(None, None, "tp"),
            P(None, "tp"),
            P("tp", None),
            P(),
            P(None, "tp"),
            P(None, "tp"),
            P("tp", None),
        ),
        check_vma=False,
    )
```

profile of v0, /device:TPU:0, one launch (start us, length us, event | category | flops | bytes accessed | tf_op | source)
XLA Modules:
  0.0 1310.2 jit_solution(7344457047982589889)
XLA Ops:
  21.2 4.9 collective-permute-start
  35.2 4.9 fusion.2
  40.1 150.0 %all-reduce.8.cloned.1.call-done = f32[2048,1024]{1,0:T(8,128)} async-done(((f32[2048,1024]{1,0:T(8,128)}), f32[2048,1024]{1,0:T(8,128)}) %all-reduce.8.cloned.1.call-update) | async-done | bytes 8388624 | tf_op jit(solution)/shard_map/psum | solution.py:60
  190.1 5.7 multiply_reduce_fusion.2
  199.5 7.9 fusion.34
  207.5 7.9 fusion.33
  215.4 16.8 %multiply_convert_fusion = (bf16[2048,1152]{1,0:T(8,128)(2,1)}, bf16[2048,1152]{1,0:T(8,128)(2,1)}, bf16[2048,1152]{1,0:T(8,128)(2,1)}) fusion(f32[2048,1152]{1,0:T(8,128)} %fusion.33, f32[2048,1152]{1,0:T(8,128)} %fusion.34, bf16[2048,1024]{1,0:T(8,128)(2,1)S(1)} %copy-done.18, bf16[1152,1024]{1,0:T(8,128)(2,1)S(1)} %copy-done), kind=kOutput, calls=%fused_computation | convolution fusion | flops 4867227648 | bytes 39583744 | tf_op jit(solution)/shard_map/dot_general | solution.py:26
  232.2 8.4 fusion.36
  240.6 8.3 convolution_add_fusion
  248.9 10.5 fusion.35
  259.4 142.7 %all-reduce.10.cloned.1.call-done = f32[2048,1024]{1,0:T(8,128)} async-done(((f32[2048,1024]{1,0:T(8,128)}), f32[2048,1024]{1,0:T(8,128)}) %all-reduce.10.cloned.1.call-update) | async-done | bytes 8388624 | tf_op jit(solution)/shard_map/psum | solution.py:87
  402.1 7.0 multiply_reduce_fusion
  410.3 6.3 fusion.1
  428.2 5.6 fusion.27
  433.9 10.1 fusion.40
  444.1 9.9 fusion.39
  454.0 7.5 fusion.38
  465.5 4.9 copy.24
  470.4 8.3 fusion.37
  483.2 239.8 %all-reduce.14.cloned.1.call-done = (f32[2048,1024]{1,0:T(8,128)}, f32[2048,1024]{1,0:T(8,128)}) async-done(((f32[2048,1024]{1,0:T(8,128)}, f32[2048,1024]{1,0:T(8,128)}), (f32[2048,1024]{1,0:T(8,128)}, f32[2048,1024]{1,0:T(8,128)})) %all-reduce.14.cloned.1.call-update) | async-done | bytes 16777232 | tf_op jit(solution)/shard_map/psum | solution.py:71
  723.0 5.8 fusion.10
  728.8 39.2 %all-reduce = (f32[1024]{0:T(1024)}, f32[3,256]{1,0:T(4,128)}, f32[1024]{0:T(1024)}) all-reduce(f32[1024]{0:T(1024)S(1)} %get-tuple-element.12, f32[3,256]{1,0:T(4,128)S(1)} %pad_maximum_fusion.4, f32[1024]{0:T(1024)S(1)} %get-tuple-element.10), channel_id=1, replica_groups=mesh['seq'=8,'tp'=4] {'seq'}, use_global_device_ids=true, to_apply=%region_9.0 | all-reduce | flops 2816 | bytes 22528 | tf_op jit(solution)/shard_map/psum | solution.py:127
  768.0 18.5 %fusion.9 = (f32[2048,1024]{1,0:T(8,128)}, bf16[2048,1024]{1,0:T(8,128)(2,1)}) fusion(f32[2048,1024]{1,0:T(8,128)} %copy-done.3, bf16[4,512,1024]{2,1,0:T(8,128)(2,1)} %param.11, f32[2048,1024]{1,0:T(8,128)} %get-tuple-element.25, f32[2048]{0:T(1024)S(1)} %broadcast_multiply_fusion, f32[1024]{0:T(1024)S(1)} %copy-done.30, f32[2048]{0:T(1024)S(1)} %bitcast.114, ...), kind=kLoop, calls=%fused_computation.18 | loop fusion | flops 20971520 | bytes 50360320 | tf_op jit(solution)/shard_map/add | solution.py:123
  786.6 503.2 %all-reduce.12.cloned.1.call-done = (f32[1024,3,256]{2,0,1:T(8,128)}, f32[256,1024]{1,0:T(8,128)}, f32[1024,1152]{1,0:T(8,128)}, f32[1024,1152]{1,0:T(8,128)}, f32[1152,1024]{1,0:T(8,128)}) async-done(((f32[1024,3,256]{2,0,1:T(8,128)}, f32[256,1024]{1,0:T(8,128)}, f32[1024,1152]{1,0:T(8,128)}, f32[1024,1152]{1,0:T(8,128)}, f32[1152,1024]{1,0:T(8,128)}), (f32[1024,3,256]{2,0,1:T(8,128)}, ...) | async-done | bytes 18350096 | tf_op jit(solution)/shard_map/psum | solution.py:127
  (138 shorter events, 61.5 us)
Async XLA Ops:
  7.2 208.2 %copy-start = (bf16[1152,1024]{1,0:T(8,128)(2,1)S(1)}, bf16[1152,1024]{1,0:T(8,128)(2,1)}, u32[]{:S(2)}) copy-start(bf16[1152,1024]{1,0:T(8,128)(2,1)} %param.20) | copy-start | bytes 7077892
  7.2 7.2 copy-start.29
  7.2 182.9 %all-reduce.8.cloned.1.call-start = ((), (), s32[]{:S(2)}) async-start(), calls=%async_computation | async-start | bytes 16777216 | tf_op jit(solution)/shard_map/psum | solution.py:60
  20.9 7.2 copy-start.4
  21.2 6.2 collective-permute-start
  35.1 366.9 %all-reduce.10.cloned.1.call-start = ((), (), s32[]{:S(2)}) async-start(), calls=%async_computation.1 | async-start | bytes 16777216 | tf_op jit(solution)/shard_map/psum | solution.py:87
  40.1 155.8 %copy-start.28 = (f32[1024]{0:T(1024)S(1)}, f32[1024]{0:T(1024)}, u32[]{:S(2)}) copy-start(f32[1024]{0:T(1024)} %param.17) | copy-start | bytes 12292
  199.5 7.9 copy-start.16
  199.5 7.9 copy-start.33
  207.4 7.9 copy-start.18
  232.2 8.4 copy-start.35
  232.2 8.4 copy-start.36
  248.9 474.1 %all-reduce.14.cloned.1.call-start = ((), (), s32[]{:S(2)}) async-start(), calls=%async_computation.3 | async-start | bytes 33554432 | tf_op jit(solution)/shard_map/psum | solution.py:71
  402.1 8.2 copy-start.5
  402.1 14.5 %slice-start.2 = ((s8[6291456]{0:T(1024)(128)(4,1)}), s8[4194304]{0:T(1024)(128)(4,1)S(1)}, s32[]{:S(2)}) async-start(s8[6291456]{0:T(1024)(128)(4,1)} %bitcast.91), calls=%async_computation.6 | async-start | bytes 8388608
  420.4 5.5 collective-permute-start.1
  433.9 855.9 %all-reduce.12.cloned.1.call-start = ((), (), s32[]{:S(2)}) async-start(), calls=%async_computation.2 | async-start | bytes 36700160 | tf_op jit(solution)/shard_map/psum | solution.py:127
  433.9 10.1 copy-start.17
  433.9 20.1 %slice-start.6 = ((s8[4718592]{0:T(1024)(128)(4,1)}), s8[4194304]{0:T(1024)(128)(4,1)S(1)}, s32[]{:S(2)}) async-start(s8[4718592]{0:T(1024)(128)(4,1)} %bitcast.124), calls=%async_computation.10 | async-start | bytes 8388608
  444.1 9.9 slice-start.7
  444.1 17.4 %slice-start = ((s8[8388608]{0:T(1024)(128)(4,1)}), s8[4194304]{0:T(1024)(128)(4,1)S(1)}, s32[]{:S(2)}) async-start(s8[8388608]{0:T(1024)(128)(4,1)} %bitcast.89), calls=%async_computation.4 | async-start | bytes 8388608
  454.0 7.5 slice-start.1
  454.0 7.5 copy-start.13
  478.8 244.2 %copy-start.30 = (f32[1024]{0:T(1024)S(1)}, f32[1024]{0:T(1024)}, u32[]{:S(2)}) copy-start(f32[1024]{0:T(1024)} %param.13) | copy-start | bytes 12292
  (27 other events, 96.4 us)
Sparse Core Ops, SparseCore 0:
  35.2 154.8 all-reduce.7
  249.0 153.0 all-reduce.9
  434.0 288.9 all-reduce.13
  729.2 560.5 all-reduce.11
where the time goes:
time: 1320 us; the launch traced here: 1310 us
  waiting for transfers between devices  1040 us (79%)
  matrix products  115 us (9%)
  other arithmetic  64.3 us (5%)
  blocking collectives  39.2 us (3%)
  local copies, waits for them, and re-layouts  30 us (2%)
  between operations  14.5 us (1%)
    psum x1, waiting for transfers between devices, per_device(): lax.psum((grad_gain_mix, grad_w_in, grad_conv, grad_w_out, ffn_totals[0],...  503 us
    psum x1, waiting for transfers between devices, per_device(): ffn_out = lax.psum(ffn_part, 'tp')  240 us
    psum x1, waiting for transfers between devices, per_device(): mixer_out = lax.psum(mixer_part, 'tp')  150 us
    psum x1, waiting for transfers between devices, per_device(): grad_mid = lax.psum(mid_part, 'tp')  143 us
    dot_general x5, matrix products, contract_cols(): lax.dot_general(left, right, (((1,), (1,)), ((), ())), preferred_element_...  42.3 us
    psum x1, blocking collectives, per_device(): lax.psum((grad_gain_mix, grad_w_in, grad_conv, grad_w_out, ffn_totals[0],...  39.2 us
    dot_general x5, matrix products, contract_rows(): lax.dot_general(left, right, (((0,), (0,)), ((), ())), preferred_element_...  38.1 us
  transfers between devices with their start and end apart: 6, of which 6 were waited for; matrix products, arithmetic and copies ran while one was open for 7% of the time, Pallas kernels for 0%

commit v1 on v0

v1 whole, which is shorter than its diff:
```python
import functools

import jax
import jax.numpy as jnp
from jax import lax
from jax.experimental import pallas as pl
from jax.experimental.pallas import tpu as pltpu
from jax.sharding import PartitionSpec as P

NORM_EPS = 1e-05
LANES = 128
HALF = 128
SLOTS_IN_FLIGHT = 10


def rms_scale(values):
    return lax.rsqrt(jnp.mean(values * values, axis=-1, keepdims=True) + NORM_EPS)


def dot_rows(left, right):
    return lax.dot_general(
        left, right, (((0,), (0,)), ((), ())), preferred_element_type=jnp.float32
    )


def dot_cols(left, right):
    return lax.dot_general(
        left, right, (((1,), (1,)), ((), ())), preferred_element_type=jnp.float32
    )


def shift_seq(block, distance):
    count = lax.axis_size("seq")
    route = [(i - distance, i) for i in range(count) if 0 <= i - distance < count]
    return lax.ppermute(block, "seq", route)


def swap_tp(block, bit):
    return lax.ppermute(block, "tp", [(i, i ^ bit) for i in range(lax.axis_size("tp"))])


class SeqSum:
    def __init__(self, places, own, out, scratch):
        self.places, self.own, self.out = places, own, out
        self.y_in, self.p_left, self.p_right, self.p_acc = scratch[0:4]
        self.q_left, self.q_right, self.q_acc, self.q_in = scratch[4:8]
        self.sems = scratch[8]
        here = lax.axis_index("seq")
        self.place, self.side = here // 2, here % 2

    def greet(self):
        barrier = pltpu.get_barrier_semaphore()
        place, side = self.place, self.side

        def signal(index):
            pl.semaphore_signal(
                barrier, inc=1, device_id={"seq": index}, device_id_type=pl.DeviceIdType.MESH
            )

        signal(place * 2 + 1 - side)

        @pl.when(place > 0)
        def _():
            signal((place - 1) * 2 + side)

        @pl.when(place < self.places - 1)
        def _():
            signal((place + 1) * 2 + side)

        ends = jnp.where(place > 0, 1, 0) + jnp.where(place < self.places - 1, 1, 0)
        pl.semaphore_wait(barrier, 1 + ends)

    def remote(self, src, dst, slot, send, recv, place, side):
        return pltpu.make_async_remote_copy(
            src_ref=src,
            dst_ref=dst,
            send_sem=self.sems.at[send, slot],
            recv_sem=self.sems.at[recv, slot],
            device_id={"seq": place * 2 + side},
            device_id_type=pl.DeviceIdType.MESH,
        )

    def chain(self, root):
        last = self.places - 1
        left = jnp.maximum(self.place - 1, 0)
        right = jnp.minimum(self.place + 1, last)
        from_left = (self.place <= root) & (self.place > 0)
        from_right = (self.place >= root) & (self.place < last)
        return left, right, from_left, from_right

    def p_stage(self, which, k):
        place, side = self.place, self.side
        own, out = self.own, self.out
        slot = lax.rem(k, SLOTS_IN_FLIGHT)
        base = pl.multiple_of(k * 4 * HALF, 4 * HALF)
        mine = pl.ds(pl.multiple_of(base + side * HALF, HALF), HALF)
        theirs = pl.ds(pl.multiple_of(base + (1 - side) * HALF, HALF), HALF)
        root = self.places // 2 - 1 + lax.rem(k, 2)
        left, right, from_left, from_right = self.chain(root)
        acc, y_in = self.p_acc.at[slot], self.y_in.at[slot]
        from_l, from_r = self.p_left.at[slot], self.p_right.at[slot]
        remote = functools.partial(functools.partial, self.remote)

        to_side = remote(own.at[theirs], y_in, slot, 0, 1, place, 1 - side)
        up_right = remote(acc, from_l, slot, 2, 3, right, side)
        up_left = remote(acc, from_r, slot, 2, 4, left, side)

        def down(src):
            return (
                remote(src, out.at[mine], slot, 5, 7, left, side),
                remote(src, out.at[mine], slot, 6, 7, right, side),
                remote(src, out.at[mine], slot, 8, 9, place, 1 - side),
            )

        def keep():
            return pltpu.make_async_copy(acc, out.at[mine], self.sems.at[10, slot])

        def hand_down(src):
            down_left, down_right, down_side = down(src)
            down_side().start()
            pl.when(from_left)(lambda: down_left().start())
            pl.when(from_right)(lambda: down_right().start())

        if which == "split":
            to_side().start()

        if which == "up":
            to_side().wait_recv()
            acc[...] = own[mine, :] + y_in[...]

            @pl.when(place < root)
            def _():
                @pl.when(from_left)
                def _():
                    up_right().wait_recv()
                    acc[...] += from_l[...]

                up_right().start()

            @pl.when(place > root)
            def _():
                @pl.when(from_right)
                def _():
                    up_left().wait_recv()
                    acc[...] += from_r[...]

                up_left().start()

        if which == "root":

            @pl.when(place == root)
            def _():
                @pl.when(from_left)
                def _():
                    up_right().wait_recv()
                    acc[...] += from_l[...]

                @pl.when(from_right)
                def _():
                    up_left().wait_recv()
                    acc[...] += from_r[...]

                hand_down(acc)
                keep().start()

        if which == "down":

            @pl.when(place != root)
            def _():
                down(acc)[0]().wait_recv()
                hand_down(out.at[mine])

        if which == "end":
            down_left, down_right, down_side = down(acc)
            down_side().wait()
            to_side().wait_send()
            pl.when(from_left)(lambda: down_left().wait_send())
            pl.when(from_right)(lambda: down_right().wait_send())
            pl.when(place == root)(lambda: keep().wait())
            pl.when(place != root)(lambda: up_left().wait_send())

    def q_stage(self, which, k):
        place, side = self.place, self.side
        own, out = self.own, self.out
        slot = lax.rem(k, SLOTS_IN_FLIGHT)
        base = pl.multiple_of(k * 4 * HALF, 4 * HALF)
        wide = pl.ds(pl.multiple_of(base + 2 * HALF, 2 * HALF), 2 * HALF)
        root = self.places // 2 - lax.rem(k, 2)
        left, right, from_left, from_right = self.chain(root)
        acc, side_in = self.q_acc.at[slot], self.q_in.at[slot]
        from_l, from_r = self.q_left.at[slot], self.q_right.at[slot]
        remote = functools.partial(functools.partial, self.remote)

        up_right = remote(acc, from_l, slot, 11, 12, right, side)
        up_left = remote(acc, from_r, slot, 11, 13, left, side)
        to_side = remote(acc, side_in, slot, 14, 15, place, 1 - side)

        def down(src):
            return (
                remote(src, out.at[wide], slot, 16, 18, left, side),
                remote(src, out.at[wide], slot, 17, 18, right, side),
            )

        def keep():
            return pltpu.make_async_copy(side_in, out.at[wide], self.sems.at[19, slot])

        def hand_down(src):
            down_left, down_right = down(src)
            pl.when(from_left)(lambda: down_left().start())
            pl.when(from_right)(lambda: down_right().start())

        if which == "up":
            acc[...] = own[wide, :]

            @pl.when(place < root)
            def _():
                @pl.when(from_left)
                def _():
                    up_right().wait_recv()
                    acc[...] += from_l[...]

                up_right().start()

            @pl.when(place > root)
            def _():
                @pl.when(from_right)
                def _():
                    up_left().wait_recv()
                    acc[...] += from_r[...]

                up_left().start()

        if which == "root":

            @pl.when(place == root)
            def _():
                @pl.when(from_left)
                def _():
                    up_right().wait_recv()
                    acc[...] += from_l[...]

                @pl.when(from_right)
                def _():
                    up_left().wait_recv()
                    acc[...] += from_r[...]

                to_side().start()

        if which == "side":

            @pl.when(place == root)
            def _():
                to_side().wait_recv()
                side_in[...] += acc[...]
                hand_down(side_in)
                keep().start()

        if which == "down":

            @pl.when(place != root)
            def _():
                down(acc)[0]().wait_recv()
                hand_down(out.at[wide])

        if which == "end":
            down_left, down_right = down(acc)
            pl.when(from_left)(lambda: down_left().wait_send())
            pl.when(from_right)(lambda: down_right().wait_send())

            @pl.when(place == root)
            def _():
                to_side().wait_send()
                keep().wait()

            pl.when(place != root)(lambda: up_left().wait_send())

    P_LAGS = (("split", 0, 0), ("up", 2, 1), ("root", 3, 3), ("down", 6, 7), ("end", 9, 9))
    Q_LAGS = (("up", 1, 0), ("root", 2, 2), ("side", 4, 4), ("down", 6, 7), ("end", 9, 9))

    def tick(self, t, count):
        middle = (self.place == self.places // 2) | (self.place == self.places // 2 - 1)
        for stage, lags in ((self.p_stage, self.P_LAGS), (self.q_stage, self.Q_LAGS)):
            for which, mid_lag, outer_lag in lags:
                k = t - jnp.where(middle, mid_lag, outer_lag)

                @pl.when((k >= 0) & (k < count))
                def _(stage=stage, which=which, k=k):
                    stage(which, k)

    def run(self, count):
        @pl.loop(0, count + self.P_LAGS[-1][1])
        def _(t):
            self.tick(t, count)


def seq_sum_scratch():
    half = pltpu.VMEM((SLOTS_IN_FLIGHT, HALF, LANES), jnp.float32)
    wide = pltpu.VMEM((SLOTS_IN_FLIGHT, 2 * HALF, LANES), jnp.float32)
    return [half] * 4 + [wide] * 4 + [pltpu.SemaphoreType.DMA((20, SLOTS_IN_FLIGHT))]


def seq_sum_kernel(places, own, out, *scratch):
    summer = SeqSum(places, own, out, scratch)
    summer.greet()
    summer.run(own.shape[0] // (4 * HALF))


def seq_sum(block, collective_id, name):
    rows = block.shape[0]
    return pl.pallas_call(
        functools.partial(seq_sum_kernel, lax.axis_size("seq") // 2),
        out_shape=jax.ShapeDtypeStruct(block.shape, jnp.float32),
        in_specs=[pl.BlockSpec(memory_space=pltpu.VMEM)],
        out_specs=pl.BlockSpec(memory_space=pl.ANY),
        scratch_shapes=seq_sum_scratch(),
        compiler_params=pltpu.CompilerParams(
            collective_id=collective_id, has_side_effects=True, vmem_limit_bytes=40 << 20
        ),
        cost_estimate=pl.CostEstimate(
            flops=rows * 256, bytes_accessed=rows * 512 * 32, transcendentals=0
        ),
        name=name,
    )(block)


def to_panels(matrix):
    rows, cols = matrix.shape
    return matrix.reshape(rows, cols // LANES, LANES).transpose(1, 0, 2).reshape(-1, LANES)


def from_panels(panels, rows, cols):
    return panels.reshape(cols // LANES, rows, LANES).transpose(1, 0, 2).reshape(rows, cols)


def per_device(
    tokens, lengths, gain_mix, w_in, conv_weight, w_out, gain_ffn, w_gate, w_up, w_down, cotangent
):
    slot_count, local_len, width = tokens.shape
    chans = w_in.shape[2]
    group = lax.axis_size("tp")
    seq_count = lax.axis_size("seq")
    tp_at, seq_at = lax.axis_index("tp"), lax.axis_index("seq")
    core, chip = tp_at % 2, tp_at // 2
    half_slots = slot_count // 2
    half_rows = half_slots * local_len
    row_count = slot_count * local_len

    def pick(is_first, first, second):
        return jnp.where(is_first, first, second)

    def both_cores(own, other):
        return jnp.concatenate(
            [pick(core == 0, own, other), pick(core == 0, other, own)], axis=0
        )

    flat = jnp.concatenate([w_in.reshape(3 * width, chans), w_out.reshape(width, chans)], axis=0)
    taps8 = jnp.pad(conv_weight, ((0, 5), (0, 0)))
    share_rows = flat.shape[0] // seq_count
    share = lax.dynamic_slice(flat, (seq_at * share_rows, 0), (share_rows, chans))
    sent = jnp.concatenate([share.astype(jnp.float32), taps8], axis=0)
    sent = swap_tp(sent, 2)
    across = lax.all_gather(sent[:share_rows], "seq", axis=0, tiled=True)
    own_flat = jnp.concatenate([flat.astype(jnp.float32), taps8], axis=0)
    across_flat = jnp.concatenate([across, sent[share_rows:]], axis=0)
    sib_own = swap_tp(own_flat, 1)
    sib_across = swap_tp(across_flat, 1)
    pair_own = [pick(core == 0, own_flat, sib_own), pick(core == 0, sib_own, own_flat)]
    pair_across = [
        pick(core == 0, across_flat, sib_across),
        pick(core == 0, sib_across, across_flat),
    ]
    quad = [pick(chip == 0, a, b) for a, b in zip(pair_own, pair_across)] + [
        pick(chip == 0, b, a) for a, b in zip(pair_own, pair_across)
    ]
    quad = lax.optimization_barrier(quad)
    taps = jnp.stack([q[4 * width : 4 * width + 3] for q in quad])
    w_in_all = jnp.stack(
        [q[: 3 * width].reshape(width, 3 * chans).astype(jnp.bfloat16) for q in quad]
    )
    w_out_all = jnp.stack(
        [q[3 * width : 4 * width].reshape(chans, width).astype(jnp.bfloat16) for q in quad]
    )

    first_pos = seq_at * local_len
    positions = first_pos + jnp.arange(local_len, dtype=jnp.int32)
    valid = (positions[None, :] < lengths[:, None]).astype(jnp.float32)[:, :, None]
    valid_all = valid.reshape(row_count, 1)
    valid_own = lax.dynamic_slice(valid, (core * half_slots, 0, 0), (half_slots, local_len, 1))
    valid_rows = valid_own.reshape(half_rows, 1)
    tokens_own = lax.dynamic_slice(
        tokens, (core * half_slots, 0, 0), (half_slots, local_len, width)
    )
    inputs_f = tokens_own.astype(jnp.float32).reshape(half_rows, width)
    scale_mix = rms_scale(inputs_f)
    unit_mix = inputs_f * scale_mix
    normed_in = (gain_mix * unit_mix).astype(jnp.bfloat16)
    projected = jnp.stack(
        [
            jnp.dot(normed_in, w_in_all[j], preferred_element_type=jnp.float32)
            for j in range(group)
        ]
    )
    in_gate = projected[:, :, :chans]
    out_gate = projected[:, :, chans : 2 * chans]
    conv_value = projected[:, :, 2 * chans :]
    seq_shape = (group, half_slots, local_len, chans)
    gated_seq = (valid_rows * in_gate * conv_value).reshape(seq_shape)
    carried = shift_seq(gated_seq[:, :, local_len - 2 :], 1)
    padded_seq = jnp.concatenate([carried, gated_seq], axis=2)

    def tap(j):
        return taps[:, j][:, None, None, :]

    conv_sum = (
        tap(0) * padded_seq[:, :, 0:local_len]
        + tap(1) * padded_seq[:, :, 1 : local_len + 1]
        + tap(2) * padded_seq[:, :, 2 : local_len + 2]
    ).reshape(group, half_rows, chans)
    mixed_seq = (out_gate * conv_sum).astype(jnp.bfloat16)
    mixer_out = sum(
        jnp.dot(mixed_seq[j], w_out_all[j], preferred_element_type=jnp.float32)
        for j in range(group)
    )
    hidden_res = inputs_f + mixer_out
    scale_ffn = rms_scale(hidden_res)
    unit_ffn = hidden_res * scale_ffn
    unit_all = both_cores(unit_ffn, swap_tp(unit_ffn, 1))
    normed_mid = (gain_ffn * unit_all).astype(jnp.bfloat16)

    gate_proj = jnp.dot(normed_mid, w_gate, preferred_element_type=jnp.float32)
    up_proj = jnp.dot(normed_mid, w_up, preferred_element_type=jnp.float32)
    sigmoid_gate = jax.nn.sigmoid(gate_proj)
    silu_gate = gate_proj * sigmoid_gate
    activated = (silu_gate * up_proj).astype(jnp.bfloat16)
    ffn_part = jnp.dot(activated, w_down, preferred_element_type=jnp.float32)
    grad_out = valid_all * cotangent.astype(jnp.float32).reshape(row_count, width)
    grad_ffn = grad_out.astype(jnp.bfloat16)
    grad_act = dot_cols(grad_ffn, w_down)
    grad_w_down = dot_rows(activated, grad_ffn)
    silu_slope = sigmoid_gate * (1.0 + gate_proj * (1.0 - sigmoid_gate))
    grad_gate = (grad_act * up_proj * silu_slope).astype(jnp.bfloat16)
    grad_up = (grad_act * silu_gate).astype(jnp.bfloat16)
    grad_w_gate = dot_rows(normed_mid, grad_gate)
    grad_w_up = dot_rows(normed_mid, grad_up)
    mid_part = dot_cols(grad_gate, w_gate) + dot_cols(grad_up, w_up)

    def own_rows(block):
        return lax.dynamic_slice(block, (core * half_rows, 0), (half_rows, width))

    def other_rows(block):
        return lax.dynamic_slice(block, ((1 - core) * half_rows, 0), (half_rows, width))

    mid_chip = own_rows(mid_part) + swap_tp(other_rows(mid_part), 1)
    grad_mid = mid_chip + swap_tp(mid_chip, 2)
    ffn_chip = own_rows(ffn_part) + swap_tp(other_rows(ffn_part), 1)
    ffn_out = ffn_chip + swap_tp(ffn_chip, 2)
    ffn_panels = jnp.concatenate(
        [to_panels(grad_w_gate), to_panels(grad_w_up), to_panels(grad_w_down)], axis=0
    )
    ffn_sums = seq_sum(ffn_panels, 1, "sum_ffn_grads")

    block_own = hidden_res + ffn_out
    block_out = both_cores(block_own, swap_tp(block_own, 1))
    block_out = (valid_all * block_out).astype(jnp.bfloat16).reshape(slot_count, local_len, width)

    grad_gain_ffn = jnp.sum(grad_mid * unit_ffn, axis=0)
    scaled_mid = gain_ffn * grad_mid
    grad_hidden = own_rows(grad_out) + scale_ffn * (
        scaled_mid - unit_ffn * jnp.mean(scaled_mid * unit_ffn, axis=-1, keepdims=True)
    )

    grad_mixer = grad_hidden.astype(jnp.bfloat16)
    grad_mixed = jnp.stack([dot_cols(grad_mixer, w_out_all[j]) for j in range(group)])
    grad_out_gate = grad_mixed * conv_sum
    grad_conv_in = (grad_mixed * out_gate).reshape(seq_shape)
    next_grad = shift_seq(grad_conv_in[:, :, :2], -1)
    extended = jnp.concatenate([grad_conv_in, next_grad], axis=2)
    grad_gated = (
        tap(2) * extended[:, :, 0:local_len]
        + tap(1) * extended[:, :, 1 : local_len + 1]
        + tap(0) * extended[:, :, 2 : local_len + 2]
    ).reshape(group, half_rows, chans)
    grad_conv = jnp.stack(
        [
            jnp.sum(grad_conv_in * padded_seq[:, :, j : j + local_len], axis=(1, 2))
            for j in range(3)
        ],
        axis=1,
    )
    grad_in_gate = grad_gated * valid_rows * conv_value
    grad_value = grad_gated * valid_rows * in_gate
    grad_proj = jnp.concatenate([grad_in_gate, grad_out_gate, grad_value], axis=2).astype(
        jnp.bfloat16
    )
    grad_in = sum(dot_cols(grad_proj[j], w_in_all[j]) for j in range(group))
    grad_gain_mix = jnp.sum(grad_in * unit_mix, axis=0)
    scaled_in = gain_mix * grad_in
    tokens_grad = grad_hidden + scale_mix * (
        scaled_in - unit_mix * jnp.mean(scaled_in * unit_mix, axis=-1, keepdims=True)
    )
    grad_tokens = both_cores(tokens_grad, swap_tp(tokens_grad, 1))
    grad_tokens = grad_tokens.reshape(slot_count, local_len, width)

    def shard_of(stacked, which):
        at = chip * 2 + which
        return lax.dynamic_slice(
            stacked, (at,) + (0,) * (stacked.ndim - 1), (1,) + stacked.shape[1:]
        )[0]

    def mixer_panels(which):
        in_part = dot_rows(normed_in, shard_of(grad_proj, which))
        out_part = dot_rows(shard_of(mixed_seq, which), grad_mixer)
        small = jnp.concatenate(
            [grad_gain_mix, grad_gain_ffn, shard_of(grad_conv, which).reshape(-1)]
        ).reshape(-1, LANES)
        pad = -small.shape[0] % (4 * HALF)
        return jnp.concatenate(
            [to_panels(in_part), to_panels(out_part), jnp.pad(small, ((0, pad), (0, 0)))], axis=0
        )

    mixer_chip = mixer_panels(core) + swap_tp(mixer_panels(1 - core), 1)
    mixer_sums = seq_sum(mixer_chip, 2, "sum_mixer_grads")

    hidden = w_gate.shape[1]
    panel = hidden * width // LANES
    total_w_gate = from_panels(ffn_sums[:panel], width, hidden)
    total_w_up = from_panels(ffn_sums[panel : 2 * panel], width, hidden)
    total_w_down = from_panels(ffn_sums[2 * panel :], hidden, width)
    in_rows = width * 3 * chans // LANES
    out_rows = width * chans // LANES
    total_w_in = from_panels(mixer_sums[:in_rows], width, 3 * chans).reshape(width, 3, chans)
    total_w_out = from_panels(mixer_sums[in_rows : in_rows + out_rows], chans, width)
    small = mixer_sums[in_rows + out_rows :].reshape(-1)
    total_gain_mix = small[:width]
    total_gain_ffn = small[width : 2 * width]
    total_conv = small[2 * width : 2 * width + 3 * chans].reshape(3, chans)
    return (
        block_out,
        grad_tokens,
        total_gain_mix,
        total_w_in,
        total_conv,
        total_w_out,
        total_gain_ffn,
        total_w_gate,
        total_w_up,
        total_w_down,
    )


def solution(mesh):
    rows, cols = P("tp", None), P(None, "tp")
    tokens, whole, stacked = P(None, "seq", None), P(), P(None, None, "tp")
    return jax.shard_map(
        per_device,
        mesh=mesh,
        in_specs=(
            tokens, whole, whole, stacked, cols, rows, whole, cols, cols, rows, tokens,
        ),
        out_specs=(
            tokens, tokens, whole, stacked, cols, rows, whole, cols, cols, rows,
        ),
        check_vma=False,
    )
```

time: 1320 us -> 944 us (0.72)
  waiting for transfers between devices: 1040 us -> 85.4 us
  Pallas kernels: 0 us -> 358 us
  local copies, waits for them, and re-layouts: 30 us -> 181 us
  other arithmetic: 64.3 us -> 169 us
  blocking collectives: 39.2 us -> 0 us
    psum x4 -> x0, waiting for transfers between devices: 1040 us -> none  [the longest x1 503 us: per_device(): lax.psum((grad_gain_mix, grad_w_in, grad_conv, grad_w_out, ffn_totals[0],...]
    pallas_call x0 -> x2, Pallas kernels: none -> 358 us  [seq_sum(): pl.pallas_call(functools.partial(seq_sum_kernel, lax.axis_size('seq') //...]
    all_gather x0 -> x1, waiting for transfers between devices: none -> 69.8 us  [per_device(): across = lax.all_gather(sent[:share_rows], 'seq', axis=0, tiled=True)]
    reshape x0 -> x10, local copies, waits for them, and re-layouts: none -> 41.2 us  [the longest x5 19.5 us: from_panels(): panels.reshape(cols // LANES, rows, LANES).transpose(1, 0, 2)]
    psum x1 -> x0, blocking collectives: 39.2 us -> none  [per_device(): lax.psum((grad_gain_mix, grad_w_in, grad_conv, grad_w_out, ffn_totals[0],...]
    unnamed x98 -> x193, local copies, waits for them, and re-layouts: 25.1 us -> 61 us
    concatenate x0 -> x8, other arithmetic: none -> 34.8 us  [the longest x1 13.5 us: per_device(): jnp.concatenate([to_panels(grad_w_gate), to_panels(grad_w_up), to_panels(...]
    add x3 -> x6, other arithmetic: 7.54 us -> 37.4 us  [the longest x1 7.26 us: per_device(): block_own = hidden_res + ffn_out]
  transfers between devices with their start and end apart: 6 -> 14, of which waited for: 6 -> 3; matrix products, arithmetic and copies ran while one was open for 7% -> 31% of each run, Pallas kernels for 0% -> 28%
where the time goes in v1:
time: 944 us; the launch traced here: 935 us
  Pallas kernels  358 us (38%)
  local copies, waits for them, and re-layouts  181 us (19%)
  other arithmetic  169 us (18%)
  matrix products  113 us (12%)
  waiting for transfers between devices  85.4 us (9%)
  between operations  15.4 us (2%)
  starting transfers between devices  12.1 us (1%)
    pallas_call x2, Pallas kernels, seq_sum(): pl.pallas_call(functools.partial(seq_sum_kernel, lax.axis_size('seq') //...  358 us
    all_gather x1, waiting for transfers between devices, per_device(): across = lax.all_gather(sent[:share_rows], 'seq', axis=0, tiled=True)  69.8 us
    unnamed x193, local copies, waits for them, and re-layouts  61 us
    dot_general x11, matrix products, dot_cols(): lax.dot_general(left, right, (((1,), (1,)), ((), ())), preferred_element_...  35.4 us
    dot_general x7, matrix products, dot_rows(): lax.dot_general(left, right, (((0,), (0,)), ((), ())), preferred_element_...  34.2 us
    select_n x5, other arithmetic, pick(): return jnp.where(is_first, first, second)  21.1 us
    reshape x5, local copies, waits for them, and re-layouts, from_panels(): panels.reshape(cols // LANES, rows, LANES).transpose(1, 0, 2)  19.5 us
  transfers between devices with their start and end apart: 14, of which 3 were waited for; matrix products, arithmetic and copies ran while one was open for 31% of the time, Pallas kernels for 28%

profile of v1, /device:TPU:0, one launch (start us, length us, event | category | flops | bytes accessed | tf_op | source)
XLA Modules:
  0.0 934.5 jit_solution(1779266946033944533)
XLA Ops:
  25.4 12.1 %collective-permute-done.1 = f32[520,256]{1,0:T(8,128)S(1)} collective-permute-done((f32[520,256]{1,0:T(8,128)S(1)}, f32[520,256]{1,0:T(8,128)S(1)}, u32[]{:S(2)}, u32[]{:S(2)}) %collective-permute-start.1) | collective-permute-done | bytes 532512 | tf_op jit(solution)/shard_map/ppermute | solution.py:39
  43.6 69.8 %all-gather.2.cloned.1.call-done = f32[4096,256]{1,0:T(8,128)} async-done(((f32[512,256]{1,0:T(8,128)}), f32[4096,256]{1,0:T(8,128)}) %all-gather.2.cloned.1.call-update) | async-done | bytes 4194320 | tf_op jit(solution)/shard_map/all_gather | solution.py:362
  137.8 6.8 broadcast_select_fusion.4
  224.3 6.6 bitcast_convert_fusion
  230.9 9.1 copy.87
  240.1 9.0 fusion.32
  249.1 8.2 fusion.36
  262.8 8.3 fusion.34
  271.1 16.2 %multiply_convert_fusion = (bf16[2048,1152]{1,0:T(8,128)(2,1)}, bf16[2048,1152]{1,0:T(8,128)(2,1)}, bf16[2048,1152]{1,0:T(8,128)(2,1)}) fusion(f32[2048,1152]{1,0:T(8,128)} %fusion.36, f32[2048,1152]{1,0:T(8,128)} %fusion.34, bf16[2048,1024]{0,1:T(8,128)(2,1)S(1)} %fusion.1, bf16[1024,1152]{1,0:T(8,128)(2,1)S(1)} %copy-done), kind=kOutput, calls=%fused_computation.2 | convolution fusion | flops 4867227648 | bytes 39583744 | tf_op jit(solution)/shard_map/dot_general | solution.py:430
  287.4 7.9 fusion.37
  318.9 10.4 %fusion.41 = f32[1024,1152]{0,1:T(8,128)} fusion(bf16[2048,1024]{0,1:T(8,128)(2,1)} %copy-done.31, bf16[2048,1152]{1,0:T(8,128)(2,1)} %get-tuple-element.51), kind=kOutput, calls=%fused_computation.169 | convolution fusion | flops 4831838208 | bytes 13631488 | tf_op jit(solution)/shard_map/dot_general | solution.py:21
  329.4 6.8 fusion.2
  343.0 6.7 fusion.40
  355.8 6.1 copy.62
  361.9 7.0 dynamic-slice_add_fusion.1
  369.4 13.5 %pad_maximum_fusion.own = f32[27648,128]{1,0:T(8,128)} fusion(f32[9216,128]{1,0:T(8,128)} %bitcast.260, f32[9216,128]{1,0:T(8,128)S(1)} %bitcast.245, f32[9216,128]{1,0:T(8,128)S(1)} %bitcast.246), kind=kLoop, calls=%fused_computation | loop fusion | flops 7077888 | bytes 28311552 | tf_op jit(solution)/shard_map/concatenate | solution.py:457
  382.9 260.1 %sum_ffn_grads.1 = f32[27648,128]{1,0:T(8,128)S(1)} custom-call(f32[27648,128]{1,0:T(8,128)} %pad_maximum_fusion.own), custom_call_target="tpu_custom_call" | custom-call | flops 7077888 | bytes 452984832 | tf_op jit(solution)/shard_map/sum_ffn_grads/pallas_call | solution.py:310
  653.1 6.8 fusion.31
  664.7 7.3 add_add_fusion.1
  715.0 7.9 multiply_add_fusion
  779.0 9.3 copy.86
  802.5 9.4 %copy.88 = f32[2048,1024]{1,0:T(8,128)} copy(f32[2048,1024]{0,1:T(8,128)} %pad_maximum_fusion.3) | data formatting | bytes 16777216
  811.9 6.1 fusion.4.own
  818.0 98.0 %sum_mixer_grads.1 = f32[8704,128]{1,0:T(8,128)S(1)} custom-call(f32[8704,128]{1,0:T(8,128)S(1)} %fusion.4.own), custom_call_target="tpu_custom_call" | custom-call | flops 2228224 | bytes 142606336 | tf_op jit(solution)/shard_map/sum_mixer_grads/pallas_call | solution.py:310
  (333 shorter events, 309.5 us)
Async XLA Ops:
  7.2 263.9 %copy-start = (bf16[1024,1152]{1,0:T(8,128)(2,1)S(1)}, bf16[1024,1152]{1,0:T(8,128)(2,1)}, u32[]{:S(2)}) copy-start(bf16[1024,1152]{1,0:T(8,128)(2,1)} %param.18) | copy-start | bytes 7077892
  7.2 106.2 %all-gather.2.cloned.1.call-start = ((), (), s32[]{:S(2)}) async-start(), calls=%async_computation | async-start | bytes 4718592 | tf_op jit(solution)/shard_map/all_gather | solution.py:362
  22.4 15.1 %collective-permute-start.1 = (f32[520,256]{1,0:T(8,128)S(1)}, f32[520,256]{1,0:T(8,128)S(1)}, u32[]{:S(2)}, u32[]{:S(2)}) collective-permute-start(f32[520,256]{1,0:T(8,128)S(1)} %pad_maximum_fusion.10), channel_id=1, source_target_pairs={{0,2},{1,3},{2,0},{3,1},{4,6},{5,7},{6,4},{7,5},{8,10},{9,11},{10,... | collective-permute-start | bytes 1597448 | tf_op jit(solution)/shard_map/ppermute | solution.py:39
  43.6 90.8 %collective-permute-start = (f32[4104,256]{1,0:T(8,128)}, f32[4104,256]{1,0:T(8,128)}, u32[]{:S(2)}, u32[]{:S(2)}) collective-permute-start(f32[4104,256]{1,0:T(8,128)} %pad_maximum_fusion.5), channel_id=1, source_target_pairs={{0,1},{1,0},{2,3},{3,2},{4,5},{5,4},{6,7},{7,6},{8,9},{9,8},{10,11... | collective-permute-start | bytes 12607496 | tf_op jit(solution)/shard_map/ppermute | solution.py:39
  43.6 74.3 %copy-start.69 = (s32[4]{0:T(128)S(1)}, s32[4]{0:T(128)}, u32[]{:S(2)}) copy-start(s32[4]{0:T(128)} %param.12) | copy-start | bytes 52
  117.9 16.5 %collective-permute-start.2 = (f32[4104,256]{1,0:T(8,128)}, f32[4104,256]{1,0:T(8,128)}, u32[]{:S(2)}, u32[]{:S(2)}) collective-permute-start(f32[4104,256]{1,0:T(8,128)} %pad_maximum_fusion.6), channel_id=1, source_target_pairs={{0,1},{1,0},{2,3},{3,2},{4,5},{5,4},{6,7},{7,6},{8,9},{9,8},{10,11... | collective-permute-start | bytes 12607496 | tf_op jit(solution)/shard_map/ppermute | solution.py:39
  118.6 61.0 %copy-start.54 = (f32[1,4,2,128]{3,1,2,0:T(4,128)}, f32[1,4,2,128]{3,1,2,0:T(4,128)S(1)}, u32[]{:S(2)}) copy-start(f32[1,4,2,128]{3,1,2,0:T(4,128)S(1)} %copy.100) | copy-start | bytes 12292
  186.1 16.4 %collective-permute-start.3 = (f32[4,2,2,256]{3,2,1,0:T(2,128)S(1)}, f32[4,2,2,256]{3,2,1,0:T(2,128)S(1)}, u32[]{:S(2)}, u32[]{:S(2)}) collective-permute-start(f32[4,2,2,256]{3,2,1,0:T(2,128)S(1)} %slice.199), channel_id=1, source_target_pairs={{0,4},{4,8},{8,12},{12,16},{16,20},{20,24},{24,28},{1,5},{5,9},{9,... | collective-permute-start | bytes 49160 | tf_op jit(solution)/shard_map/ppermute | solution.py:35
  196.5 18.0 %copy-start.33 = (bf16[256,1024]{1,0:T(8,128)(2,1)}, bf16[256,1024]{1,0:T(8,128)(2,1)S(1)}, u32[]{:S(2)}) copy-start(bf16[256,1024]{1,0:T(8,128)(2,1)S(1)} %convert_element_type.125) | copy-start | bytes 1572868
  218.3 38.9 %copy-start.50 = (f32[1024]{0:T(1024)}, f32[1024]{0:T(1024)S(1)}, u32[]{:S(2)}) copy-start(f32[1024]{0:T(1024)S(1)} %add_rsqrt_fusion) | copy-start | bytes 12292
  221.7 35.6 %collective-permute-start.4 = (f32[1024,1024]{0,1:T(8,128)}, f32[1024,1024]{0,1:T(8,128)}, u32[]{:S(2)}, u32[]{:S(2)}) collective-permute-start(f32[1024,1024]{0,1:T(8,128)} %broadcast_multiply_fusion.1), channel_id=1, source_target_pairs={{0,1},{1,0},{2,3},{3,2},{4,5},{5,4},{6,7},{7,6},{8,9},{9,8},{10,11... | collective-permute-start | bytes 12582920 | tf_op jit(solution)/shard_map/ppermute | solution.py:39
  307.2 29.1 %collective-permute-start.8 = (f32[1024,1024]{0,1:T(8,128)}, f32[1024,1024]{0,1:T(8,128)}, u32[]{:S(2)}, u32[]{:S(2)}) collective-permute-start(f32[1024,1024]{0,1:T(8,128)} %constant_dynamic-slice_fusion.2), channel_id=1, source_target_pairs={{0,1},{1,0},{2,3},{3,2},{4,5},{5,4},{6,7},{7,6},{8,9},{9,8},{10,11... | collective-permute-start | bytes 12582920 | tf_op jit(solution)/shard_map/ppermute | solution.py:39
  318.9 43.0 %collective-permute-start.5 = (f32[1024,1024]{0,1:T(8,128)}, f32[1024,1024]{0,1:T(8,128)}, u32[]{:S(2)}, u32[]{:S(2)}) collective-permute-start(f32[1024,1024]{0,1:T(8,128)} %constant_dynamic-slice_fusion.3), channel_id=1, source_target_pairs={{0,1},{1,0},{2,3},{3,2},{4,5},{5,4},{6,7},{7,6},{8,9},{9,8},{10,11... | collective-permute-start | bytes 12582920 | tf_op jit(solution)/shard_map/ppermute | solution.py:39
  318.9 17.3 %slice-start.9 = ((s8[8388608]{0:T(1024)(128)(4,1)}), s8[4194304]{0:T(1024)(128)(4,1)S(1)}, s32[]{:S(2)}) async-start(s8[8388608]{0:T(1024)(128)(4,1)} %bitcast.257), calls=%async_computation.10 | async-start | bytes 8388608
  318.9 24.1 %slice-start.11 = ((s8[4718592]{0:T(1024)(128)(4,1)}), s8[4194304]{0:T(1024)(128)(4,1)S(1)}, s32[]{:S(2)}) async-start(s8[4718592]{0:T(1024)(128)(4,1)} %bitcast.294), calls=%async_computation.12 | async-start | bytes 8388608
  341.5 306.6 %collective-permute-start.9 = (f32[1024,1024]{0,1:T(8,128)}, f32[1024,1024]{0,1:T(8,128)}, u32[]{:S(2)}, u32[]{:S(2)}) collective-permute-start(f32[1024,1024]{0,1:T(8,128)} %dynamic-slice_add_fusion), channel_id=1, source_target_pairs={{0,2},{1,3},{2,0},{3,1},{4,6},{5,7},{6,4},{7,5},{8,10},{9,11},{10,... | collective-permute-start | bytes 12582920 | tf_op jit(solution)/shard_map/ppermute | solution.py:39
  368.8 295.8 %collective-permute-start.6 = (f32[1024,1024]{0,1:T(8,128)}, f32[1024,1024]{0,1:T(8,128)}, u32[]{:S(2)}, u32[]{:S(2)}) collective-permute-start(f32[1024,1024]{0,1:T(8,128)} %dynamic-slice_add_fusion.1), channel_id=1, source_target_pairs={{0,2},{1,3},{2,0},{3,1},{4,6},{5,7},{6,4},{7,5},{8,10},{9,11},{10,... | collective-permute-start | bytes 12582920 | tf_op jit(solution)/shard_map/ppermute | solution.py:39
  382.9 265.2 %copy-start.6 = (f32[1024,1024]{0,1:T(8,128)S(1)}, f32[1024,1024]{0,1:T(8,128)}, u32[]{:S(2)}) copy-start(f32[1024,1024]{0,1:T(8,128)} %copy-done.4) | copy-start | bytes 12582916
  382.9 265.2 %copy-start.51 = (f32[1024]{0:T(1024)S(1)}, f32[1024]{0:T(1024)}, u32[]{:S(2)}) copy-start(f32[1024]{0:T(1024)} %copy-done.50) | copy-start | bytes 12292
  660.0 22.9 %copy-start.20 = (bf16[1024,1024]{0,1:T(8,128)(2,1)}, bf16[1024,1024]{0,1:T(8,128)(2,1)S(1)}, u32[]{:S(2)}) copy-start(bf16[1024,1024]{0,1:T(8,128)(2,1)S(1)} %get-tuple-element.47) | copy-start | bytes 6291460
  671.9 99.9 %collective-permute-start.7 = (f32[1024,1024]{0,1:T(8,128)}, f32[1024,1024]{0,1:T(8,128)}, u32[]{:S(2)}, u32[]{:S(2)}) collective-permute-start(f32[1024,1024]{0,1:T(8,128)} %add_add_fusion.1), channel_id=1, source_target_pairs={{0,1},{1,0},{2,3},{3,2},{4,5},{5,4},{6,7},{7,6},{8,9},{9,8},{10,11... | collective-permute-start | bytes 12582920 | tf_op jit(solution)/shard_map/ppermute | solution.py:39
  681.5 5.8 collective-permute-start.10
  722.8 71.4 %collective-permute-start.11 = (f32[1024,1024]{0,1:T(8,128)}, f32[1024,1024]{0,1:T(8,128)}, u32[]{:S(2)}, u32[]{:S(2)}) collective-permute-start(f32[1024,1024]{0,1:T(8,128)} %multiply_add_fusion), channel_id=1, source_target_pairs={{0,1},{1,0},{2,3},{3,2},{4,5},{5,4},{6,7},{7,6},{8,9},{9,8},{10,11... | collective-permute-start | bytes 12582920 | tf_op jit(solution)/shard_map/ppermute | solution.py:39
  730.8 81.1 %collective-permute-start.12 = (f32[8704,128]{1,0:T(8,128)}, f32[8704,128]{1,0:T(8,128)}, u32[]{:S(2)}, u32[]{:S(2)}) collective-permute-start(f32[8704,128]{1,0:T(8,128)} %select_maximum_fusion), channel_id=1, source_target_pairs={{0,1},{1,0},{2,3},{3,2},{4,5},{5,4},{6,7},{7,6},{8,9},{9,8},{10,11... | collective-permute-start | bytes 13369352 | tf_op jit(solution)/shard_map/ppermute | solution.py:39
  (80 other events, 514.9 us)
Sparse Core Ops, SparseCore 0:
  38.5 74.8 all-gather.1

commit v2 on v1

--- a/solution.py
+++ b/solution.py
@@ -9,6 +9,7 @@
 
 NORM_EPS = 1e-05
 LANES = 128
+VMEM_LIMIT = 64 << 20
 HALF = 128
 SLOTS_IN_FLIGHT = 10
 
@@ -48,7 +49,7 @@
         here = lax.axis_index("seq")
         self.place, self.side = here // 2, here % 2
 
-    def greet(self):
+    def greet(self, others=()):
         barrier = pltpu.get_barrier_semaphore()
         place, side = self.place, self.side
 
@@ -58,6 +59,10 @@
             )
 
         signal(place * 2 + 1 - side)
+        for other in others:
+            pl.semaphore_signal(
+                barrier, inc=1, device_id=other, device_id_type=pl.DeviceIdType.MESH
+            )
 
         @pl.when(place > 0)
         def _():
@@ -68,7 +73,7 @@
             signal((place + 1) * 2 + side)
 
         ends = jnp.where(place > 0, 1, 0) + jnp.where(place < self.places - 1, 1, 0)
-        pl.semaphore_wait(barrier, 1 + ends)
+        pl.semaphore_wait(barrier, 1 + len(others) + ends)
 
     def remote(self, src, dst, slot, send, recv, place, side):
         return pltpu.make_async_remote_copy(
@@ -321,6 +326,218 @@
         ),
         name=name,
     )(block)
+
+
+FFN_PARTS = 3
+ROW_BLOCK = 512
+OUT_BLOCK = 256
+
+
+def ffn_kernel(places, *refs):
+    (mid_hbm, mid_t_hbm, cot_hbm, cot_t_hbm, w_gu_hbm, w_d_hbm) = refs[0:6]
+    (sums, mid_chip, mid_far, ffn_chip, ffn_far, mid_land, ffn_land) = refs[6:13]
+    (mid, mid_t, cot, cot_t, w_gu, w_d, act, ggu, own, staged, fetched) = refs[13:24]
+    load_sems, near_sems, far_sems, keep_sem, fetch_sem = refs[24:29]
+    summer = SeqSum(places, own, sums, refs[29:])
+    tp_at = lax.axis_index("tp")
+    core = lax.rem(tp_at, 2)
+    sibling = tp_at + 1 - 2 * core
+    across = lax.rem(tp_at + 2, 4)
+    rows, width = mid.shape
+    parts, _, wide = w_gu.shape
+    hidden = wide // 2
+    panels = 3 * hidden // LANES
+
+    loads = [
+        pltpu.make_async_copy(src, dst, load_sems.at[i])
+        for i, (src, dst) in enumerate(
+            (
+                (mid_hbm, mid),
+                (w_gu_hbm, w_gu),
+                (cot_hbm, cot),
+                (w_d_hbm, w_d),
+                (mid_t_hbm, mid_t),
+                (cot_t_hbm, cot_t),
+            )
+        )
+    ]
+    for load in loads:
+        load.start()
+    summer.greet(({"tp": sibling}, {"tp": across}))
+    count = own.shape[0] // (4 * HALF)
+    for load in loads[:4]:
+        load.wait()
+
+    def part_cols(c):
+        return pl.ds(pl.multiple_of(c * hidden, LANES), hidden)
+
+    @pl.loop(0, parts)
+    def _(c):
+        @pl.loop(0, rows // ROW_BLOCK)
+        def _(r):
+            at = pl.ds(pl.multiple_of(r * ROW_BLOCK, ROW_BLOCK), ROW_BLOCK)
+            both = jnp.dot(mid[at, :], w_gu[c], preferred_element_type=jnp.float32)
+            gate, up = both[:, :hidden], both[:, hidden:]
+            grad_act = dot_cols(cot[at, :], w_d[c])
+            sigmoid = 1.0 / (1.0 + jnp.exp(-gate))
+            silu = gate * sigmoid
+            act[at, part_cols(c)] = (silu * up).astype(jnp.bfloat16)
+            slope = sigmoid * (1.0 + gate * (1.0 - sigmoid))
+            ggu[c, at, :hidden] = (grad_act * up * slope).astype(jnp.bfloat16)
+            ggu[c, at, hidden:] = (grad_act * silu).astype(jnp.bfloat16)
+
+        @pl.when(c == 0)
+        def _():
+            for load in loads[4:]:
+                load.wait()
+
+        @pl.loop(0, width // OUT_BLOCK)
+        def _(m):
+            first = pl.multiple_of(m * OUT_BLOCK, OUT_BLOCK)
+            at = pl.ds(first, OUT_BLOCK)
+            base = c * (panels * width) + first
+
+            def put(block, panel):
+                for j in range(block.shape[1] // LANES):
+                    to = pl.multiple_of(base + (panel + j) * width, OUT_BLOCK)
+                    own[pl.ds(to, OUT_BLOCK), :] = block[:, j * LANES : (j + 1) * LANES]
+
+            put(jnp.dot(mid_t[at, :], ggu[c], preferred_element_type=jnp.float32), 0)
+            put(
+                jnp.dot(cot_t[at, :], act[:, part_cols(c)], preferred_element_type=jnp.float32),
+                wide // LANES,
+            )
+
+            @pl.when(c > 0)
+            def _():
+                summer.tick((c - 1) * (width // OUT_BLOCK) + m, count)
+
+    early = (parts - 1) * (width // OUT_BLOCK)
+    blocks = rows // 2 // OUT_BLOCK
+
+    def row_block(half, k):
+        return pl.ds(pl.multiple_of((half * blocks + k) * OUT_BLOCK, OUT_BLOCK), OUT_BLOCK)
+
+    def mid_part(at):
+        return sum(dot_cols(ggu[c, at, :], w_gu[c]) for c in range(parts))
+
+    def ffn_part(at):
+        return sum(
+            jnp.dot(
+                act[at, c * hidden : (c + 1) * hidden],
+                w_d[c],
+                preferred_element_type=jnp.float32,
+            )
+            for c in range(parts)
+        )
+
+    def near(which, land, k):
+        return pltpu.make_async_remote_copy(
+            src_ref=staged.at[lax.rem(k, 2)],
+            dst_ref=land.at[row_block(0, k)],
+            send_sem=near_sems.at[which, 0, k],
+            recv_sem=near_sems.at[which, 1, k],
+            device_id={"tp": sibling},
+            device_id_type=pl.DeviceIdType.MESH,
+        )
+
+    def far(which, chip, there, k):
+        return pltpu.make_async_remote_copy(
+            src_ref=chip.at[row_block(0, k)],
+            dst_ref=there.at[row_block(0, k)],
+            send_sem=far_sems.at[which, 0, k],
+            recv_sem=far_sems.at[which, 1, k],
+            device_id={"tp": across},
+            device_id_type=pl.DeviceIdType.MESH,
+        )
+
+    def tp_sum(which, part, land, chip, there, first_tick):
+        @pl.loop(0, blocks)
+        def _(k):
+            @pl.when(k >= 2)
+            def _():
+                near(which, land, k - 2).wait_send()
+
+            staged[lax.rem(k, 2)] = part(row_block(1 - core, k))
+            near(which, land, k).start()
+
+        for k in range(max(blocks - 2, 0), blocks):
+            near(which, land, k).wait_send()
+
+        @pl.loop(0, blocks)
+        def _(k):
+            near(which, land, k).wait_recv()
+            fetch = pltpu.make_async_copy(land.at[row_block(0, k)], fetched, fetch_sem)
+            fetch.start()
+            staged[0] = part(row_block(core, k))
+            fetch.wait()
+            staged[0] += fetched[...]
+            keep = pltpu.make_async_copy(staged.at[0], chip.at[row_block(0, k)], keep_sem)
+            keep.start()
+            summer.tick(first_tick + k, count)
+            keep.wait()
+            far(which, chip, there, k).start()
+
+    tp_sum(0, mid_part, mid_land, mid_chip, mid_far, early)
+    tp_sum(1, ffn_part, ffn_land, ffn_chip, ffn_far, early + blocks)
+
+    @pl.loop(early + 2 * blocks, count + summer.P_LAGS[-1][1])
+    def _(t):
+        summer.tick(t, count)
+
+    for which, chip, there in ((0, mid_chip, mid_far), (1, ffn_chip, ffn_far)):
+
+        @pl.loop(0, blocks)
+        def _(k, which=which, chip=chip, there=there):
+            far(which, chip, there, k).wait()
+
+
+def ffn_both_ways(normed_mid, grad_ffn, w_gate, w_up, w_down, collective_id):
+    rows, width = normed_mid.shape
+    local = w_gate.shape[1]
+    hidden = local // FFN_PARTS
+
+    def in_parts(weights):
+        return weights.reshape(width, FFN_PARTS, hidden)
+
+    w_gu = jnp.concatenate([in_parts(w_gate), in_parts(w_up)], axis=2).transpose(1, 0, 2)
+    w_d = w_down.reshape(FFN_PARTS, hidden, width)
+    grad_rows = 3 * local * width // LANES
+    half = jax.ShapeDtypeStruct((rows // 2, width), jnp.float32)
+    low = jnp.bfloat16
+    blocks = rows // 2 // OUT_BLOCK
+    return pl.pallas_call(
+        functools.partial(ffn_kernel, lax.axis_size("seq") // 2),
+        out_shape=[jax.ShapeDtypeStruct((grad_rows, LANES), jnp.float32)] + [half] * 6,
+        in_specs=[pl.BlockSpec(memory_space=pl.ANY)] * 6,
+        out_specs=[pl.BlockSpec(memory_space=pl.ANY)] * 7,
+        scratch_shapes=[
+            pltpu.VMEM((rows, width), low),
+            pltpu.VMEM((width, rows), low),
+            pltpu.VMEM((rows, width), low),
+            pltpu.VMEM((width, rows), low),
+            pltpu.VMEM(w_gu.shape, low),
+            pltpu.VMEM(w_d.shape, low),
+            pltpu.VMEM((rows, local), low),
+            pltpu.VMEM((FFN_PARTS, rows, 2 * hidden), low),
+            pltpu.VMEM((grad_rows, LANES), jnp.float32),
+            pltpu.VMEM((2, OUT_BLOCK, width), jnp.float32),
+            pltpu.VMEM((OUT_BLOCK, width), jnp.float32),
+            pltpu.SemaphoreType.DMA((6,)),
+            pltpu.SemaphoreType.DMA((2, 2, blocks)),
+            pltpu.SemaphoreType.DMA((2, 2, blocks)),
+            pltpu.SemaphoreType.DMA,
+            pltpu.SemaphoreType.DMA,
+        ]
+        + seq_sum_scratch(),
+        compiler_params=pltpu.CompilerParams(
+            collective_id=collective_id, has_side_effects=True, vmem_limit_bytes=VMEM_LIMIT
+        ),
+        cost_estimate=pl.CostEstimate(
+            flops=18 * rows * width * local, bytes_accessed=800 << 20, transcendentals=0
+        ),
+        name="ffn_both_ways",
+    )(normed_mid, normed_mid.T, grad_ffn, grad_ffn.T, w_gu, w_d)
 
 
 def to_panels(matrix):
@@ -427,37 +644,16 @@
     unit_all = both_cores(unit_ffn, swap_tp(unit_ffn, 1))
     normed_mid = (gain_ffn * unit_all).astype(jnp.bfloat16)
 
-    gate_proj = jnp.dot(normed_mid, w_gate, preferred_element_type=jnp.float32)
-    up_proj = jnp.dot(normed_mid, w_up, preferred_element_type=jnp.float32)
-    sigmoid_gate = jax.nn.sigmoid(gate_proj)
-    silu_gate = gate_proj * sigmoid_gate
-    activated = (silu_gate * up_proj).astype(jnp.bfloat16)
-    ffn_part = jnp.dot(activated, w_down, preferred_element_type=jnp.float32)
     grad_out = valid_all * cotangent.astype(jnp.float32).reshape(row_count, width)
     grad_ffn = grad_out.astype(jnp.bfloat16)
-    grad_act = dot_cols(grad_ffn, w_down)
-    grad_w_down = dot_rows(activated, grad_ffn)
-    silu_slope = sigmoid_gate * (1.0 + gate_proj * (1.0 - sigmoid_gate))
-    grad_gate = (grad_act * up_proj * silu_slope).astype(jnp.bfloat16)
-    grad_up = (grad_act * silu_gate).astype(jnp.bfloat16)
-    grad_w_gate = dot_rows(normed_mid, grad_gate)
-    grad_w_up = dot_rows(normed_mid, grad_up)
-    mid_part = dot_cols(grad_gate, w_gate) + dot_cols(grad_up, w_up)
+    ffn_sums, mid_chip, mid_far, ffn_chip, ffn_far = ffn_both_ways(
+        normed_mid, grad_ffn, w_gate, w_up, w_down, 1
+    )[:5]
+    grad_mid = mid_chip + mid_far
+    ffn_out = ffn_chip + ffn_far
 
     def own_rows(block):
         return lax.dynamic_slice(block, (core * half_rows, 0), (half_rows, width))
-
-    def other_rows(block):
-        return lax.dynamic_slice(block, ((1 - core) * half_rows, 0), (half_rows, width))
-
-    mid_chip = own_rows(mid_part) + swap_tp(other_rows(mid_part), 1)
-    grad_mid = mid_chip + swap_tp(mid_chip, 2)
-    ffn_chip = own_rows(ffn_part) + swap_tp(other_rows(ffn_part), 1)
-    ffn_out = ffn_chip + swap_tp(ffn_chip, 2)
-    ffn_panels = jnp.concatenate(
-        [to_panels(grad_w_gate), to_panels(grad_w_up), to_panels(grad_w_down)], axis=0
-    )
-    ffn_sums = seq_sum(ffn_panels, 1, "sum_ffn_grads")
 
     block_own = hidden_res + ffn_out
     block_out = both_cores(block_own, swap_tp(block_own, 1))
@@ -522,10 +718,10 @@
     mixer_sums = seq_sum(mixer_chip, 2, "sum_mixer_grads")
 
     hidden = w_gate.shape[1]
-    panel = hidden * width // LANES
-    total_w_gate = from_panels(ffn_sums[:panel], width, hidden)
-    total_w_up = from_panels(ffn_sums[panel : 2 * panel], width, hidden)
-    total_w_down = from_panels(ffn_sums[2 * panel :], hidden, width)
+    by_part = ffn_sums.reshape(FFN_PARTS, 3, hidden // FFN_PARTS // LANES, width, LANES)
+    total_w_gate = by_part[:, 0].transpose(2, 0, 1, 3).reshape(width, hidden)
+    total_w_up = by_part[:, 1].transpose(2, 0, 1, 3).reshape(width, hidden)
+    total_w_down = by_part[:, 2].transpose(0, 1, 3, 2).reshape(hidden, width)
     in_rows = width * 3 * chans // LANES
     out_rows = width * chans // LANES
     total_w_in = from_panels(mixer_sums[:in_rows], width, 3 * chans).reshape(width, 3, chans)

time: 944 us -> 901 us (0.954)
  matrix products: 113 us -> 46.6 us
  Pallas kernels: 358 us -> 398 us
  other arithmetic: 169 us -> 141 us
    pallas_call x0 -> x1, Pallas kernels: none -> 298 us  [ffn_both_ways(): pl.pallas_call(functools.partial(ffn_kernel, lax.axis_size('seq') // 2),...]
    pallas_call x2 -> x1, Pallas kernels: 358 us -> 100 us  [seq_sum(): pl.pallas_call(functools.partial(seq_sum_kernel, lax.axis_size('seq') //...]
    dot_general x3 -> x0, matrix products: 30.5 us -> none  [the longest x1 16.2 us: per_device(): gate_proj = jnp.dot(normed_mid, w_gate, preferred_element_type=jnp.float32)]
    dot_general x11 -> x8, matrix products: 35.4 us -> 12.7 us  [dot_cols(): lax.dot_general(left, right, (((1,), (1,)), ((), ())), preferred_element_...]
    dot_general x7 -> x4, matrix products: 34.2 us -> 11.8 us  [dot_rows(): lax.dot_general(left, right, (((0,), (0,)), ((), ())), preferred_element_...]
    pallas_call x0 -> x4, local copies, waits for them, and re-layouts: none -> 21.5 us  [ffn_both_ways(): pl.pallas_call(functools.partial(ffn_kernel, lax.axis_size('seq') // 2),...]
    reshape x5 -> x2, local copies, waits for them, and re-layouts: 19.5 us -> 3.52 us  [from_panels(): panels.reshape(cols // LANES, rows, LANES).transpose(1, 0, 2)]
    concatenate x1 -> x0, other arithmetic: 13.5 us -> none  [per_device(): jnp.concatenate([to_panels(grad_w_gate), to_panels(grad_w_up), to_panels(...]
  transfers between devices with their start and end apart: 14 -> 10, of which waited for: 3 -> 2; matrix products, arithmetic and copies ran while one was open for 31% -> 26% of each run, Pallas kernels for 28% -> 0%
where the time goes in v2:
time: 901 us; the launch traced here: 884 us
  Pallas kernels  398 us (44%)
  local copies, waits for them, and re-layouts  187 us (21%)
  other arithmetic  141 us (16%)
  waiting for transfers between devices  83.6 us (9%)
  matrix products  46.6 us (5%)
  between operations  15.4 us (2%)
  starting transfers between devices  12.1 us (1%)
    pallas_call x1, Pallas kernels, ffn_both_ways(): pl.pallas_call(functools.partial(ffn_kernel, lax.axis_size('seq') // 2),...  298 us
    pallas_call x1, Pallas kernels, seq_sum(): pl.pallas_call(functools.partial(seq_sum_kernel, lax.axis_size('seq') //...  100 us
    all_gather x1, waiting for transfers between devices, per_device(): across = lax.all_gather(sent[:share_rows], 'seq', axis=0, tiled=True)  71.4 us
    unnamed x163, local copies, waits for them, and re-layouts  70.5 us
    pallas_call x4, local copies, waits for them, and re-layouts, ffn_both_ways(): pl.pallas_call(functools.partial(ffn_kernel, lax.axis_size('seq') // 2),...  21.5 us
    dot_general x4, matrix products, per_device(): jnp.dot(normed_in, w_in_all[j], preferred_element_type=jnp.float32)  18.2 us
  transfers between devices with their start and end apart: 10, of which 2 were waited for; matrix products, arithmetic and copies ran while one was open for 26% of the time, Pallas kernels for 0%

profile of v2, /device:TPU:0, one launch (start us, length us, event | category | flops | bytes accessed | tf_op | source)
XLA Modules:
  0.0 883.9 jit_solution(9629887757492900448)
XLA Ops:
  17.5 12.1 %collective-permute-done.1 = f32[520,256]{1,0:T(8,128)S(1)} collective-permute-done((f32[520,256]{1,0:T(8,128)S(1)}, f32[520,256]{1,0:T(8,128)S(1)}, u32[]{:S(2)}, u32[]{:S(2)}) %collective-permute-start.1) | collective-permute-done | bytes 532512 | tf_op jit(solution)/shard_map/ppermute | solution.py:40
  34.1 71.4 %all-gather.2.cloned.1.call-done = f32[4096,256]{1,0:T(8,128)} async-done(((f32[512,256]{1,0:T(8,128)}), f32[4096,256]{1,0:T(8,128)}) %all-gather.2.cloned.1.call-update) | async-done | bytes 4194320 | tf_op jit(solution)/shard_map/all_gather | solution.py:579
  207.8 6.6 bitcast_convert_fusion
  214.5 9.1 %copy.86 = f32[2048,1024]{0,1:T(8,128)} copy(f32[2048,1024]{1,0:T(8,128)} %bitcast_convert_fusion) | data formatting | bytes 16777216 | tf_op jit(solution)/shard_map/reshape | solution.py:647
  223.6 10.3 %fusion.27 = (bf16[2048,1024]{0,1:T(8,128)(2,1)}, f32[2048,1024]{0,1:T(8,128)}) fusion(f32[2048,1024]{0,1:T(8,128)} %copy.86, f32[2048]{0:T(1024)S(1)} %bitcast.254), kind=kLoop, calls=%fused_computation.146 | loop fusion | flops 4194304 | bytes 20979712 | tf_op jit(solution)/shard_map/convert_element_type | solution.py:648
  233.9 6.4 copy.52.refs_2_
  262.9 6.4 copy.51.refs_0_
  269.3 298.1 %ffn_both_ways.1 = (f32[27648,128]{1,0:T(8,128)}, f32[1024,1024]{1,0:T(8,128)}, f32[1024,1024]{1,0:T(8,128)}, f32[1024,1024]{1,0:T(8,128)}, f32[1024,1024]{1,0:T...) custom-call(bf16[2048,1024]{1,0:T(8,128)(2,1)} %copy.51.refs_0_, bf16[1024,2048]{1,0:T(8,128)(2,1)} %bitcast.221, ...), custom_call_target="tpu_custom_call" | custom-call | flops 43486543872 | bytes 838860800 | tf_op jit(solution)/shard_map/ffn_both_ways/pallas_call | solution.py:509
  578.2 6.1 multiply_reduce_fusion.3
  618.9 8.6 add_add_fusion.1
  627.7 5.7 fusion.5
  654.5 7.8 multiply_add_fusion
  664.7 5.7 select_maximum_fusion
  670.4 10.6 %slice_bitcast_fusion = (f32[3,3,128,1024]{2,3,1,0:T(8,128)}, f32[3,1,3,1024,128]{4,3,2,1,0:T(8,128)}, f32[3,1,3,1024,128]{4,3,2,1,0:T(8,128)}) fusion(f32[3,3,3,1024,128]{4,3,2,1,0:T(8,128)} %bitcast.223), kind=kLoop, calls=%fused_computation.7 | loop fusion | bytes 28311552 | tf_op jit(solution)/shard_map/transpose | solution.py:724
  681.0 6.1 copy.96
  687.1 6.0 copy.75
  693.1 6.0 copy.97
  699.2 6.0 copy.76
  705.2 6.0 copy.72
  728.0 9.3 %copy.87 = f32[2048,1024]{1,0:T(8,128)} copy(f32[2048,1024]{0,1:T(8,128)} %pad_maximum_fusion.1) | data formatting | bytes 16777216 | tf_op jit(solution)/shard_map/concatenate | solution.py:569
  737.3 5.9 multiply_convert_fusion
  751.6 9.2 %copy.88 = f32[2048,1024]{1,0:T(8,128)} copy(f32[2048,1024]{0,1:T(8,128)} %pad_maximum_fusion.2) | data formatting | bytes 16777216
  760.8 6.1 fusion.1.own
  767.0 100.1 %sum_mixer_grads.1 = f32[8704,128]{1,0:T(8,128)S(1)} custom-call(f32[8704,128]{1,0:T(8,128)S(1)} %fusion.1.own), custom_call_target="tpu_custom_call" | custom-call | flops 2228224 | bytes 142606336 | tf_op jit(solution)/shard_map/sum_mixer_grads/pallas_call | solution.py:315
  (283 shorter events, 242.6 us)
Async XLA Ops:
  7.2 98.4 %all-gather.2.cloned.1.call-start = ((), (), s32[]{:S(2)}) async-start(), calls=%async_computation | async-start | bytes 4718592 | tf_op jit(solution)/shard_map/all_gather | solution.py:579
  14.5 15.1 %collective-permute-start.1 = (f32[520,256]{1,0:T(8,128)S(1)}, f32[520,256]{1,0:T(8,128)S(1)}, u32[]{:S(2)}, u32[]{:S(2)}) collective-permute-start(f32[520,256]{1,0:T(8,128)S(1)} %pad_maximum_fusion.9), channel_id=1, source_target_pairs={{0,2},{1,3},{2,0},{3,1},{4,6},{5,7},{6,4},{7,5},{8,10},{9,11},{10,... | collective-permute-start | bytes 1597448 | tf_op jit(solution)/shard_map/ppermute | solution.py:40
  34.1 91.2 %collective-permute-start = (f32[4104,256]{1,0:T(8,128)}, f32[4104,256]{1,0:T(8,128)}, u32[]{:S(2)}, u32[]{:S(2)}) collective-permute-start(f32[4104,256]{1,0:T(8,128)} %pad_maximum_fusion.4), channel_id=1, source_target_pairs={{0,1},{1,0},{2,3},{3,2},{4,5},{5,4},{6,7},{7,6},{8,9},{9,8},{10,11... | collective-permute-start | bytes 12607496 | tf_op jit(solution)/shard_map/ppermute | solution.py:40
  34.1 75.9 %copy-start.69 = (s32[4]{0:T(128)S(1)}, s32[4]{0:T(128)}, u32[]{:S(2)}) copy-start(s32[4]{0:T(128)} %param.12) | copy-start | bytes 52
  110.0 15.3 %collective-permute-start.2 = (f32[4104,256]{1,0:T(8,128)}, f32[4104,256]{1,0:T(8,128)}, u32[]{:S(2)}, u32[]{:S(2)}) collective-permute-start(f32[4104,256]{1,0:T(8,128)} %pad_maximum_fusion.5), channel_id=1, source_target_pairs={{0,1},{1,0},{2,3},{3,2},{4,5},{5,4},{6,7},{7,6},{8,9},{9,8},{10,11... | collective-permute-start | bytes 12607496 | tf_op jit(solution)/shard_map/ppermute | solution.py:40
  110.1 9.5 %copy-start.55 = (f32[4,512]{1,0:T(4,128)}, f32[4,512]{1,0:T(4,128)S(1)}, u32[]{:S(2)}) copy-start(f32[4,512]{1,0:T(4,128)S(1)} %get-tuple-element.87) | copy-start | bytes 24580
  110.1 58.9 %copy-start.53 = (f32[1,4,2,128]{3,1,2,0:T(4,128)}, f32[1,4,2,128]{3,1,2,0:T(4,128)S(1)}, u32[]{:S(2)}) copy-start(f32[1,4,2,128]{3,1,2,0:T(4,128)S(1)} %copy.100) | copy-start | bytes 12292
  141.9 9.3 %copy-start.26 = (bf16[1024,768]{1,0:T(8,128)(2,1)}, bf16[1024,768]{1,0:T(8,128)(2,1)S(1)}, u32[]{:S(2)}) copy-start(bf16[1024,768]{1,0:T(8,128)(2,1)S(1)} %convert_element_type.113) | copy-start | bytes 4718596
  175.7 9.0 %collective-permute-start.3 = (f32[4,2,2,256]{3,2,1,0:T(2,128)S(1)}, f32[4,2,2,256]{3,2,1,0:T(2,128)S(1)}, u32[]{:S(2)}, u32[]{:S(2)}) collective-permute-start(f32[4,2,2,256]{3,2,1,0:T(2,128)S(1)} %slice.199), channel_id=1, source_target_pairs={{0,4},{4,8},{8,12},{12,16},{16,20},{20,24},{24,28},{1,5},{5,9},{9,... | collective-permute-start | bytes 49160 | tf_op jit(solution)/shard_map/ppermute | solution.py:36
  183.7 10.8 %copy-start.32 = (bf16[256,1024]{1,0:T(8,128)(2,1)}, bf16[256,1024]{1,0:T(8,128)(2,1)S(1)}, u32[]{:S(2)}) copy-start(bf16[256,1024]{1,0:T(8,128)(2,1)S(1)} %convert_element_type.118) | copy-start | bytes 1572868
  184.0 11.3 %copy-start.38 = (bf16[256,1024]{1,0:T(8,128)(2,1)}, bf16[256,1024]{1,0:T(8,128)(2,1)S(1)}, u32[]{:S(2)}) copy-start(bf16[256,1024]{1,0:T(8,128)(2,1)S(1)} %convert_element_type.116) | copy-start | bytes 1572868
  184.3 11.7 %copy-start.34 = (bf16[256,1024]{1,0:T(8,128)(2,1)}, bf16[256,1024]{1,0:T(8,128)(2,1)S(1)}, u32[]{:S(2)}) copy-start(bf16[256,1024]{1,0:T(8,128)(2,1)S(1)} %convert_element_type.120) | copy-start | bytes 1572868
  184.7 12.2 %copy-start.36 = (bf16[256,1024]{1,0:T(8,128)(2,1)}, bf16[256,1024]{1,0:T(8,128)(2,1)S(1)}, u32[]{:S(2)}) copy-start(bf16[256,1024]{1,0:T(8,128)(2,1)S(1)} %convert_element_type.122) | copy-start | bytes 1572868
  199.8 56.8 %copy-start.49 = (f32[1024]{0:T(1024)}, f32[1024]{0:T(1024)S(1)}, u32[]{:S(2)}) copy-start(f32[1024]{0:T(1024)S(1)} %add_rsqrt_fusion) | copy-start | bytes 12292
  203.0 53.6 %collective-permute-start.4 = (f32[1024,1024]{0,1:T(8,128)}, f32[1024,1024]{0,1:T(8,128)}, u32[]{:S(2)}, u32[]{:S(2)}) collective-permute-start(f32[1024,1024]{0,1:T(8,128)} %broadcast_multiply_fusion.1), channel_id=1, source_target_pairs={{0,1},{1,0},{2,3},{3,2},{4,5},{5,4},{6,7},{7,6},{8,9},{9,8},{10,11... | collective-permute-start | bytes 12582920 | tf_op jit(solution)/shard_map/ppermute | solution.py:40
  604.4 23.3 %collective-permute-start.6 = (f32[4,2,2,256]{3,2,1,0:T(2,128)S(1)}, f32[4,2,2,256]{3,2,1,0:T(2,128)S(1)}, u32[]{:S(2)}, u32[]{:S(2)}) collective-permute-start(f32[4,2,2,256]{3,2,1,0:T(2,128)S(1)} %slice.206), channel_id=1, source_target_pairs={{4,0},{8,4},{12,8},{16,12},{20,16},{24,20},{28,24},{5,1},{9,5},{13... | collective-permute-start | bytes 49160 | tf_op jit(solution)/shard_map/ppermute | solution.py:36
  618.8 8.8 copy-start.60
  618.9 8.8 copy-start.62
  618.9 8.8 copy-start.64
  627.6 93.2 %collective-permute-start.5 = (f32[1024,1024]{0,1:T(8,128)}, f32[1024,1024]{0,1:T(8,128)}, u32[]{:S(2)}, u32[]{:S(2)}) collective-permute-start(f32[1024,1024]{0,1:T(8,128)} %add_add_fusion.1), channel_id=1, source_target_pairs={{0,1},{1,0},{2,3},{3,2},{4,5},{5,4},{6,7},{7,6},{8,9},{9,8},{10,11... | collective-permute-start | bytes 12582920 | tf_op jit(solution)/shard_map/ppermute | solution.py:40
  654.5 8.3 copy-start.41
  662.3 80.9 %collective-permute-start.7 = (f32[1024,1024]{0,1:T(8,128)}, f32[1024,1024]{0,1:T(8,128)}, u32[]{:S(2)}, u32[]{:S(2)}) collective-permute-start(f32[1024,1024]{0,1:T(8,128)} %multiply_add_fusion), channel_id=1, source_target_pairs={{0,1},{1,0},{2,3},{3,2},{4,5},{5,4},{6,7},{7,6},{8,9},{9,8},{10,11... | collective-permute-start | bytes 12582920 | tf_op jit(solution)/shard_map/ppermute | solution.py:40
  670.4 90.5 %collective-permute-start.8 = (f32[8704,128]{1,0:T(8,128)}, f32[8704,128]{1,0:T(8,128)}, u32[]{:S(2)}, u32[]{:S(2)}) collective-permute-start(f32[8704,128]{1,0:T(8,128)} %select_maximum_fusion), channel_id=1, source_target_pairs={{0,1},{1,0},{2,3},{3,2},{4,5},{5,4},{6,7},{7,6},{8,9},{9,8},{10,11... | collective-permute-start | bytes 13369352 | tf_op jit(solution)/shard_map/ppermute | solution.py:40
  728.0 9.3 %copy-start.56 = (f32[4,512]{1,0:T(4,128)S(1)}, f32[4,512]{1,0:T(4,128)}, u32[]{:S(2)}) copy-start(f32[4,512]{1,0:T(4,128)} %copy-done.55) | copy-start | bytes 24580
  (61 other events, 260.6 us)
Sparse Core Ops, SparseCore 0:
  30.6 74.8 all-gather.1

commit v3 on v2

--- a/solution.py
+++ b/solution.py
@@ -38,6 +38,25 @@
 
 def swap_tp(block, bit):
     return lax.ppermute(block, "tp", [(i, i ^ bit) for i in range(lax.axis_size("tp"))])
+
+
+def greet_seq(places, others=()):
+    barrier = pltpu.get_barrier_semaphore()
+    here = lax.axis_index("seq")
+    place, side = here // 2, lax.rem(here, 2)
+
+    def signal(device):
+        pl.semaphore_signal(
+            barrier, inc=1, device_id=device, device_id_type=pl.DeviceIdType.MESH
+        )
+
+    signal({"seq": here + 1 - 2 * side})
+    for other in others:
+        signal(other)
+    pl.when(place > 0)(lambda: signal({"seq": here - 2}))
+    pl.when(place < places - 1)(lambda: signal({"seq": here + 2}))
+    ends = jnp.where(place > 0, 1, 0) + jnp.where(place < places - 1, 1, 0)
+    pl.semaphore_wait(barrier, 1 + len(others) + ends)
 
 
 class SeqSum:
@@ -48,32 +67,6 @@
         self.sems = scratch[8]
         here = lax.axis_index("seq")
         self.place, self.side = here // 2, here % 2
-
-    def greet(self, others=()):
-        barrier = pltpu.get_barrier_semaphore()
-        place, side = self.place, self.side
-
-        def signal(index):
-            pl.semaphore_signal(
-                barrier, inc=1, device_id={"seq": index}, device_id_type=pl.DeviceIdType.MESH
-            )
-
-        signal(place * 2 + 1 - side)
-        for other in others:
-            pl.semaphore_signal(
-                barrier, inc=1, device_id=other, device_id_type=pl.DeviceIdType.MESH
-            )
-
-        @pl.when(place > 0)
-        def _():
-            signal((place - 1) * 2 + side)
-
-        @pl.when(place < self.places - 1)
-        def _():
-            signal((place + 1) * 2 + side)
-
-        ends = jnp.where(place > 0, 1, 0) + jnp.where(place < self.places - 1, 1, 0)
-        pl.semaphore_wait(barrier, 1 + len(others) + ends)
 
     def remote(self, src, dst, slot, send, recv, place, side):
         return pltpu.make_async_remote_copy(
@@ -306,7 +299,7 @@
 
 def seq_sum_kernel(places, own, out, *scratch):
     summer = SeqSum(places, own, out, scratch)
-    summer.greet()
+    greet_seq(places)
     summer.run(own.shape[0] // (4 * HALF))
 
 
@@ -363,7 +356,7 @@
     ]
     for load in loads:
         load.start()
-    summer.greet(({"tp": sibling}, {"tp": across}))
+    greet_seq(places, ({"tp": sibling}, {"tp": across}))
     count = own.shape[0] // (4 * HALF)
     for load in loads[:4]:
         load.wait()
@@ -540,6 +533,204 @@
     )(normed_mid, normed_mid.T, grad_ffn, grad_ffn.T, w_gu, w_d)
 
 
+def gather_kernel(places, w_in, w_out, taps, full_in, full_out, full_taps, *scratch):
+    own_in, own_out, far_in, far_out, sib_in, sib_out, sibfar_in, sibfar_out = scratch[0:8]
+    own_taps, far_taps, sib_taps, sibfar_taps, share_in, share_out = scratch[8:14]
+    sends, recvs, once = scratch[14:17]
+    here = lax.axis_index("seq")
+    place, side = here // 2, lax.rem(here, 2)
+    last = places - 1
+    tp_at = lax.axis_index("tp")
+    core = lax.rem(tp_at, 2)
+    sibling = tp_at + 1 - 2 * core
+    across = lax.rem(tp_at + 2, 4)
+    far_sibling = sibling + across - tp_at
+    in_rows = w_in.shape[0] // (2 * places)
+    out_rows = w_out.shape[0] // (2 * places)
+    chans = w_in.shape[1] // 3
+    width = w_out.shape[1]
+
+    greet_seq(places, ({"tp": sibling}, {"tp": across}))
+
+    def shares(j):
+        return (
+            pl.ds(pl.multiple_of(j * in_rows, in_rows), in_rows),
+            pl.ds(pl.multiple_of(j * out_rows, out_rows), out_rows),
+        )
+
+    def copies(source, target, j, kind, device):
+        for i, at in enumerate(shares(j)):
+            yield pltpu.make_async_remote_copy(
+                src_ref=source[i] if kind == 0 else source[i].at[at],
+                dst_ref=target[i].at[at],
+                send_sem=sends.at[kind, i, j],
+                recv_sem=recvs.at[0 if kind < 4 else 1, i, j],
+                device_id=device,
+                device_id_type=pl.DeviceIdType.MESH,
+            )
+
+    share, far, sibfar = (share_in, share_out), (far_in, far_out), (sibfar_in, sibfar_out)
+
+    def across_share():
+        return copies(share, far, here, 0, {"tp": across})
+
+    def to_right(j):
+        return copies(far, far, j, 1, {"seq": here + 2})
+
+    def to_left(j):
+        return copies(far, far, j, 2, {"seq": here - 2})
+
+    def to_side(j):
+        return copies(far, far, j, 3, {"seq": here + 1 - 2 * side})
+
+    def to_sibling(j):
+        return copies(far, sibfar, j, 4, {"tp": sibling})
+
+    def start(group):
+        for copy in group:
+            copy.start()
+
+    def arrived(group):
+        for copy in group:
+            copy.wait_recv()
+
+    def left_source(group):
+        for copy in group:
+            copy.wait_send()
+
+    def single(i, src, dst, device):
+        return pltpu.make_async_remote_copy(
+            src_ref=src,
+            dst_ref=dst,
+            send_sem=once.at[0, i],
+            recv_sem=once.at[1, i],
+            device_id=device,
+            device_id_type=pl.DeviceIdType.MESH,
+        )
+
+    for source, held, at in zip((w_in, w_out), share, shares(here)):
+        held[...] = source[at, :].astype(jnp.float32)
+    start(across_share())
+    own_taps[...] = taps[...]
+    taps_far = single(0, own_taps, far_taps, {"tp": across})
+    taps_sib = single(1, own_taps, sib_taps, {"tp": sibling})
+    taps_sibfar = single(2, far_taps, sibfar_taps, {"tp": sibling})
+    own_in[...] = w_in[...].astype(jnp.float32)
+    own_out[...] = w_out[...].astype(jnp.float32)
+    in_sib = single(3, own_in, sib_in, {"tp": sibling})
+    out_sib = single(4, own_out, sib_out, {"tp": sibling})
+    for copy in (taps_far, taps_sib, in_sib, out_sib):
+        copy.start()
+
+    arrived(across_share())
+    start(to_side(here))
+    pl.when(place < last)(lambda: start(to_right(here)))
+    pl.when(place > 0)(lambda: start(to_left(here)))
+    start(to_sibling(here))
+    taps_far.wait_recv()
+    taps_sibfar.start()
+
+    def place_shard(shard_in, shard_out, shard_taps, index):
+        for g in range(3):
+            cols = pl.ds(pl.multiple_of(g * width + index * chans, LANES), chans)
+            full_in[:, cols] = shard_in[:, g * chans : (g + 1) * chans].astype(jnp.bfloat16)
+        rows = pl.ds(pl.multiple_of(index * chans, chans), chans)
+        full_out[rows, :] = shard_out[...].astype(jnp.bfloat16)
+        cols = pl.ds(pl.multiple_of(index * chans, LANES), chans)
+        full_taps[:, cols] = shard_taps[...]
+
+    def from_side(q):
+        j = 2 * q + 1 - side
+        arrived(to_side(j))
+        start(to_sibling(j))
+
+    @pl.loop(1, places)
+    def _(d):
+        @pl.when(place - d >= 0)
+        def _():
+            j = here - 2 * d
+            arrived(to_right(j))
+            pl.when(place < last)(lambda: start(to_right(j)))
+            start(to_side(j))
+            start(to_sibling(j))
+
+        @pl.when(place + d <= last)
+        def _():
+            j = here + 2 * d
+            arrived(to_left(j))
+            pl.when(place > 0)(lambda: start(to_left(j)))
+            start(to_side(j))
+            start(to_sibling(j))
+
+        @pl.when(d == 1)
+        def _():
+            from_side(place)
+            place_shard(own_in, own_out, own_taps, tp_at)
+            in_sib.wait_recv()
+            out_sib.wait_recv()
+            taps_sib.wait_recv()
+            place_shard(sib_in, sib_out, sib_taps, sibling)
+
+        pl.when(place - d >= 0)(lambda: from_side(place - d))
+        pl.when(place + d <= last)(lambda: from_side(place + d))
+
+    place_shard(far_in, far_out, far_taps, across)
+    taps_sibfar.wait_recv()
+
+    @pl.loop(0, 2 * places)
+    def _(j):
+        arrived(to_sibling(j))
+
+    place_shard(sibfar_in, sibfar_out, sibfar_taps, far_sibling)
+
+    left_source(across_share())
+    for copy in (taps_far, taps_sib, taps_sibfar, in_sib, out_sib):
+        copy.wait_send()
+
+    @pl.loop(0, places)
+    def _(q):
+        j = 2 * q + side
+        left_source(to_side(j))
+        pl.when((q <= place) & (place < last))(lambda: left_source(to_right(j)))
+        pl.when((q >= place) & (place > 0))(lambda: left_source(to_left(j)))
+        left_source(to_sibling(j))
+        left_source(to_sibling(2 * q + 1 - side))
+
+
+def gather_mixer(w_in, w_out, taps, collective_id):
+    width, _, chans = w_in.shape
+    count = lax.axis_size("seq")
+    group = lax.axis_size("tp")
+    f32 = jnp.float32
+    pair = [pltpu.VMEM((width, 3 * chans), f32), pltpu.VMEM((chans, width), f32)]
+    whole = pl.BlockSpec(memory_space=pltpu.VMEM)
+    return pl.pallas_call(
+        functools.partial(gather_kernel, count // 2),
+        out_shape=[
+            jax.ShapeDtypeStruct((width, 3 * chans * group), jnp.bfloat16),
+            jax.ShapeDtypeStruct((chans * group, width), jnp.bfloat16),
+            jax.ShapeDtypeStruct((8, chans * group), f32),
+        ],
+        in_specs=[whole] * 3,
+        out_specs=[whole] * 3,
+        scratch_shapes=pair * 4
+        + [pltpu.VMEM((8, chans), f32)] * 4
+        + [
+            pltpu.VMEM((width // count, 3 * chans), f32),
+            pltpu.VMEM((chans // count, width), f32),
+        ]
+        + [
+            pltpu.SemaphoreType.DMA((5, 2, count)),
+            pltpu.SemaphoreType.DMA((2, 2, count)),
+            pltpu.SemaphoreType.DMA((2, 5)),
+        ],
+        compiler_params=pltpu.CompilerParams(
+            collective_id=collective_id, has_side_effects=True, vmem_limit_bytes=48 << 20
+        ),
+        name="gather_mixer",
+    )(w_in.reshape(width, 3 * chans), w_out, jnp.pad(taps, ((0, 5), (0, 0))))
+
+
 def to_panels(matrix):
     rows, cols = matrix.shape
     return matrix.reshape(rows, cols // LANES, LANES).transpose(1, 0, 2).reshape(-1, LANES)
@@ -570,33 +761,7 @@
             [pick(core == 0, own, other), pick(core == 0, other, own)], axis=0
         )
 
-    flat = jnp.concatenate([w_in.reshape(3 * width, chans), w_out.reshape(width, chans)], axis=0)
-    taps8 = jnp.pad(conv_weight, ((0, 5), (0, 0)))
-    share_rows = flat.shape[0] // seq_count
-    share = lax.dynamic_slice(flat, (seq_at * share_rows, 0), (share_rows, chans))
-    sent = jnp.concatenate([share.astype(jnp.float32), taps8], axis=0)
-    sent = swap_tp(sent, 2)
-    across = lax.all_gather(sent[:share_rows], "seq", axis=0, tiled=True)
-    own_flat = jnp.concatenate([flat.astype(jnp.float32), taps8], axis=0)
-    across_flat = jnp.concatenate([across, sent[share_rows:]], axis=0)
-    sib_own = swap_tp(own_flat, 1)
-    sib_across = swap_tp(across_flat, 1)
-    pair_own = [pick(core == 0, own_flat, sib_own), pick(core == 0, sib_own, own_flat)]
-    pair_across = [
-        pick(core == 0, across_flat, sib_across),
-        pick(core == 0, sib_across, across_flat),
-    ]
-    quad = [pick(chip == 0, a, b) for a, b in zip(pair_own, pair_across)] + [
-        pick(chip == 0, b, a) for a, b in zip(pair_own, pair_across)
-    ]
-    quad = lax.optimization_barrier(quad)
-    taps = jnp.stack([q[4 * width : 4 * width + 3] for q in quad])
-    w_in_all = jnp.stack(
-        [q[: 3 * width].reshape(width, 3 * chans).astype(jnp.bfloat16) for q in quad]
-    )
-    w_out_all = jnp.stack(
-        [q[3 * width : 4 * width].reshape(chans, width).astype(jnp.bfloat16) for q in quad]
-    )
+    w_in_all, w_out_all, taps = gather_mixer(w_in, w_out, conv_weight, 3)
 
     first_pos = seq_at * local_len
     positions = first_pos + jnp.arange(local_len, dtype=jnp.int32)
@@ -611,33 +776,21 @@
     scale_mix = rms_scale(inputs_f)
     unit_mix = inputs_f * scale_mix
     normed_in = (gain_mix * unit_mix).astype(jnp.bfloat16)
-    projected = jnp.stack(
-        [
-            jnp.dot(normed_in, w_in_all[j], preferred_element_type=jnp.float32)
-            for j in range(group)
-        ]
-    )
-    in_gate = projected[:, :, :chans]
-    out_gate = projected[:, :, chans : 2 * chans]
-    conv_value = projected[:, :, 2 * chans :]
-    seq_shape = (group, half_slots, local_len, chans)
+    projected = jnp.dot(normed_in, w_in_all, preferred_element_type=jnp.float32)
+    in_gate = projected[:, :width]
+    out_gate = projected[:, width : 2 * width]
+    conv_value = projected[:, 2 * width :]
+    seq_shape = (half_slots, local_len, width)
     gated_seq = (valid_rows * in_gate * conv_value).reshape(seq_shape)
-    carried = shift_seq(gated_seq[:, :, local_len - 2 :], 1)
-    padded_seq = jnp.concatenate([carried, gated_seq], axis=2)
-
-    def tap(j):
-        return taps[:, j][:, None, None, :]
-
+    carried = shift_seq(gated_seq[:, local_len - 2 :], 1)
+    padded_seq = jnp.concatenate([carried, gated_seq], axis=1)
     conv_sum = (
-        tap(0) * padded_seq[:, :, 0:local_len]
-        + tap(1) * padded_seq[:, :, 1 : local_len + 1]
-        + tap(2) * padded_seq[:, :, 2 : local_len + 2]
-    ).reshape(group, half_rows, chans)
+        taps[0] * padded_seq[:, 0:local_len]
+        + taps[1] * padded_seq[:, 1 : local_len + 1]
+        + taps[2] * padded_seq[:, 2 : local_len + 2]
+    ).reshape(half_rows, width)
     mixed_seq = (out_gate * conv_sum).astype(jnp.bfloat16)
-    mixer_out = sum(
-        jnp.dot(mixed_seq[j], w_out_all[j], preferred_element_type=jnp.float32)
-        for j in range(group)
-    )
+    mixer_out = jnp.dot(mixed_seq, w_out_all, preferred_element_type=jnp.float32)
     hidden_res = inputs_f + mixer_out
     scale_ffn = rms_scale(hidden_res)
     unit_ffn = hidden_res * scale_ffn
@@ -666,29 +819,25 @@
     )
 
     grad_mixer = grad_hidden.astype(jnp.bfloat16)
-    grad_mixed = jnp.stack([dot_cols(grad_mixer, w_out_all[j]) for j in range(group)])
+    grad_mixed = dot_cols(grad_mixer, w_out_all)
     grad_out_gate = grad_mixed * conv_sum
     grad_conv_in = (grad_mixed * out_gate).reshape(seq_shape)
-    next_grad = shift_seq(grad_conv_in[:, :, :2], -1)
-    extended = jnp.concatenate([grad_conv_in, next_grad], axis=2)
+    next_grad = shift_seq(grad_conv_in[:, :2], -1)
+    extended = jnp.concatenate([grad_conv_in, next_grad], axis=1)
     grad_gated = (
-        tap(2) * extended[:, :, 0:local_len]
-        + tap(1) * extended[:, :, 1 : local_len + 1]
-        + tap(0) * extended[:, :, 2 : local_len + 2]
-    ).reshape(group, half_rows, chans)
+        taps[2] * extended[:, 0:local_len]
+        + taps[1] * extended[:, 1 : local_len + 1]
+        + taps[0] * extended[:, 2 : local_len + 2]
+    ).reshape(half_rows, width)
     grad_conv = jnp.stack(
-        [
-            jnp.sum(grad_conv_in * padded_seq[:, :, j : j + local_len], axis=(1, 2))
-            for j in range(3)
-        ],
-        axis=1,
+        [jnp.sum(grad_conv_in * padded_seq[:, j : j + local_len], axis=(0, 1)) for j in range(3)]
     )
     grad_in_gate = grad_gated * valid_rows * conv_value
     grad_value = grad_gated * valid_rows * in_gate
-    grad_proj = jnp.concatenate([grad_in_gate, grad_out_gate, grad_value], axis=2).astype(
+    grad_proj = jnp.concatenate([grad_in_gate, grad_out_gate, grad_value], axis=1).astype(
         jnp.bfloat16
     )
-    grad_in = sum(dot_cols(grad_proj[j], w_in_all[j]) for j in range(group))
+    grad_in = dot_cols(grad_proj, w_in_all)
     grad_gain_mix = jnp.sum(grad_in * unit_mix, axis=0)
     scaled_in = gain_mix * grad_in
     tokens_grad = grad_hidden + scale_mix * (
@@ -697,17 +846,18 @@
     grad_tokens = both_cores(tokens_grad, swap_tp(tokens_grad, 1))
     grad_tokens = grad_tokens.reshape(slot_count, local_len, width)
 
-    def shard_of(stacked, which):
-        at = chip * 2 + which
-        return lax.dynamic_slice(
-            stacked, (at,) + (0,) * (stacked.ndim - 1), (1,) + stacked.shape[1:]
-        )[0]
+    def chans_of(block, which):
+        first = (chip * 2 + which) * chans
+        return lax.dynamic_slice(block, (0, first), (block.shape[0], chans))
 
     def mixer_panels(which):
-        in_part = dot_rows(normed_in, shard_of(grad_proj, which))
-        out_part = dot_rows(shard_of(mixed_seq, which), grad_mixer)
+        proj = jnp.concatenate(
+            [chans_of(grad_proj[:, g * width : (g + 1) * width], which) for g in range(3)], axis=1
+        )
+        in_part = dot_rows(normed_in, proj)
+        out_part = dot_rows(chans_of(mixed_seq, which), grad_mixer)
         small = jnp.concatenate(
-            [grad_gain_mix, grad_gain_ffn, shard_of(grad_conv, which).reshape(-1)]
+            [grad_gain_mix, grad_gain_ffn, chans_of(grad_conv, which).reshape(-1)]
         ).reshape(-1, LANES)
         pad = -small.shape[0] % (4 * HALF)
         return jnp.concatenate(

time: 901 us -> 807 us (0.90)
  waiting for transfers between devices: 83.6 us -> 1.18 us
  Pallas kernels: 398 us -> 479 us
  local copies, waits for them, and re-layouts: 187 us -> 145 us
  other arithmetic: 141 us -> 120 us
  between operations: 15.4 us -> 1.86 us
    pallas_call x0 -> x1, Pallas kernels: none -> 78.2 us  [gather_mixer(): pl.pallas_call(functools.partial(gather_kernel, count // 2), out_shape=[j...]
    all_gather x1 -> x0, waiting for transfers between devices: 71.4 us -> none  [per_device(): across = lax.all_gather(sent[:share_rows], 'seq', axis=0, tiled=True)]
    unnamed x163 -> x109, local copies, waits for them, and re-layouts: 70.5 us -> 50.8 us
    ppermute x7 -> x4, waiting for transfers between devices: 12.1 us -> 0.01 us  [swap_tp(): lax.ppermute(block, 'tp', [(i, i ^ bit) for i in range(lax.axis_size('tp'...]
    slice x12 -> x3, local copies, waits for them, and re-layouts: 11.3 us -> 0.03 us  [the longest x1 0.01 us: per_device(): taps[0] * padded_seq[:, 0:local_len]]
    convert_element_type x8 -> x0, local copies, waits for them, and re-layouts: 10.6 us -> none  [the longest x4 9.37 us: per_device(): q[:3 * width].reshape(width, 3 * chans).astype(jnp.bfloat16)]
    slice x1 -> x2, other arithmetic: 0.01 us -> 10.2 us  [mixer_panels(): grad_proj[:, g * width:(g + 1) * width]]
    dot_general x8 -> x2, matrix products: 12.7 us -> 18.1 us  [dot_cols(): lax.dot_general(left, right, (((1,), (1,)), ((), ())), preferred_element_...]
  transfers between devices with their start and end apart: 10 -> 6, of which waited for: 2 -> 1; matrix products, arithmetic and copies ran while one was open for 26% -> 26% of each run, Pallas kernels for 0% -> 0%
where the time goes in v3:
time: 807 us; the launch traced here: 799 us
  Pallas kernels  479 us (59%)
  local copies, waits for them, and re-layouts  145 us (18%)
  other arithmetic  120 us (15%)
  matrix products  47.2 us (6%)
    pallas_call x1, Pallas kernels, ffn_both_ways(): pl.pallas_call(functools.partial(ffn_kernel, lax.axis_size('seq') // 2),...  300 us
    pallas_call x1, Pallas kernels, seq_sum(): pl.pallas_call(functools.partial(seq_sum_kernel, lax.axis_size('seq') //...  99.9 us
    pallas_call x1, Pallas kernels, gather_mixer(): pl.pallas_call(functools.partial(gather_kernel, count // 2), out_shape=[j...  78.2 us
    unnamed x109, local copies, waits for them, and re-layouts  50.8 us
    pallas_call x4, local copies, waits for them, and re-layouts, ffn_both_ways(): pl.pallas_call(functools.partial(ffn_kernel, lax.axis_size('seq') // 2),...  21.4 us
    dot_general x2, matrix products, dot_cols(): lax.dot_general(left, right, (((1,), (1,)), ((), ())), preferred_element_...  18.1 us
    transpose x2, local copies, waits for them, and re-layouts, per_device(): total_w_down = by_part[:, 2].transpose(0, 1, 3, 2).reshape(hidden, width)  16.7 us
  transfers between devices with their start and end apart: 6, of which 1 were waited for; matrix products, arithmetic and copies ran while one was open for 26% of the time, Pallas kernels for 0%

profile of v3, /device:TPU:0, one launch (start us, length us, event | category | flops | bytes accessed | tf_op | source)
XLA Modules:
  0.0 798.9 jit_solution(18047751621478514069)
XLA Ops:
  15.1 78.2 %gather_mixer.1 = (bf16[1024,3072]{1,0:T(8,128)(2,1)}, bf16[1024,1024]{1,0:T(8,128)(2,1)S(1)}, f32[8,1024]{1,0:T(8,128)S(1)}) custom-call(bf16[1024,768]{1,0:T(8,128)(2,1)S(1)} %copy.47.w_in, bf16[256,1024]{1,0:T(8,128)(2,1)S(1)} %copy-done.3, f32[8,256]{1,0:T(8,128)S(1)} %pad.11.taps), custom_call_target="tpu_custom_call" | custom-call | tf_op jit(solution)/shard_map/gather_mixer/pallas_call | solution.py:707
  93.4 11.3 %fusion.16 = f32[1024,3072]{1,0:T(8,128)S(1)} fusion(bf16[1024,3072]{1,0:T(8,128)(2,1)} %get-tuple-element.18, f32[1024,1024]{0,1:T(8,128)} %copy.82, f32[1024]{0:T(1024)S(1)} %bitcast.163, f32[1024]{0:T(1024)S(1)} %copy-done.42), kind=kOutput, calls=%fused_computation.55 | convolution fusion | flops 6445596672 | bytes 23076864 | tf_op jit(solution)/shard_map/dot_general | solution.py:779
  123.4 6.6 bitcast_convert_fusion
  130.0 9.2 %copy.83 = f32[2048,1024]{0,1:T(8,128)} copy(f32[2048,1024]{1,0:T(8,128)} %bitcast_convert_fusion) | data formatting | bytes 16777216 | tf_op jit(solution)/shard_map/reshape | solution.py:800
  139.2 10.2 %fusion.30 = (bf16[2048,1024]{0,1:T(8,128)(2,1)}, f32[2048,1024]{0,1:T(8,128)}) fusion(f32[2048,1024]{0,1:T(8,128)} %copy.83, f32[2048]{0:T(1024)S(1)} %bitcast.160), kind=kLoop, calls=%fused_computation.106 | loop fusion | flops 4194304 | bytes 20979712 | tf_op jit(solution)/shard_map/convert_element_type | solution.py:801
  149.4 6.5 copy.55.refs_2_
  180.7 6.4 copy.54.refs_0_
  187.1 300.5 %ffn_both_ways.1 = (f32[27648,128]{1,0:T(8,128)}, f32[1024,1024]{1,0:T(8,128)}, f32[1024,1024]{1,0:T(8,128)}, f32[1024,1024]{1,0:T(8,128)}, f32[1024,1024]{1,0:T...) custom-call(bf16[2048,1024]{1,0:T(8,128)(2,1)} %copy.54.refs_0_, bf16[1024,2048]{1,0:T(8,128)(2,1)} %bitcast.132, ...), custom_call_target="tpu_custom_call" | custom-call | flops 43486543872 | bytes 838860800 | tf_op jit(solution)/shard_map/ffn_both_ways/pallas_call | solution.py:502
  498.4 6.1 multiply_reduce_fusion.3
  510.4 9.4 %multiply_reduce_fusion.2 = (f32[1024]{0:T(1024)S(1)}, f32[1024]{0:T(1024)S(1)}, f32[1024,1024]{1,0:T(8,128)S(1)}, f32[1024,1024]{1,0:T(8,128)}) fusion(f32[2,512,1024]{2,1,0:T(8,128)} %bitcast.125, f32[2,2,1024]{2,1,0:T(2,128)S(1)} %copy-done.27, f32[1024,3072]{1,0:T(8,128)} %copy-done.9, bf16[1024,1024]{1,0:T(8,128)(2,1)S(1)} %copy-done.2, ...), kind=kOutput, calls=%fused_computation.37 | convolution fusion | flops 2155870208 | bytes 23093248 | tf_op jit(solution)/shard_map/dot_general | solution.py:28
  541.6 8.6 %add_add_fusion = f32[1024,1024]{0,1:T(8,128)} fusion(f32[1024,1024]{0,1:T(8,128)} %copy-done.4, f32[1024,1024]{0,1:T(8,128)} %copy.56, f32[1024,1024]{0,1:T(8,128)} %copy.57), kind=kLoop, calls=%fused_computation.47 | loop fusion | flops 2097152 | bytes 16777216 | tf_op jit(solution)/shard_map/add | solution.py:811
  564.4 8.7 %multiply_reduce_fusion.4 = (f32[1024]{0:T(1024)S(1)}, f32[1024]{0:T(1024)S(1)}, f32[1024,1024]{0,1:T(8,128)}) fusion(f32[1024,1024]{0,1:T(8,128)S(1)} %copy-done.15, f32[1024]{0:T(1024)S(1)} %bitcast.164, f32[1024]{0:T(1024)S(1)} %copy-done.43, bf16[1024,3072]{1,0:T(8,128)(2,1)S(1)} %bitcast.168, bf16[1024,1024]{1,0:T(8,128)(2,1)S(1)} %get-tuple-element.56, ...), kind=kOutput, calls=%fused_computation.39 | convolution fusion | flops 6467614720 | bytes 20987904 | tf_op jit(solution)/shard_map/dot_general | solution.py:28
  575.1 7.8 multiply_add_fusion
  592.9 10.6 %slice_bitcast_fusion = (f32[3,3,128,1024]{2,3,1,0:T(8,128)}, f32[3,1,3,1024,128]{4,3,2,1,0:T(8,128)}, f32[3,1,3,1024,128]{4,3,2,1,0:T(8,128)}) fusion(f32[3,3,3,1024,128]{4,3,2,1,0:T(8,128)} %bitcast.134), kind=kLoop, calls=%fused_computation.11 | loop fusion | bytes 28311552 | tf_op jit(solution)/shard_map/transpose | solution.py:874
  603.5 6.0 copy.88
  609.5 6.0 copy.76
  615.6 6.0 copy.89
  621.6 6.0 copy.77
  627.6 6.1 copy.73
  649.8 9.3 %copy.84 = f32[2048,1024]{1,0:T(8,128)} copy(f32[2048,1024]{0,1:T(8,128)} %pad_maximum_fusion) | data formatting | bytes 16777216 | tf_op jit(solution)/shard_map/concatenate | solution.py:760
  659.2 5.9 multiply_convert_fusion
  673.4 9.2 %copy.85 = f32[2048,1024]{1,0:T(8,128)} copy(f32[2048,1024]{0,1:T(8,128)} %pad_maximum_fusion.1) | data formatting | bytes 16777216
  682.7 6.1 fusion.7.own
  688.8 99.9 %sum_mixer_grads.1 = f32[8704,128]{1,0:T(8,128)S(1)} custom-call(f32[8704,128]{1,0:T(8,128)S(1)} %fusion.7.own), custom_call_target="tpu_custom_call" | custom-call | flops 2228224 | bytes 142606336 | tf_op jit(solution)/shard_map/sum_mixer_grads/pallas_call | solution.py:308
  (181 shorter events, 156.1 us)
Async XLA Ops:
  10.9 82.4 %copy-start.40 = (f32[1,4,2,128]{3,1,2,0:T(4,128)}, f32[1,4,2,128]{3,1,2,0:T(4,128)S(1)}, u32[]{:S(2)}) copy-start(f32[1,4,2,128]{3,1,2,0:T(4,128)S(1)} %copy.94) | copy-start | bytes 12292
  10.9 82.4 %copy-start.42 = (f32[1024]{0:T(1024)S(1)}, f32[1024]{0:T(1024)}, u32[]{:S(2)}) copy-start(f32[1024]{0:T(1024)} %param.13) | copy-start | bytes 12292
  15.1 89.7 %copy-start.28 = (f32[1,4,2,128]{3,1,2,0:T(4,128)}, f32[1,4,2,128]{3,1,2,0:T(4,128)S(1)}, u32[]{:S(2)}) copy-start(f32[1,4,2,128]{3,1,2,0:T(4,128)S(1)} %copy.95) | copy-start | bytes 12292
  93.3 21.0 %copy-start.1 = (bf16[1024,1024]{1,0:T(8,128)(2,1)}, bf16[1024,1024]{1,0:T(8,128)(2,1)S(1)}, u32[]{:S(2)}) copy-start(bf16[1024,1024]{1,0:T(8,128)(2,1)S(1)} %get-tuple-element.20) | copy-start | bytes 6291460
  104.7 7.6 copy-start.9
  105.2 4.3 collective-permute-start
  120.1 53.3 %copy-start.24 = (f32[1024]{0:T(1024)}, f32[1024]{0:T(1024)S(1)}, u32[]{:S(2)}) copy-start(f32[1024]{0:T(1024)S(1)} %add_rsqrt_fusion) | copy-start | bytes 12292
  123.3 50.1 %collective-permute-start.1 = (f32[1024,1024]{0,1:T(8,128)}, f32[1024,1024]{0,1:T(8,128)}, u32[]{:S(2)}, u32[]{:S(2)}) collective-permute-start(f32[1024,1024]{0,1:T(8,128)} %broadcast_multiply_fusion.1), channel_id=1, source_target_pairs={{0,1},{1,0},{2,3},{3,2},{4,5},{5,4},{6,7},{7,6},{8,9},{9,8},{10,11... | collective-permute-start | bytes 12582920 | tf_op jit(solution)/shard_map/ppermute | solution.py:40
  510.4 16.6 %copy-start.7 = (f32[1024,1024]{0,1:T(8,128)}, f32[1024,1024]{0,1:T(8,128)S(1)}, u32[]{:S(2)}) copy-start(f32[1024,1024]{0,1:T(8,128)S(1)} %multiply_add_fusion.1) | copy-start | bytes 12582916
  510.4 10.7 %copy-start.13 = (f32[2,512,1024]{2,1,0:T(8,128)S(1)}, f32[2,512,1024]{2,1,0:T(8,128)}, u32[]{:S(2)}) copy-start(f32[2,512,1024]{2,1,0:T(8,128)} %copy-done.12) | copy-start | bytes 12582916
  510.4 10.7 %copy-start.29 = (f32[1,4,2,128]{3,1,2,0:T(4,128)S(1)}, f32[1,4,2,128]{3,1,2,0:T(4,128)}, u32[]{:S(2)}) copy-start(f32[1,4,2,128]{3,1,2,0:T(4,128)} %copy-done.28) | copy-start | bytes 12292
  519.8 7.2 copy-start.11
  519.8 31.8 %collective-permute-start.3 = (f32[2,2,1024]{2,1,0:T(2,128)S(1)}, f32[2,2,1024]{2,1,0:T(2,128)S(1)}, u32[]{:S(2)}, u32[]{:S(2)}) collective-permute-start(f32[2,2,1024]{2,1,0:T(2,128)S(1)} %slice.119), channel_id=1, source_target_pairs={{4,0},{8,4},{12,8},{16,12},{20,16},{24,20},{28,24},{5,1},{9,5},{13... | collective-permute-start | bytes 49160 | tf_op jit(solution)/shard_map/ppermute | solution.py:36
  541.5 10.1 %copy-start.35 = (f32[1,1024]{1,0:T(1,128)S(1)}, f32[1,1024]{1,0:T(1,128)}, u32[]{:S(2)}) copy-start(f32[1,1024]{1,0:T(1,128)} %copy-done.34) | copy-start | bytes 12292
  541.6 10.1 %copy-start.37 = (f32[1,1024]{1,0:T(1,128)S(1)}, f32[1,1024]{1,0:T(1,128)}, u32[]{:S(2)}) copy-start(f32[1,1024]{1,0:T(1,128)} %copy-done.36) | copy-start | bytes 12292
  541.6 10.1 %copy-start.39 = (f32[1,1024]{1,0:T(1,128)S(1)}, f32[1,1024]{1,0:T(1,128)}, u32[]{:S(2)}) copy-start(f32[1,1024]{1,0:T(1,128)} %copy-done.38) | copy-start | bytes 12292
  551.6 91.1 %collective-permute-start.2 = (f32[1024,1024]{0,1:T(8,128)}, f32[1024,1024]{0,1:T(8,128)}, u32[]{:S(2)}, u32[]{:S(2)}) collective-permute-start(f32[1024,1024]{0,1:T(8,128)} %add_add_fusion), channel_id=1, source_target_pairs={{0,1},{1,0},{2,3},{3,2},{4,5},{5,4},{6,7},{7,6},{8,9},{9,8},{10,11... | collective-permute-start | bytes 12582920 | tf_op jit(solution)/shard_map/ppermute | solution.py:40
  551.7 11.5 %slice-start.2 = ((s8[6291456]{0:T(1024)(128)(4,1)}), s8[4194304]{0:T(1024)(128)(4,1)S(1)}, s32[]{:S(2)}) async-start(s8[6291456]{0:T(1024)(128)(4,1)} %bitcast.167), calls=%async_computation.2 | async-start | bytes 8388608
  564.4 8.7 %copy-start.21 = (bf16[1024,256]{1,0:T(8,128)(2,1)S(1)}, bf16[1024,256]{1,0:T(8,128)(2,1)}, u32[]{:S(2)}) copy-start(bf16[1024,256]{1,0:T(8,128)(2,1)} %get-tuple-element.71) | copy-start | bytes 1572868
  575.1 8.3 %copy-start.19 = (bf16[2,512,1024]{2,1,0:T(8,128)(2,1)S(1)}, bf16[2,512,1024]{2,1,0:T(8,128)(2,1)}, u32[]{:S(2)}) copy-start(bf16[2,512,1024]{2,1,0:T(8,128)(2,1)} %multiply_convert_fusion.1) | copy-start | bytes 6291460
  575.1 8.3 %copy-start.23 = (bf16[768,1024]{1,0:T(8,128)(2,1)S(1)}, bf16[768,1024]{1,0:T(8,128)(2,1)}, u32[]{:S(2)}) copy-start(bf16[768,1024]{1,0:T(8,128)(2,1)} %copy.66) | copy-start | bytes 4718596
  582.9 82.2 %collective-permute-start.4 = (f32[1024,1024]{0,1:T(8,128)}, f32[1024,1024]{0,1:T(8,128)}, u32[]{:S(2)}, u32[]{:S(2)}) collective-permute-start(f32[1024,1024]{0,1:T(8,128)} %multiply_add_fusion), channel_id=1, source_target_pairs={{0,1},{1,0},{2,3},{3,2},{4,5},{5,4},{6,7},{7,6},{8,9},{9,8},{10,11... | collective-permute-start | bytes 12582920 | tf_op jit(solution)/shard_map/ppermute | solution.py:40
  591.0 91.7 %collective-permute-start.5 = (f32[8704,128]{1,0:T(8,128)}, f32[8704,128]{1,0:T(8,128)}, u32[]{:S(2)}, u32[]{:S(2)}) collective-permute-start(f32[8704,128]{1,0:T(8,128)} %select_maximum_fusion), channel_id=1, source_target_pairs={{0,1},{1,0},{2,3},{3,2},{4,5},{5,4},{6,7},{7,6},{8,9},{9,8},{10,11... | collective-permute-start | bytes 13369352 | tf_op jit(solution)/shard_map/ppermute | solution.py:40
  649.8 9.3 %copy-start.31 = (f32[4,512]{1,0:T(4,128)S(1)}, f32[4,512]{1,0:T(4,128)}, u32[]{:S(2)}) copy-start(f32[4,512]{1,0:T(4,128)} %copy-done.30) | copy-start | bytes 24580
  (32 other events, 131.6 us)

commit v4 on v3

--- a/solution.py
+++ b/solution.py
@@ -40,7 +40,7 @@
     return lax.ppermute(block, "tp", [(i, i ^ bit) for i in range(lax.axis_size("tp"))])
 
 
-def greet_seq(places, others=()):
+def greet_seq(places, others=(), more=0):
     barrier = pltpu.get_barrier_semaphore()
     here = lax.axis_index("seq")
     place, side = here // 2, lax.rem(here, 2)
@@ -56,7 +56,7 @@
     pl.when(place > 0)(lambda: signal({"seq": here - 2}))
     pl.when(place < places - 1)(lambda: signal({"seq": here + 2}))
     ends = jnp.where(place > 0, 1, 0) + jnp.where(place < places - 1, 1, 0)
-    pl.semaphore_wait(barrier, 1 + len(others) + ends)
+    pl.semaphore_wait(barrier, 1 + len(others) + ends + more)
 
 
 class SeqSum:
@@ -297,30 +297,7 @@
     return [half] * 4 + [wide] * 4 + [pltpu.SemaphoreType.DMA((20, SLOTS_IN_FLIGHT))]
 
 
-def seq_sum_kernel(places, own, out, *scratch):
-    summer = SeqSum(places, own, out, scratch)
-    greet_seq(places)
-    summer.run(own.shape[0] // (4 * HALF))
-
-
-def seq_sum(block, collective_id, name):
-    rows = block.shape[0]
-    return pl.pallas_call(
-        functools.partial(seq_sum_kernel, lax.axis_size("seq") // 2),
-        out_shape=jax.ShapeDtypeStruct(block.shape, jnp.float32),
-        in_specs=[pl.BlockSpec(memory_space=pltpu.VMEM)],
-        out_specs=pl.BlockSpec(memory_space=pl.ANY),
-        scratch_shapes=seq_sum_scratch(),
-        compiler_params=pltpu.CompilerParams(
-            collective_id=collective_id, has_side_effects=True, vmem_limit_bytes=40 << 20
-        ),
-        cost_estimate=pl.CostEstimate(
-            flops=rows * 256, bytes_accessed=rows * 512 * 32, transcendentals=0
-        ),
-        name=name,
-    )(block)
-
-
+FFN_PIECES = 36
 FFN_PARTS = 3
 ROW_BLOCK = 512
 OUT_BLOCK = 256
@@ -328,7 +305,7 @@
 
 def ffn_kernel(places, *refs):
     (mid_hbm, mid_t_hbm, cot_hbm, cot_t_hbm, w_gu_hbm, w_d_hbm) = refs[0:6]
-    (sums, mid_chip, mid_far, ffn_chip, ffn_far, mid_land, ffn_land) = refs[6:13]
+    (sums, rest, mid_chip, mid_far, ffn_chip, mid_land, ffn_land) = refs[6:13]
     (mid, mid_t, cot, cot_t, w_gu, w_d, act, ggu, own, staged, fetched) = refs[13:24]
     load_sems, near_sems, far_sems, keep_sem, fetch_sem = refs[24:29]
     summer = SeqSum(places, own, sums, refs[29:])
@@ -357,7 +334,7 @@
     for load in loads:
         load.start()
     greet_seq(places, ({"tp": sibling}, {"tp": across}))
-    count = own.shape[0] // (4 * HALF)
+    count = FFN_PIECES
     for load in loads[:4]:
         load.wait()
 
@@ -407,6 +384,10 @@
 
     early = (parts - 1) * (width // OUT_BLOCK)
     blocks = rows // 2 // OUT_BLOCK
+    for_later = pltpu.make_async_copy(
+        own.at[pl.ds(count * 4 * HALF, rest.shape[0])], rest, load_sems.at[0]
+    )
+    for_later.start()
 
     def row_block(half, k):
         return pl.ds(pl.multiple_of((half * blocks + k) * OUT_BLOCK, OUT_BLOCK), OUT_BLOCK)
@@ -434,17 +415,17 @@
             device_id_type=pl.DeviceIdType.MESH,
         )
 
-    def far(which, chip, there, k):
+    def far(k):
         return pltpu.make_async_remote_copy(
-            src_ref=chip.at[row_block(0, k)],
-            dst_ref=there.at[row_block(0, k)],
-            send_sem=far_sems.at[which, 0, k],
-            recv_sem=far_sems.at[which, 1, k],
+            src_ref=mid_chip.at[row_block(0, k)],
+            dst_ref=mid_far.at[row_block(0, k)],
+            send_sem=far_sems.at[0, k],
+            recv_sem=far_sems.at[1, k],
             device_id={"tp": across},
             device_id_type=pl.DeviceIdType.MESH,
         )
 
-    def tp_sum(which, part, land, chip, there, first_tick):
+    def tp_sum(which, part, land, chip, first_tick):
         @pl.loop(0, blocks)
         def _(k):
             @pl.when(k >= 2)
@@ -469,20 +450,21 @@
             keep.start()
             summer.tick(first_tick + k, count)
             keep.wait()
-            far(which, chip, there, k).start()
-
-    tp_sum(0, mid_part, mid_land, mid_chip, mid_far, early)
-    tp_sum(1, ffn_part, ffn_land, ffn_chip, ffn_far, early + blocks)
+            if which == 0:
+                far(k).start()
+
+    tp_sum(0, mid_part, mid_land, mid_chip, early)
+    tp_sum(1, ffn_part, ffn_land, ffn_chip, early + blocks)
 
     @pl.loop(early + 2 * blocks, count + summer.P_LAGS[-1][1])
     def _(t):
         summer.tick(t, count)
 
-    for which, chip, there in ((0, mid_chip, mid_far), (1, ffn_chip, ffn_far)):
-
-        @pl.loop(0, blocks)
-        def _(k, which=which, chip=chip, there=there):
-            far(which, chip, there, k).wait()
+    for_later.wait()
+
+    @pl.loop(0, blocks)
+    def _(k):
+        far(k).wait()
 
 
 def ffn_both_ways(normed_mid, grad_ffn, w_gate, w_up, w_down, collective_id):
@@ -496,12 +478,17 @@
     w_gu = jnp.concatenate([in_parts(w_gate), in_parts(w_up)], axis=2).transpose(1, 0, 2)
     w_d = w_down.reshape(FFN_PARTS, hidden, width)
     grad_rows = 3 * local * width // LANES
+    summed = FFN_PIECES * 4 * HALF
     half = jax.ShapeDtypeStruct((rows // 2, width), jnp.float32)
     low = jnp.bfloat16
     blocks = rows // 2 // OUT_BLOCK
     return pl.pallas_call(
         functools.partial(ffn_kernel, lax.axis_size("seq") // 2),
-        out_shape=[jax.ShapeDtypeStruct((grad_rows, LANES), jnp.float32)] + [half] * 6,
+        out_shape=[
+            jax.ShapeDtypeStruct((summed, LANES), jnp.float32),
+            jax.ShapeDtypeStruct((grad_rows - summed, LANES), jnp.float32),
+        ]
+        + [half] * 5,
         in_specs=[pl.BlockSpec(memory_space=pl.ANY)] * 6,
         out_specs=[pl.BlockSpec(memory_space=pl.ANY)] * 7,
         scratch_shapes=[
@@ -518,7 +505,7 @@
             pltpu.VMEM((OUT_BLOCK, width), jnp.float32),
             pltpu.SemaphoreType.DMA((6,)),
             pltpu.SemaphoreType.DMA((2, 2, blocks)),
-            pltpu.SemaphoreType.DMA((2, 2, blocks)),
+            pltpu.SemaphoreType.DMA((2, blocks)),
             pltpu.SemaphoreType.DMA,
             pltpu.SemaphoreType.DMA,
         ]
@@ -731,9 +718,472 @@
     )(w_in.reshape(width, 3 * chans), w_out, jnp.pad(taps, ((0, 5), (0, 0))))
 
 
-def to_panels(matrix):
-    rows, cols = matrix.shape
-    return matrix.reshape(rows, cols // LANES, LANES).transpose(1, 0, 2).reshape(-1, LANES)
+SUB_ROWS = 64
+SUB_COLS = 256
+
+
+def norm_back(grad, gain, unit, scale):
+    scaled = gain * grad
+    return scale * (scaled - unit * jnp.mean(scaled * unit, axis=-1, keepdims=True))
+
+
+def mixer_kernel(places, *refs):
+    (rest_hbm, mid_chip, mid_far, ffn_chip, hidden_hbm, proj_hbm, gated_hbm) = refs[0:7]
+    (normed_t_hbm, mixed_t_hbm, w_in_hbm, w_out_hbm, cot_hbm, tokens_hbm) = refs[7:13]
+    (valid, taps, gain_mix, gain_ffn) = refs[13:17]
+    (sums, tokens_out, block_out, ffn_far, land_in, land_out, land_small) = refs[17:24]
+    (own, normed_t, mixed_t, w_in, w_out, cot, tokens, grad_mixer, grad_proj) = refs[24:33]
+    (chip, far, hidden, proj, gated, mixed_buf, conv_in, grad_hid, grad_tok) = refs[33:42]
+    (halo_out, halo_in, halo_keep, small, small_stage, small_fetch) = refs[42:48]
+    (stage_in, fetch_in, stage_out, fetch_out) = refs[48:52]
+    (load_sems, row_sems, halo_sems, near_sems, far_sems, out_sems) = refs[52:58]
+    summer = SeqSum(places, own, sums, refs[58:])
+    here = lax.axis_index("seq")
+    last = 2 * places - 1
+    tp_at = lax.axis_index("tp")
+    core = lax.rem(tp_at, 2)
+    sibling = tp_at + 1 - 2 * core
+    across = lax.rem(tp_at + 2, 4)
+    rows, width = tokens.shape
+    slots = halo_in.shape[0]
+    slot_len = rows // slots
+    per_slot = slot_len // OUT_BLOCK
+    blocks = rows // OUT_BLOCK
+    chans = w_out.shape[0] // 4
+    count = own.shape[0] // (4 * HALF)
+    early_rows = rest_hbm.shape[0]
+
+    loads = [
+        pltpu.make_async_copy(src, dst, load_sems.at[i])
+        for i, (src, dst) in enumerate(
+            (
+                (rest_hbm, own.at[pl.ds(0, early_rows)]),
+                (cot_hbm, cot),
+                (w_out_hbm, w_out),
+                (tokens_hbm, tokens),
+                (w_in_hbm, w_in),
+                (normed_t_hbm, normed_t),
+                (mixed_t_hbm, mixed_t),
+            )
+        )
+    ]
+    for load in loads:
+        load.start()
+
+    def place_of(n):
+        slot = n // per_slot
+        block = per_slot - 1 - lax.rem(n, per_slot)
+        return slot, block, pl.multiple_of(slot * slot_len + block * OUT_BLOCK, OUT_BLOCK)
+
+    def mid_loads(first):
+        at = pl.ds(first, OUT_BLOCK)
+        return [
+            pltpu.make_async_copy(src.at[at], dst, row_sems.at[i])
+            for i, (src, dst) in enumerate(((mid_chip, chip), (mid_far, far), (hidden_hbm, hidden)))
+        ]
+
+    def proj_loads(slot, block, first):
+        return [
+            pltpu.make_async_copy(proj_hbm.at[pl.ds(first, OUT_BLOCK)], proj, row_sems.at[3]),
+            pltpu.make_async_copy(
+                gated_hbm.at[slot, pl.ds(pl.multiple_of(block * OUT_BLOCK, 8), OUT_BLOCK + 8)],
+                gated,
+                row_sems.at[4],
+            ),
+        ]
+
+    def start(copies):
+        for copy in copies:
+            copy.start()
+
+    def wait(copies):
+        for copy in copies:
+            copy.wait()
+
+    def remote(src, dst, sems, i, device):
+        return pltpu.make_async_remote_copy(
+            src_ref=src,
+            dst_ref=dst,
+            send_sem=sems.at[0, i],
+            recv_sem=sems.at[1, i],
+            device_id=device,
+            device_id_type=pl.DeviceIdType.MESH,
+        )
+
+    barrier = pltpu.get_barrier_semaphore()
+
+    def signal(device):
+        pl.semaphore_signal(barrier, inc=1, device_id=device, device_id_type=pl.DeviceIdType.MESH)
+
+    pl.when(here > 0)(lambda: signal({"seq": here - 1}))
+    pl.when(here < last)(lambda: signal({"seq": here + 1}))
+    ends = jnp.where(here > 0, 1, 0) + jnp.where(here < last, 1, 0)
+    greet_seq(places, ({"tp": sibling}, {"tp": across}), ends)
+
+    def block_at(k):
+        return pl.ds(pl.multiple_of(k * OUT_BLOCK, OUT_BLOCK), OUT_BLOCK)
+
+    def ffn_across(k):
+        at = block_at(k)
+        return remote(ffn_chip.at[at], ffn_far.at[at], far_sems, k, {"tp": across})
+
+    @pl.loop(0, blocks)
+    def _(k):
+        ffn_across(k).start()
+
+    small[...] = jnp.zeros_like(small)
+    wait(loads[:3])
+
+    def hidden_grad(chip_rows, far_rows, hidden_rows, cot_rows):
+        grad_mid = chip_rows + far_rows
+        scale = rms_scale(hidden_rows)
+        unit = hidden_rows * scale
+        grad = cot_rows.astype(jnp.float32) + norm_back(grad_mid, gain_ffn[...], unit, scale)
+        return grad, grad_mid * unit
+
+    def halo_copy(slot, device):
+        return remote(halo_out.at[slot], halo_in.at[slot], halo_sems, slot, {"seq": device})
+
+    head = 16
+    for slot in range(slots):
+        at = pl.ds(slot * slot_len, head)
+        top = pl.ds(0, head)
+        copies = [
+            pltpu.make_async_copy(src.at[at], dst, row_sems.at[i])
+            for i, (src, dst) in enumerate(
+                (
+                    (mid_chip, chip.at[top]),
+                    (mid_far, far.at[top]),
+                    (hidden_hbm, hidden.at[top]),
+                    (proj_hbm, proj.at[top]),
+                )
+            )
+        ]
+        start(copies)
+        wait(copies)
+        grad, _ = hidden_grad(chip[top, :], far[top, :], hidden[top, :], cot[at, :])
+        grad_mixed = dot_cols(grad.astype(jnp.bfloat16), w_out[...])
+        halo_out[slot] = (grad_mixed * proj[top, width : 2 * width])[:8]
+        pl.when(here > 0)(lambda slot=slot: halo_copy(slot, here - 1).start())
+
+    slot, block, first = place_of(0)
+    start(mid_loads(first))
+    start(proj_loads(slot, block, first))
+
+    @pl.when(here == last)
+    def _():
+        halo_in[...] = jnp.zeros_like(halo_in)
+
+    @pl.when(here < last)
+    def _():
+        for slot in range(slots):
+            halo_copy(slot, here + 1).wait_recv()
+
+    wait(loads[3:])
+
+    def out_rows(first):
+        return pl.ds(pl.multiple_of(core * rows + first, OUT_BLOCK), OUT_BLOCK)
+
+    def hand_out(target, first, i):
+        at = out_rows(first)
+        return (
+            pltpu.make_async_copy(grad_tok, target.at[at], out_sems.at[0, 2 * blocks]),
+            remote(grad_tok, target.at[at], out_sems, i, {"tp": sibling}),
+        )
+
+    @pl.loop(0, blocks)
+    def _(n):
+        slot, block, first = place_of(n)
+        at = pl.ds(first, OUT_BLOCK)
+        wait(mid_loads(first))
+
+        @pl.loop(0, OUT_BLOCK // SUB_ROWS)
+        def _(r):
+            sub = pl.ds(pl.multiple_of(r * SUB_ROWS, SUB_ROWS), SUB_ROWS)
+            whole = pl.ds(pl.multiple_of(first + r * SUB_ROWS, SUB_ROWS), SUB_ROWS)
+            grad, for_gain = hidden_grad(chip[sub, :], far[sub, :], hidden[sub, :], cot[whole, :])
+            grad_hid[sub, :] = grad
+            grad_mixer[whole, :] = grad.astype(jnp.bfloat16)
+            small[1:2, :] += jnp.sum(for_gain, axis=0, keepdims=True)
+
+        @pl.when(n < blocks - 1)
+        def _():
+            start(mid_loads(place_of(n + 1)[2]))
+
+        mixed_buf[...] = dot_cols(grad_mixer[at, :], w_out[...])
+        wait(proj_loads(slot, block, first))
+
+        @pl.when(block == per_slot - 1)
+        def _():
+            conv_in[pl.ds(OUT_BLOCK, 8), :] = halo_in[slot]
+
+        @pl.when(block < per_slot - 1)
+        def _():
+            conv_in[pl.ds(OUT_BLOCK, 8), :] = halo_keep[...]
+
+        summer.tick(2 * n, count)
+        mask = valid[at, :]
+
+        @pl.loop(0, width // SUB_COLS)
+        def _(c):
+            def cols(gate):
+                return pl.ds(pl.multiple_of(gate * width + c * SUB_COLS, SUB_COLS), SUB_COLS)
+
+            here_cols = cols(0)
+            in_gate, out_gate, conv_value = (proj[:, cols(g)] for g in range(3))
+            grad_mixed = mixed_buf[:, here_cols]
+            now = grad_mixed * out_gate
+            conv_in[pl.ds(0, OUT_BLOCK), here_cols] = now
+            seen = [gated[pl.ds(6 + j, OUT_BLOCK), here_cols] for j in range(3)]
+            tap = [taps[j : j + 1, here_cols] for j in range(3)]
+            conv_sum = tap[0] * seen[0] + tap[1] * seen[1] + tap[2] * seen[2]
+            for j in range(3):
+                small[2 + j : 3 + j, here_cols] += jnp.sum(now * seen[j], axis=0, keepdims=True)
+            grad_proj[at, cols(1)] = (grad_mixed * conv_sum).astype(jnp.bfloat16)
+            grad_gated = mask * (
+                tap[2] * now
+                + tap[1] * conv_in[pl.ds(1, OUT_BLOCK), here_cols]
+                + tap[0] * conv_in[pl.ds(2, OUT_BLOCK), here_cols]
+            )
+            grad_proj[at, cols(0)] = (grad_gated * conv_value).astype(jnp.bfloat16)
+            grad_proj[at, cols(2)] = (grad_gated * in_gate).astype(jnp.bfloat16)
+
+        halo_keep[...] = conv_in[pl.ds(0, 8), :]
+
+        @pl.when(n < blocks - 1)
+        def _():
+            start(proj_loads(*place_of(n + 1)))
+
+        mixed_buf[...] = dot_cols(grad_proj[at, :], w_in[...])
+
+        @pl.when(n > 0)
+        def _():
+            local, there = hand_out(tokens_out, place_of(n - 1)[2], n - 1)
+            local.wait()
+            there.wait_send()
+
+        @pl.loop(0, OUT_BLOCK // SUB_ROWS)
+        def _(r):
+            sub = pl.ds(pl.multiple_of(r * SUB_ROWS, SUB_ROWS), SUB_ROWS)
+            whole = pl.ds(pl.multiple_of(first + r * SUB_ROWS, SUB_ROWS), SUB_ROWS)
+            inputs = tokens[whole, :].astype(jnp.float32)
+            scale = rms_scale(inputs)
+            unit = inputs * scale
+            grad_in = mixed_buf[sub, :]
+            grad_tok[sub, :] = grad_hid[sub, :] + norm_back(grad_in, gain_mix[...], unit, scale)
+            small[0:1, :] += jnp.sum(grad_in * unit, axis=0, keepdims=True)
+
+        start(hand_out(tokens_out, first, n))
+        summer.tick(2 * n + 1, count)
+
+    def near(src, dst, i):
+        return remote(src, dst, near_sems, i, {"tp": sibling})
+
+    in_blocks = width // OUT_BLOCK
+    panels_in = 3 * chans // LANES
+
+    def near_in(m):
+        return near(stage_in.at[lax.rem(m, 2)], land_in.at[m], m)
+
+    near_out = near(stage_out, land_out, in_blocks)
+    near_small = near(small_stage, land_small, in_blocks + 1)
+
+    def in_part(m, g, shard):
+        at = pl.ds(pl.multiple_of(m * OUT_BLOCK, OUT_BLOCK), OUT_BLOCK)
+        cols = pl.ds(pl.multiple_of(g * width + shard * chans, LANES), chans)
+        return jnp.dot(normed_t[at, :], grad_proj[:, cols], preferred_element_type=jnp.float32)
+
+    def out_part(shard):
+        at = pl.ds(pl.multiple_of(shard * chans, chans), chans)
+        return jnp.dot(mixed_t[at, :], grad_mixer[...], preferred_element_type=jnp.float32)
+
+    for p in range(width // LANES):
+        small_stage[8 * p : 8 * p + 8, :] = small[:, p * LANES : (p + 1) * LANES]
+    near_small.start()
+    halves = chans // LANES
+
+    @pl.loop(0, in_blocks)
+    def _(m):
+        @pl.when(m >= 2)
+        def _():
+            near_in(m - 2).wait_send()
+
+        for g in range(3):
+            part = in_part(m, g, sibling)
+            for h in range(halves):
+                stage_in[lax.rem(m, 2), g * halves + h] = part[:, h * LANES : (h + 1) * LANES]
+        near_in(m).start()
+        summer.tick(2 * blocks + m, count)
+
+    part = out_part(sibling)
+    for p in range(width // LANES):
+        stage_out[p] = part[:, p * LANES : (p + 1) * LANES]
+    near_out.start()
+
+    @pl.loop(0, in_blocks)
+    def _(m):
+        near_in(m).wait_recv()
+        fetch = pltpu.make_async_copy(land_in.at[m], fetch_in, row_sems.at[0])
+        fetch.start()
+        parts = [in_part(m, g, tp_at) for g in range(3)]
+        fetch.wait()
+        for g in range(3):
+            for h in range(halves):
+                i = g * halves + h
+                to = pl.multiple_of(early_rows + i * width + m * OUT_BLOCK, OUT_BLOCK)
+                own[pl.ds(to, OUT_BLOCK), :] = (
+                    parts[g][:, h * LANES : (h + 1) * LANES] + fetch_in[i]
+                )
+
+        summer.tick(2 * blocks + in_blocks + m, count)
+
+    near_out.wait_recv()
+    near_small.wait_recv()
+    fetches = [
+        pltpu.make_async_copy(land_out, fetch_out, row_sems.at[0]),
+        pltpu.make_async_copy(land_small, small_fetch, row_sems.at[1]),
+    ]
+    start(fetches)
+    part = out_part(tp_at)
+    wait(fetches)
+    out_first = early_rows + panels_in * width
+    for p in range(width // LANES):
+        own[pl.ds(out_first + p * chans, chans), :] = (
+            part[:, p * LANES : (p + 1) * LANES] + fetch_out[p]
+        )
+    small_first = out_first + width // LANES * chans
+    small_rows = small_stage.shape[0]
+    own[pl.ds(small_first, small_rows), :] = small_stage[...] + small_fetch[...]
+    unused = own.shape[0] - small_first - small_rows
+    own[pl.ds(small_first + small_rows, unused), :] = jnp.zeros((unused, LANES), jnp.float32)
+
+    local, there = hand_out(tokens_out, place_of(blocks - 1)[2], blocks - 1)
+    local.wait()
+    there.wait_send()
+    done = 2 * blocks + 2 * in_blocks
+    pause = min(done + 10, count)
+
+    @pl.loop(done, pause)
+    def _(t):
+        summer.tick(t, count)
+
+    @pl.loop(0, blocks)
+    def _(k):
+        ffn_across(k).wait_recv()
+        at = block_at(k)
+        copies = [
+            pltpu.make_async_copy(src.at[at], dst, row_sems.at[i])
+            for i, (src, dst) in enumerate(((ffn_chip, chip), (ffn_far, far), (hidden_hbm, hidden)))
+        ]
+        start(copies)
+
+        @pl.when(k > 0)
+        def _():
+            local, there = hand_out(block_out, (k - 1) * OUT_BLOCK, blocks + k - 1)
+            local.wait()
+            there.wait_send()
+
+        wait(copies)
+        grad_tok[...] = hidden[...] + (chip[...] + far[...])
+        start(hand_out(block_out, k * OUT_BLOCK, blocks + k))
+        summer.tick(pause + k, count)
+
+    @pl.loop(pause + blocks, count + summer.P_LAGS[-1][1])
+    def _(t):
+        summer.tick(t, count)
+
+    local, there = hand_out(block_out, (blocks - 1) * OUT_BLOCK, 2 * blocks - 1)
+    local.wait()
+    there.wait_send()
+
+    @pl.loop(0, blocks)
+    def _(k):
+        ffn_across(k).wait_send()
+        hand_out(tokens_out, place_of(k)[2], k)[1].wait_recv()
+        hand_out(block_out, k * OUT_BLOCK, blocks + k)[1].wait_recv()
+
+    for m in range(max(in_blocks - 2, 0), in_blocks):
+        near_in(m).wait_send()
+    near_out.wait_send()
+    near_small.wait_send()
+
+    @pl.when(here > 0)
+    def _():
+        for slot in range(slots):
+            halo_copy(slot, here - 1).wait_send()
+
+
+def mixer_back(hbm, vmem, slots, collective_id):
+    rest, _, _, _, hidden, _, gated, normed_t, mixed_t, w_in, w_out, _, tokens = hbm
+    rows, width = tokens.shape
+    chans = w_out.shape[0] // 4
+    blocks = rows // OUT_BLOCK
+    in_blocks = width // OUT_BLOCK
+    f32, low = jnp.float32, jnp.bfloat16
+    panels_in = 3 * chans // LANES
+    grad_rows = rest.shape[0] + panels_in * width + width // LANES * chans + 4 * HALF
+    small_rows = 8 * width // LANES
+    block = pltpu.VMEM((OUT_BLOCK, width), f32)
+    full = jax.ShapeDtypeStruct((2 * rows, width), f32)
+    anywhere = pl.BlockSpec(memory_space=pl.ANY)
+    return pl.pallas_call(
+        functools.partial(mixer_kernel, lax.axis_size("seq") // 2),
+        out_shape=[
+            jax.ShapeDtypeStruct((grad_rows, LANES), f32),
+            full,
+            full,
+            jax.ShapeDtypeStruct((rows, width), f32),
+            jax.ShapeDtypeStruct((in_blocks, panels_in, OUT_BLOCK, LANES), f32),
+            jax.ShapeDtypeStruct((width // LANES, chans, LANES), f32),
+            jax.ShapeDtypeStruct((small_rows, LANES), f32),
+        ],
+        in_specs=[anywhere] * len(hbm) + [pl.BlockSpec(memory_space=pltpu.VMEM)] * len(vmem),
+        out_specs=[anywhere] * 7,
+        scratch_shapes=[
+            pltpu.VMEM((grad_rows, LANES), f32),
+            pltpu.VMEM(normed_t.shape, low),
+            pltpu.VMEM(mixed_t.shape, low),
+            pltpu.VMEM(w_in.shape, low),
+            pltpu.VMEM(w_out.shape, low),
+            pltpu.VMEM((rows, width), low),
+            pltpu.VMEM((rows, width), low),
+            pltpu.VMEM((rows, width), low),
+            pltpu.VMEM((rows, 3 * width), low),
+            block,
+            block,
+            block,
+            pltpu.VMEM((OUT_BLOCK, 3 * width), f32),
+            pltpu.VMEM((OUT_BLOCK + 8, width), f32),
+            block,
+            pltpu.VMEM((OUT_BLOCK + 8, width), f32),
+            block,
+            block,
+            pltpu.VMEM((slots, 8, width), f32),
+            pltpu.VMEM((slots, 8, width), f32),
+            pltpu.VMEM((8, width), f32),
+            pltpu.VMEM((8, width), f32),
+            pltpu.VMEM((small_rows, LANES), f32),
+            pltpu.VMEM((small_rows, LANES), f32),
+            pltpu.VMEM((2, panels_in, OUT_BLOCK, LANES), f32),
+            pltpu.VMEM((panels_in, OUT_BLOCK, LANES), f32),
+            pltpu.VMEM((width // LANES, chans, LANES), f32),
+            pltpu.VMEM((width // LANES, chans, LANES), f32),
+            pltpu.SemaphoreType.DMA((7,)),
+            pltpu.SemaphoreType.DMA((5,)),
+            pltpu.SemaphoreType.DMA((2, slots)),
+            pltpu.SemaphoreType.DMA((2, in_blocks + 2)),
+            pltpu.SemaphoreType.DMA((2, blocks)),
+            pltpu.SemaphoreType.DMA((2, 2 * blocks + 1)),
+        ]
+        + seq_sum_scratch(),
+        compiler_params=pltpu.CompilerParams(
+            collective_id=collective_id, has_side_effects=True, vmem_limit_bytes=VMEM_LIMIT
+        ),
+        cost_estimate=pl.CostEstimate(
+            flops=26 * rows * width * width, bytes_accessed=400 << 20, transcendentals=0
+        ),
+        name="mixer_back",
+    )(*hbm, *vmem)
 
 
 def from_panels(panels, rows, cols):
@@ -799,75 +1249,39 @@
 
     grad_out = valid_all * cotangent.astype(jnp.float32).reshape(row_count, width)
     grad_ffn = grad_out.astype(jnp.bfloat16)
-    ffn_sums, mid_chip, mid_far, ffn_chip, ffn_far = ffn_both_ways(
+    ffn_sums, rest, mid_chip, mid_far, ffn_chip = ffn_both_ways(
         normed_mid, grad_ffn, w_gate, w_up, w_down, 1
     )[:5]
-    grad_mid = mid_chip + mid_far
-    ffn_out = ffn_chip + ffn_far
-
-    def own_rows(block):
-        return lax.dynamic_slice(block, (core * half_rows, 0), (half_rows, width))
-
-    block_own = hidden_res + ffn_out
-    block_out = both_cores(block_own, swap_tp(block_own, 1))
-    block_out = (valid_all * block_out).astype(jnp.bfloat16).reshape(slot_count, local_len, width)
-
-    grad_gain_ffn = jnp.sum(grad_mid * unit_ffn, axis=0)
-    scaled_mid = gain_ffn * grad_mid
-    grad_hidden = own_rows(grad_out) + scale_ffn * (
-        scaled_mid - unit_ffn * jnp.mean(scaled_mid * unit_ffn, axis=-1, keepdims=True)
-    )
-
-    grad_mixer = grad_hidden.astype(jnp.bfloat16)
-    grad_mixed = dot_cols(grad_mixer, w_out_all)
-    grad_out_gate = grad_mixed * conv_sum
-    grad_conv_in = (grad_mixed * out_gate).reshape(seq_shape)
-    next_grad = shift_seq(grad_conv_in[:, :2], -1)
-    extended = jnp.concatenate([grad_conv_in, next_grad], axis=1)
-    grad_gated = (
-        taps[2] * extended[:, 0:local_len]
-        + taps[1] * extended[:, 1 : local_len + 1]
-        + taps[0] * extended[:, 2 : local_len + 2]
-    ).reshape(half_rows, width)
-    grad_conv = jnp.stack(
-        [jnp.sum(grad_conv_in * padded_seq[:, j : j + local_len], axis=(0, 1)) for j in range(3)]
-    )
-    grad_in_gate = grad_gated * valid_rows * conv_value
-    grad_value = grad_gated * valid_rows * in_gate
-    grad_proj = jnp.concatenate([grad_in_gate, grad_out_gate, grad_value], axis=1).astype(
-        jnp.bfloat16
-    )
-    grad_in = dot_cols(grad_proj, w_in_all)
-    grad_gain_mix = jnp.sum(grad_in * unit_mix, axis=0)
-    scaled_in = gain_mix * grad_in
-    tokens_grad = grad_hidden + scale_mix * (
-        scaled_in - unit_mix * jnp.mean(scaled_in * unit_mix, axis=-1, keepdims=True)
-    )
-    grad_tokens = both_cores(tokens_grad, swap_tp(tokens_grad, 1))
+    cot_own = lax.dynamic_slice(grad_ffn, (core * half_rows, 0), (half_rows, width))
+    lead = jnp.zeros((half_slots, 6, width), jnp.float32)
+    gated_rows = jnp.concatenate([lead, padded_seq], axis=1)
+    mixer_sums, grad_tokens, block_sum = mixer_back(
+        (
+            rest,
+            mid_chip,
+            mid_far,
+            ffn_chip,
+            hidden_res,
+            projected,
+            gated_rows,
+            normed_in.T,
+            mixed_seq.T,
+            w_in_all,
+            w_out_all,
+            cot_own,
+            tokens_own.reshape(half_rows, width),
+        ),
+        (valid_rows, taps, gain_mix.reshape(1, width), gain_ffn.reshape(1, width)),
+        half_slots,
+        2,
+    )[:3]
     grad_tokens = grad_tokens.reshape(slot_count, local_len, width)
-
-    def chans_of(block, which):
-        first = (chip * 2 + which) * chans
-        return lax.dynamic_slice(block, (0, first), (block.shape[0], chans))
-
-    def mixer_panels(which):
-        proj = jnp.concatenate(
-            [chans_of(grad_proj[:, g * width : (g + 1) * width], which) for g in range(3)], axis=1
-        )
-        in_part = dot_rows(normed_in, proj)
-        out_part = dot_rows(chans_of(mixed_seq, which), grad_mixer)
-        small = jnp.concatenate(
-            [grad_gain_mix, grad_gain_ffn, chans_of(grad_conv, which).reshape(-1)]
-        ).reshape(-1, LANES)
-        pad = -small.shape[0] % (4 * HALF)
-        return jnp.concatenate(
-            [to_panels(in_part), to_panels(out_part), jnp.pad(small, ((0, pad), (0, 0)))], axis=0
-        )
-
-    mixer_chip = mixer_panels(core) + swap_tp(mixer_panels(1 - core), 1)
-    mixer_sums = seq_sum(mixer_chip, 2, "sum_mixer_grads")
+    block_out = (valid_all * block_sum).astype(jnp.bfloat16)
+    block_out = block_out.reshape(slot_count, local_len, width)
 
     hidden = w_gate.shape[1]
+    ffn_sums = jnp.concatenate([ffn_sums, mixer_sums[: rest.shape[0]]], axis=0)
+    mixer_sums = mixer_sums[rest.shape[0] :]
     by_part = ffn_sums.reshape(FFN_PARTS, 3, hidden // FFN_PARTS // LANES, width, LANES)
     total_w_gate = by_part[:, 0].transpose(2, 0, 1, 3).reshape(width, hidden)
     total_w_up = by_part[:, 1].transpose(2, 0, 1, 3).reshape(width, hidden)
@@ -876,10 +1290,10 @@
     out_rows = width * chans // LANES
     total_w_in = from_panels(mixer_sums[:in_rows], width, 3 * chans).reshape(width, 3, chans)
     total_w_out = from_panels(mixer_sums[in_rows : in_rows + out_rows], chans, width)
-    small = mixer_sums[in_rows + out_rows :].reshape(-1)
-    total_gain_mix = small[:width]
-    total_gain_ffn = small[width : 2 * width]
-    total_conv = small[2 * width : 2 * width + 3 * chans].reshape(3, chans)
+    small = mixer_sums[in_rows + out_rows :][: 8 * width // LANES]
+    small = small.reshape(width // LANES, 8, LANES).transpose(1, 0, 2).reshape(8, width)
+    total_gain_mix, total_gain_ffn = small[0], small[1]
+    total_conv = lax.dynamic_slice(small, (2, tp_at * chans), (3, chans))
     return (
         block_out,
         grad_tokens,

time: 807 us -> 699 us (0.87)
  other arithmetic: 120 us -> 61.6 us
  matrix products: 47.2 us -> 16.4 us
  local copies, waits for them, and re-layouts: 145 us -> 119 us
  Pallas kernels: 479 us -> 490 us
    pallas_call x1, Pallas kernels: 99.9 us -> 190 us  [mixer_back(): pl.pallas_call(functools.partial(mixer_kernel, lax.axis_size('seq') // 2)...]
    pallas_call x1, Pallas kernels: 300 us -> 222 us  [ffn_both_ways(): pl.pallas_call(functools.partial(ffn_kernel, lax.axis_size('seq') // 2),...]
    add x5 -> x0, other arithmetic: 34.1 us -> none  [the longest x1 8.63 us: per_device(): block_own = hidden_res + ffn_out]
    dot_general x6 -> x0, matrix products: 30.2 us -> none  [the longest x2 18.1 us: dot_cols(): lax.dot_general(left, right, (((1,), (1,)), ((), ())), preferred_element_...]
    pallas_call x4 -> x0, local copies, waits for them, and re-layouts: 21.4 us -> none  [ffn_both_ways(): pl.pallas_call(functools.partial(ffn_kernel, lax.axis_size('seq') // 2),...]
    slice x2 -> x0, other arithmetic: 10.2 us -> none  [mixer_panels(): grad_proj[:, g * width:(g + 1) * width]]
    convert_element_type x3 -> x1, other arithmetic: 12 us -> 2.53 us  [per_device(): block_out = (valid_all * block_sum).astype(jnp.bfloat16)]
    concatenate x1, local copies, waits for them, and re-layouts: 9.33 us -> 0.01 us  [per_device(): gated_rows = jnp.concatenate([lead, padded_seq], axis=1)]
  transfers between devices with their start and end apart: 6 -> 2, of which waited for: 1 -> 0; matrix products, arithmetic and copies ran while one was open for 26% -> 7% of each run, Pallas kernels for 0% -> 0%
where the time goes in v4:
time: 699 us; the launch traced here: 692 us
  Pallas kernels  490 us (70%)
  local copies, waits for them, and re-layouts  119 us (17%)
  other arithmetic  61.6 us (9%)
  matrix products  16.4 us (2%)
    pallas_call x1, Pallas kernels, ffn_both_ways(): pl.pallas_call(functools.partial(ffn_kernel, lax.axis_size('seq') // 2),...  222 us
    pallas_call x1, Pallas kernels, mixer_back(): pl.pallas_call(functools.partial(mixer_kernel, lax.axis_size('seq') // 2)...  190 us
    pallas_call x1, Pallas kernels, gather_mixer(): pl.pallas_call(functools.partial(gather_kernel, count // 2), out_shape=[j...  78.2 us
    unnamed x52, local copies, waits for them, and re-layouts  52.7 us
    transpose x2, local copies, waits for them, and re-layouts, per_device(): total_w_down = by_part[:, 2].transpose(0, 1, 3, 2).reshape(hidden, width)  16.6 us
  transfers between devices with their start and end apart: 2, of which 0 were waited for; matrix products, arithmetic and copies ran while one was open for 7% of the time, Pallas kernels for 0%

profile of v4, /device:TPU:0, one launch (start us, length us, event | category | flops | bytes accessed | tf_op | source)
XLA Modules:
  0.0 691.8 jit_solution(12316261330654509809)
XLA Ops:
  11.4 78.2 %gather_mixer.1 = (bf16[1024,3072]{1,0:T(8,128)(2,1)}, bf16[1024,1024]{1,0:T(8,128)(2,1)S(1)}, f32[8,1024]{1,0:T(8,128)S(1)}) custom-call(bf16[1024,768]{1,0:T(8,128)(2,1)S(1)} %copy.35.w_in, bf16[256,1024]{1,0:T(8,128)(2,1)S(1)} %copy-done, f32[8,256]{1,0:T(8,128)S(1)} %pad.4.taps), custom_call_target="tpu_custom_call" | custom-call | tf_op jit(solution)/shard_map/gather_mixer/pallas_call | solution.py:694
  89.6 13.7 %fusion.9.refs_5_ = f32[1024,3072]{1,0:T(8,128)} fusion(bf16[1024,3072]{1,0:T(8,128)(2,1)} %get-tuple-element.21.refs_9_, f32[1024,1024]{0,1:T(8,128)} %copy.56, f32[1024]{0:T(1024)S(1)} %bitcast.106, f32[1024]{0:T(1024)S(1)} %copy-done.13), kind=kOutput, calls=%fused_computation.41 | convolution fusion | flops 6445596672 | bytes 23076864 | tf_op jit(solution)/shard_map/dot_general | solution.py:1229
  103.4 7.7 %slice_multiply_fusion = (f32[1024,1024]{1,0:T(8,128)S(1)}, f32[1024,1024]{1,0:T(8,128)}) fusion(f32[1024,3072]{1,0:T(8,128)} %fusion.9.refs_5_, f32[1024]{0:T(1024)S(1)} %bitcast.112), kind=kLoop, calls=%fused_computation.17 | loop fusion | flops 2097152 | bytes 20975616 | tf_op jit(solution)/shard_map/mul | solution.py:1234
  114.3 5.3 copy.58
  119.6 7.0 %fusion.5 = f32[2,512,1024]{2,1,0:T(8,128)} fusion(f32[2,2,1024]{2,1,0:T(2,128)S(1)} %collective-permute-done, f32[2,512,1024]{2,1,0:T(8,128)} %bitcast.81, f32[1024]{0:T(1024)S(1)} %bitcast.110, f32[1024]{0:T(1024)S(1)} %bitcast.111, f32[1024]{0:T(1024)S(1)} %bitcast.109), kind=kLoop, calls=%fused_computation.14 | loop fusion | flops 7340032 | bytes 8417280 | tf_op jit(solution)/shard_map/add | solution.py:1238
  126.6 5.3 copy.57
  132.0 4.3 multiply_convert_fusion.1
  155.2 4.9 fusion.1.refs_2_
  160.1 6.5 copy.44.refs_3_
  169.9 4.4 maximum_bitcast_fusion.refs_4_
  176.0 5.4 copy.45.refs_4_
  181.3 4.7 pad_maximum_fusion.1.refs_6_
  192.3 6.4 copy.43.refs_0_
  198.7 221.8 %ffn_both_ways.1 = (f32[18432,128]{1,0:T(8,128)}, f32[9216,128]{1,0:T(8,128)}, f32[1024,1024]{1,0:T(8,128)}, f32[1024,1024]{1,0:T(8,128)}, f32[1024,1024]{1,0:T(...) custom-call(bf16[2048,1024]{1,0:T(8,128)(2,1)} %copy.43.refs_0_, bf16[1024,2048]{1,0:T(8,128)(2,1)} %bitcast.86, ...), custom_call_target="tpu_custom_call" | custom-call | flops 43486543872 | bytes 838860800 | tf_op jit(solution)/shard_map/ffn_both_ways/pallas_call | solution.py:485
  420.6 189.5 %mixer_back.1 = (f32[17920,128]{1,0:T(8,128)}, f32[2048,1024]{1,0:T(8,128)}, f32[2048,1024]{1,0:T(8,128)}, f32[1024,1024]{1,0:T(8,128)}, f32[4,6,256,128]{3,2,1,...) custom-call(f32[9216,128]{1,0:T(8,128)} %get-tuple-element.24.refs_0_, f32[1024,1024]{1,0:T(8,128)} %get-tuple-element.25.refs_1_, ...), custom_call_target="tpu_custom_call" | custom-call | flops 27917287424 | bytes 419430400 | tf_op jit(solution)/shard_map/mixer_back/pallas_call | solution.py:1129
  614.5 4.3 slice.76
  629.9 11.2 %pad_maximum_fusion = f32[27648,128]{1,0:T(8,128)} fusion(f32[9216,128]{1,0:T(8,128)} %slice.76, f32[18432,128]{1,0:T(8,128)} %get-tuple-element.31), kind=kLoop, calls=%fused_computation | loop fusion | flops 3538944 | bytes 28311552 | tf_op jit(solution)/shard_map/concatenate | solution.py:1283
  641.1 10.6 %slice_bitcast_fusion = (f32[3,3,128,1024]{2,3,1,0:T(8,128)}, f32[3,1,3,1024,128]{4,3,2,1,0:T(8,128)}, f32[3,1,3,1024,128]{4,3,2,1,0:T(8,128)}) fusion(f32[3,3,3,1024,128]{4,3,2,1,0:T(8,128)} %bitcast.79), kind=kLoop, calls=%fused_computation.6 | loop fusion | bytes 28311552 | tf_op jit(solution)/shard_map/transpose | solution.py:1288
  651.7 6.0 copy.51
  657.7 6.3 copy.59
  664.0 6.0 copy.53
  670.1 6.1 copy.60
  676.1 6.0 copy.54
  682.9 8.4 %copy.70 = f32[4,512,1024]{2,1,0:T(8,128)} copy(f32[4,512,1024]{2,1,0:T(8,128)} %bitcast.94) | data formatting | bytes 16777216
  (79 shorter events, 60.0 us)
Async XLA Ops:
  7.2 4.2 copy-start.15
  7.2 4.2 copy-start
  7.2 82.4 %copy-start.13 = (f32[1024]{0:T(1024)S(1)}, f32[1024]{0:T(1024)}, u32[]{:S(2)}) copy-start(f32[1024]{0:T(1024)} %param.13) | copy-start | bytes 12292
  89.6 13.8 %copy-start.2 = (bf16[1024,1024]{1,0:T(8,128)(2,1)}, bf16[1024,1024]{1,0:T(8,128)(2,1)S(1)}, u32[]{:S(2)}) copy-start(bf16[1024,1024]{1,0:T(8,128)(2,1)S(1)} %get-tuple-element.23.refs_10_) | copy-start | bytes 6291460
  89.6 24.6 %copy-start.1 = (f32[8,1024]{1,0:T(8,128)}, f32[8,1024]{1,0:T(8,128)S(1)}, u32[]{:S(2)}) copy-start(f32[8,1024]{1,0:T(8,128)S(1)} %get-tuple-element.22.refs_14_) | copy-start | bytes 98308
  111.1 3.1 copy-start.4
  111.1 8.5 %collective-permute-start = (f32[2,2,1024]{2,1,0:T(2,128)S(1)}, f32[2,2,1024]{2,1,0:T(2,128)S(1)}, u32[]{:S(2)}, u32[]{:S(2)}) collective-permute-start(f32[2,2,1024]{2,1,0:T(2,128)S(1)} %slice.83), channel_id=1, source_target_pairs={{0,4},{4,8},{8,12},{12,16},{16,20},{20,24},{24,28},{1,5},{5,9},{9,... | collective-permute-start | bytes 49160 | tf_op jit(solution)/shard_map/ppermute | solution.py:36
  132.0 4.4 copy-start.3
  132.0 5.3 copy-start.7
  136.3 3.6 copy-start.10
  139.9 3.2 copy-start.5
  143.2 42.9 %collective-permute-start.1 = (f32[1024,1024]{0,1:T(8,128)}, f32[1024,1024]{0,1:T(8,128)}, u32[]{:S(2)}, u32[]{:S(2)}) collective-permute-start(f32[1024,1024]{0,1:T(8,128)} %broadcast_multiply_fusion), channel_id=1, source_target_pairs={{0,1},{1,0},{2,3},{3,2},{4,5},{5,4},{6,7},{7,6},{8,9},{9,8},{10,11... | collective-permute-start | bytes 12582920 | tf_op jit(solution)/shard_map/ppermute | solution.py:40
  143.7 11.6 %copy-start.11 = (f32[1,4,4,128]{3,1,2,0:T(4,128)}, f32[1,4,4,128]{3,1,2,0:T(4,128)S(1)}, u32[]{:S(2)}) copy-start(f32[1,4,4,128]{3,1,2,0:T(4,128)S(1)} %copy.62) | copy-start | bytes 24580
  166.6 3.2 copy-start.9
  169.8 4.4 copy-start.8
  181.3 4.7 copy-start.6
  186.0 3.8 copy-start.14
  612.2 6.6 slice-start
  614.4 5.3 slice-start.1
  614.4 5.3 copy-start.12

commit v5 on v4

--- a/solution.py
+++ b/solution.py
@@ -60,8 +60,8 @@
 
 
 class SeqSum:
-    def __init__(self, places, own, out, scratch):
-        self.places, self.own, self.out = places, own, out
+    def __init__(self, places, own, out, panel_of, scratch):
+        self.places, self.own, self.out, self.panel_of = places, own, out, panel_of
         self.y_in, self.p_left, self.p_right, self.p_acc = scratch[0:4]
         self.q_left, self.q_right, self.q_acc, self.q_in = scratch[4:8]
         self.sems = scratch[8]
@@ -86,13 +86,22 @@
         from_right = (self.place >= root) & (self.place < last)
         return left, right, from_left, from_right
 
+    def out_at(self, k, first, size):
+        per_panel = self.out.shape[0] // (4 * HALF)
+        panel = self.panel_of(k // per_panel)
+        row = lax.rem(k, per_panel) * 4 * HALF + first
+        return self.out.at[
+            pl.ds(pl.multiple_of(row, size), size), pl.ds(pl.multiple_of(panel * LANES, LANES), LANES)
+        ]
+
     def p_stage(self, which, k):
         place, side = self.place, self.side
-        own, out = self.own, self.out
+        own = self.own
         slot = lax.rem(k, SLOTS_IN_FLIGHT)
         base = pl.multiple_of(k * 4 * HALF, 4 * HALF)
         mine = pl.ds(pl.multiple_of(base + side * HALF, HALF), HALF)
         theirs = pl.ds(pl.multiple_of(base + (1 - side) * HALF, HALF), HALF)
+        out_mine = self.out_at(k, side * HALF, HALF)
         root = self.places // 2 - 1 + lax.rem(k, 2)
         left, right, from_left, from_right = self.chain(root)
         acc, y_in = self.p_acc.at[slot], self.y_in.at[slot]
@@ -105,13 +114,13 @@
 
         def down(src):
             return (
-                remote(src, out.at[mine], slot, 5, 7, left, side),
-                remote(src, out.at[mine], slot, 6, 7, right, side),
-                remote(src, out.at[mine], slot, 8, 9, place, 1 - side),
+                remote(src, out_mine, slot, 5, 7, left, side),
+                remote(src, out_mine, slot, 6, 7, right, side),
+                remote(src, out_mine, slot, 8, 9, place, 1 - side),
             )
 
         def keep():
-            return pltpu.make_async_copy(acc, out.at[mine], self.sems.at[10, slot])
+            return pltpu.make_async_copy(acc, out_mine, self.sems.at[10, slot])
 
         def hand_down(src):
             down_left, down_right, down_side = down(src)
@@ -166,7 +175,7 @@
             @pl.when(place != root)
             def _():
                 down(acc)[0]().wait_recv()
-                hand_down(out.at[mine])
+                hand_down(out_mine)
 
         if which == "end":
             down_left, down_right, down_side = down(acc)
@@ -179,10 +188,11 @@
 
     def q_stage(self, which, k):
         place, side = self.place, self.side
-        own, out = self.own, self.out
+        own = self.own
         slot = lax.rem(k, SLOTS_IN_FLIGHT)
         base = pl.multiple_of(k * 4 * HALF, 4 * HALF)
         wide = pl.ds(pl.multiple_of(base + 2 * HALF, 2 * HALF), 2 * HALF)
+        out_wide = self.out_at(k, 2 * HALF, 2 * HALF)
         root = self.places // 2 - lax.rem(k, 2)
         left, right, from_left, from_right = self.chain(root)
         acc, side_in = self.q_acc.at[slot], self.q_in.at[slot]
@@ -195,12 +205,12 @@
 
         def down(src):
             return (
-                remote(src, out.at[wide], slot, 16, 18, left, side),
-                remote(src, out.at[wide], slot, 17, 18, right, side),
+                remote(src, out_wide, slot, 16, 18, left, side),
+                remote(src, out_wide, slot, 17, 18, right, side),
             )
 
         def keep():
-            return pltpu.make_async_copy(side_in, out.at[wide], self.sems.at[19, slot])
+            return pltpu.make_async_copy(side_in, out_wide, self.sems.at[19, slot])
 
         def hand_down(src):
             down_left, down_right = down(src)
@@ -258,7 +268,7 @@
             @pl.when(place != root)
             def _():
                 down(acc)[0]().wait_recv()
-                hand_down(out.at[wide])
+                hand_down(out_wide)
 
         if which == "end":
             down_left, down_right = down(acc)
@@ -298,9 +308,18 @@
 
 
 FFN_PIECES = 36
+FFN_PANELS = 27
 FFN_PARTS = 3
 ROW_BLOCK = 512
 OUT_BLOCK = 256
+
+
+def panel_in_sums(panel):
+    per_part = FFN_PANELS // FFN_PARTS
+    third = per_part // 3
+    inside = lax.rem(panel, per_part)
+    kind = inside // third
+    return kind * (FFN_PANELS // 3) + panel // per_part * third + lax.rem(inside, third)
 
 
 def ffn_kernel(places, *refs):
@@ -308,7 +327,7 @@
     (sums, rest, mid_chip, mid_far, ffn_chip, mid_land, ffn_land) = refs[6:13]
     (mid, mid_t, cot, cot_t, w_gu, w_d, act, ggu, own, staged, fetched) = refs[13:24]
     load_sems, near_sems, far_sems, keep_sem, fetch_sem = refs[24:29]
-    summer = SeqSum(places, own, sums, refs[29:])
+    summer = SeqSum(places, own, sums, panel_in_sums, refs[29:])
     tp_at = lax.axis_index("tp")
     core = lax.rem(tp_at, 2)
     sibling = tp_at + 1 - 2 * core
@@ -467,7 +486,7 @@
         far(k).wait()
 
 
-def ffn_both_ways(normed_mid, grad_ffn, w_gate, w_up, w_down, collective_id):
+def ffn_both_ways(normed_mid, grad_ffn, w_gate, w_up, w_down, sum_cols, collective_id):
     rows, width = normed_mid.shape
     local = w_gate.shape[1]
     hidden = local // FFN_PARTS
@@ -485,7 +504,7 @@
     return pl.pallas_call(
         functools.partial(ffn_kernel, lax.axis_size("seq") // 2),
         out_shape=[
-            jax.ShapeDtypeStruct((summed, LANES), jnp.float32),
+            jax.ShapeDtypeStruct((width, sum_cols), jnp.float32),
             jax.ShapeDtypeStruct((grad_rows - summed, LANES), jnp.float32),
         ]
         + [half] * 5,
@@ -731,13 +750,19 @@
     (rest_hbm, mid_chip, mid_far, ffn_chip, hidden_hbm, proj_hbm, gated_hbm) = refs[0:7]
     (normed_t_hbm, mixed_t_hbm, w_in_hbm, w_out_hbm, cot_hbm, tokens_hbm) = refs[7:13]
     (valid, taps, gain_mix, gain_ffn) = refs[13:17]
-    (sums, tokens_out, block_out, ffn_far, land_in, land_out, land_small) = refs[17:24]
-    (own, normed_t, mixed_t, w_in, w_out, cot, tokens, grad_mixer, grad_proj) = refs[24:33]
-    (chip, far, hidden, proj, gated, mixed_buf, conv_in, grad_hid, grad_tok) = refs[33:42]
-    (halo_out, halo_in, halo_keep, small, small_stage, small_fetch) = refs[42:48]
-    (stage_in, fetch_in, stage_out, fetch_out) = refs[48:52]
-    (load_sems, row_sems, halo_sems, near_sems, far_sems, out_sems) = refs[52:58]
-    summer = SeqSum(places, own, sums, refs[58:])
+    (sums, tokens_out, block_out, ffn_far, land_in, land_out, land_small) = refs[18:25]
+    (own, normed_t, mixed_t, w_in, w_out, cot, tokens, grad_mixer, grad_proj) = refs[25:34]
+    (chip, far, hidden, proj, gated, mixed_buf, conv_in, grad_hid, grad_tok) = refs[34:43]
+    (halo_out, halo_in, halo_keep, small, small_stage, small_fetch) = refs[43:49]
+    (stage_in, fetch_in, stage_out, fetch_out) = refs[49:53]
+    (load_sems, row_sems, halo_sems, near_sems, far_sems, out_sems) = refs[53:59]
+    first_panel = FFN_PIECES * 4 * HALF // LANES // 8
+
+    def panel_of(panel):
+        panel = first_panel + panel
+        return jnp.where(panel < FFN_PANELS, panel_in_sums(panel), panel)
+
+    summer = SeqSum(places, own, sums, panel_of, refs[59:])
     here = lax.axis_index("seq")
     last = 2 * places - 1
     tp_at = lax.axis_index("tp")
@@ -1113,7 +1138,7 @@
             halo_copy(slot, here - 1).wait_send()
 
 
-def mixer_back(hbm, vmem, slots, collective_id):
+def mixer_back(hbm, vmem, sums, slots, collective_id):
     rest, _, _, _, hidden, _, gated, normed_t, mixed_t, w_in, w_out, _, tokens = hbm
     rows, width = tokens.shape
     chans = w_out.shape[0] // 4
@@ -1129,7 +1154,7 @@
     return pl.pallas_call(
         functools.partial(mixer_kernel, lax.axis_size("seq") // 2),
         out_shape=[
-            jax.ShapeDtypeStruct((grad_rows, LANES), f32),
+            jax.ShapeDtypeStruct(sums.shape, f32),
             full,
             full,
             jax.ShapeDtypeStruct((rows, width), f32),
@@ -1137,7 +1162,10 @@
             jax.ShapeDtypeStruct((width // LANES, chans, LANES), f32),
             jax.ShapeDtypeStruct((small_rows, LANES), f32),
         ],
-        in_specs=[anywhere] * len(hbm) + [pl.BlockSpec(memory_space=pltpu.VMEM)] * len(vmem),
+        in_specs=[anywhere] * len(hbm)
+        + [pl.BlockSpec(memory_space=pltpu.VMEM)] * len(vmem)
+        + [anywhere],
+        input_output_aliases={len(hbm) + len(vmem): 0},
         out_specs=[anywhere] * 7,
         scratch_shapes=[
             pltpu.VMEM((grad_rows, LANES), f32),
@@ -1183,11 +1211,7 @@
             flops=26 * rows * width * width, bytes_accessed=400 << 20, transcendentals=0
         ),
         name="mixer_back",
-    )(*hbm, *vmem)
-
-
-def from_panels(panels, rows, cols):
-    return panels.reshape(cols // LANES, rows, LANES).transpose(1, 0, 2).reshape(rows, cols)
+    )(*hbm, *vmem, sums)
 
 
 def per_device(
@@ -1249,13 +1273,15 @@
 
     grad_out = valid_all * cotangent.astype(jnp.float32).reshape(row_count, width)
     grad_ffn = grad_out.astype(jnp.bfloat16)
+    mixer_cols = 4 * chans
+    sum_cols = FFN_PANELS * LANES + mixer_cols + LANES
     ffn_sums, rest, mid_chip, mid_far, ffn_chip = ffn_both_ways(
-        normed_mid, grad_ffn, w_gate, w_up, w_down, 1
+        normed_mid, grad_ffn, w_gate, w_up, w_down, sum_cols, 1
     )[:5]
     cot_own = lax.dynamic_slice(grad_ffn, (core * half_rows, 0), (half_rows, width))
     lead = jnp.zeros((half_slots, 6, width), jnp.float32)
     gated_rows = jnp.concatenate([lead, padded_seq], axis=1)
-    mixer_sums, grad_tokens, block_sum = mixer_back(
+    sums, grad_tokens, block_sum = mixer_back(
         (
             rest,
             mid_chip,
@@ -1272,6 +1298,7 @@
             tokens_own.reshape(half_rows, width),
         ),
         (valid_rows, taps, gain_mix.reshape(1, width), gain_ffn.reshape(1, width)),
+        ffn_sums,
         half_slots,
         2,
     )[:3]
@@ -1280,17 +1307,15 @@
     block_out = block_out.reshape(slot_count, local_len, width)
 
     hidden = w_gate.shape[1]
-    ffn_sums = jnp.concatenate([ffn_sums, mixer_sums[: rest.shape[0]]], axis=0)
-    mixer_sums = mixer_sums[rest.shape[0] :]
-    by_part = ffn_sums.reshape(FFN_PARTS, 3, hidden // FFN_PARTS // LANES, width, LANES)
-    total_w_gate = by_part[:, 0].transpose(2, 0, 1, 3).reshape(width, hidden)
-    total_w_up = by_part[:, 1].transpose(2, 0, 1, 3).reshape(width, hidden)
-    total_w_down = by_part[:, 2].transpose(0, 1, 3, 2).reshape(hidden, width)
-    in_rows = width * 3 * chans // LANES
-    out_rows = width * chans // LANES
-    total_w_in = from_panels(mixer_sums[:in_rows], width, 3 * chans).reshape(width, 3, chans)
-    total_w_out = from_panels(mixer_sums[in_rows : in_rows + out_rows], chans, width)
-    small = mixer_sums[in_rows + out_rows :][: 8 * width // LANES]
+    total_w_gate = sums[:, :hidden]
+    total_w_up = sums[:, hidden : 2 * hidden]
+    total_w_down = sums[:, 2 * hidden : 3 * hidden].T
+    mixer_sums = sums[:, 3 * hidden :]
+    total_w_in = mixer_sums[:, : 3 * chans].reshape(width, 3, chans)
+    out_parts = mixer_sums[:, 3 * chans : 4 * chans]
+    out_parts = out_parts.reshape(width // chans, chans, chans // LANES, LANES)
+    total_w_out = out_parts.transpose(1, 2, 0, 3).reshape(chans, width)
+    small = mixer_sums[: 8 * width // LANES, 4 * chans :]
     small = small.reshape(width // LANES, 8, LANES).transpose(1, 0, 2).reshape(8, width)
     total_gain_mix, total_gain_ffn = small[0], small[1]
     total_conv = lax.dynamic_slice(small, (2, tp_at * chans), (3, chans))

time: 699 us -> 669 us (0.957)
  local copies, waits for them, and re-layouts: 119 us -> 97.3 us
  other arithmetic: 61.6 us -> 53.8 us
    unnamed x52 -> x45, local copies, waits for them, and re-layouts: 52.7 us -> 33.2 us
    concatenate x1 -> x0, other arithmetic: 11.2 us -> none  [per_device(): ffn_sums = jnp.concatenate([ffn_sums, mixer_sums[:rest.shape[0]]], axis=0)]
where the time goes in v5:
time: 669 us; the launch traced here: 662 us
  Pallas kernels  490 us (73%)
  local copies, waits for them, and re-layouts  97.3 us (15%)
  other arithmetic  53.8 us (8%)
  matrix products  16.4 us (2%)
    pallas_call x1, Pallas kernels, ffn_both_ways(): pl.pallas_call(functools.partial(ffn_kernel, lax.axis_size('seq') // 2),...  222 us
    pallas_call x1, Pallas kernels, mixer_back(): pl.pallas_call(functools.partial(mixer_kernel, lax.axis_size('seq') // 2)...  189 us
    pallas_call x1, Pallas kernels, gather_mixer(): pl.pallas_call(functools.partial(gather_kernel, count // 2), out_shape=[j...  78.3 us
    unnamed x45, local copies, waits for them, and re-layouts  33.2 us
    dot_general x1, matrix products, per_device(): projected = jnp.dot(normed_in, w_in_all, preferred_element_type=jnp.float32)  13.7 us
  transfers between devices with their start and end apart: 2, of which 0 were waited for; matrix products, arithmetic and copies ran while one was open for 7% of the time, Pallas kernels for 0%

profile of v5, /device:TPU:0, one launch (start us, length us, event | category | flops | bytes accessed | tf_op | source)
XLA Modules:
  0.0 662.1 jit_solution(1711563322233730101)
XLA Ops:
  3.9 3.3 multiply_reduce_fusion.1
  7.2 4.2 copy.52
  11.4 78.3 %gather_mixer.1 = (bf16[1024,3072]{1,0:T(8,128)(2,1)}, bf16[1024,1024]{1,0:T(8,128)(2,1)S(1)}, f32[8,1024]{1,0:T(8,128)S(1)}) custom-call(bf16[1024,768]{1,0:T(8,128)(2,1)S(1)} %copy.35.w_in, bf16[256,1024]{1,0:T(8,128)(2,1)S(1)} %copy-done, f32[8,256]{1,0:T(8,128)S(1)} %pad.4.taps), custom_call_target="tpu_custom_call" | custom-call | tf_op jit(solution)/shard_map/gather_mixer/pallas_call | solution.py:713
  89.8 13.7 %fusion.9.refs_5_ = f32[1024,3072]{1,0:T(8,128)} fusion(bf16[1024,3072]{1,0:T(8,128)(2,1)} %get-tuple-element.21.refs_9_, f32[1024,1024]{0,1:T(8,128)} %copy.52, f32[1024]{0:T(1024)S(1)} %bitcast.75, f32[1024]{0:T(1024)S(1)} %copy-done.13), kind=kOutput, calls=%fused_computation.39 | convolution fusion | flops 6445596672 | bytes 23076864 | tf_op jit(solution)/shard_map/dot_general | solution.py:1253
  103.5 7.7 %slice_multiply_fusion = (f32[1024,1024]{1,0:T(8,128)S(1)}, f32[1024,1024]{1,0:T(8,128)}) fusion(f32[1024,3072]{1,0:T(8,128)} %fusion.9.refs_5_, f32[1024]{0:T(1024)S(1)} %bitcast.81), kind=kLoop, calls=%fused_computation.16 | loop fusion | flops 2097152 | bytes 20975616 | tf_op jit(solution)/shard_map/mul | solution.py:1258
  114.4 5.3 copy.54
  119.7 6.9 %fusion.5 = f32[2,512,1024]{2,1,0:T(8,128)} fusion(f32[2,2,1024]{2,1,0:T(2,128)S(1)} %collective-permute-done, f32[2,512,1024]{2,1,0:T(8,128)} %bitcast.57, f32[1024]{0:T(1024)S(1)} %bitcast.79, f32[1024]{0:T(1024)S(1)} %bitcast.80, f32[1024]{0:T(1024)S(1)} %bitcast.78), kind=kLoop, calls=%fused_computation.13 | loop fusion | flops 7340032 | bytes 8417280 | tf_op jit(solution)/shard_map/add | solution.py:1262
  126.7 5.3 copy.53
  132.0 4.3 multiply_convert_fusion.1
  155.3 4.9 fusion.1.refs_2_
  160.2 6.5 copy.44.refs_3_
  166.7 3.2 constant_dynamic-slice_fusion.refs_11_
  169.9 4.4 maximum_bitcast_fusion.refs_4_
  176.0 5.4 copy.45.refs_4_
  181.4 4.7 pad_maximum_fusion.refs_6_
  186.1 3.8 broadcast_select_fusion.1
  192.4 6.4 copy.43.refs_0_
  198.8 221.9 %ffn_both_ways.1 = (f32[1024,4608]{1,0:T(8,128)}, f32[9216,128]{1,0:T(8,128)}, f32[1024,1024]{1,0:T(8,128)}, f32[1024,1024]{1,0:T(8,128)}, f32[1024,1024]{1,0:T(...) custom-call(bf16[2048,1024]{1,0:T(8,128)(2,1)} %copy.43.refs_0_, bf16[1024,2048]{1,0:T(8,128)(2,1)} %bitcast.60, ...), custom_call_target="tpu_custom_call" | custom-call | flops 43486543872 | bytes 838860800 | tf_op jit(solution)/shard_map/ffn_both_ways/pallas_call | solution.py:504
  420.7 189.4 %mixer_back.1 = (f32[1024,4608]{1,0:T(8,128)}, f32[2048,1024]{1,0:T(8,128)}, f32[2048,1024]{1,0:T(8,128)}, f32[1024,1024]{1,0:T(8,128)}, f32[4,6,256,128]{3,2,1,...) custom-call(f32[9216,128]{1,0:T(8,128)} %get-tuple-element.24.refs_0_, ...), custom_call_target="tpu_custom_call", output_to_operand_aliasing={{0}: (17, {})} | custom-call | flops 27917287424 | bytes 419430400 | tf_op jit(solution)/shard_map/mixer_back/pallas_call | solution.py:1154
  615.2 10.6 %slice_bitcast_fusion = (f32[1152,1024]{0,1:T(8,128)}, f32[1024,1152]{1,0:T(8,128)}, f32[1024,1152]{1,0:T(8,128)}) fusion(f32[1024,4608]{1,0:T(8,128)} %get-tuple-element.31), kind=kLoop, calls=%fused_computation.6 | loop fusion | bytes 28311552 | tf_op jit(solution)/shard_map/transpose | solution.py:1312
  625.8 5.9 multiply_convert_fusion
  640.5 6.0 copy.50
  648.9 3.5 copy.49
  653.1 8.4 %copy.62 = f32[4,512,1024]{2,1,0:T(8,128)} copy(f32[4,512,1024]{2,1,0:T(8,128)} %bitcast.67) | data formatting | bytes 16777216
  (70 shorter events, 46.3 us)
Async XLA Ops:
  7.2 4.2 copy-start.15
  7.2 4.2 copy-start
  7.2 82.5 %copy-start.13 = (f32[1024]{0:T(1024)S(1)}, f32[1024]{0:T(1024)}, u32[]{:S(2)}) copy-start(f32[1024]{0:T(1024)} %param.13) | copy-start | bytes 12292
  89.7 13.7 %copy-start.2 = (bf16[1024,1024]{1,0:T(8,128)(2,1)}, bf16[1024,1024]{1,0:T(8,128)(2,1)S(1)}, u32[]{:S(2)}) copy-start(bf16[1024,1024]{1,0:T(8,128)(2,1)S(1)} %get-tuple-element.23.refs_10_) | copy-start | bytes 6291460
  89.8 24.6 %copy-start.1 = (f32[8,1024]{1,0:T(8,128)}, f32[8,1024]{1,0:T(8,128)S(1)}, u32[]{:S(2)}) copy-start(f32[8,1024]{1,0:T(8,128)S(1)} %get-tuple-element.22.refs_14_) | copy-start | bytes 98308
  111.2 3.1 copy-start.4
  111.3 8.5 %collective-permute-start = (f32[2,2,1024]{2,1,0:T(2,128)S(1)}, f32[2,2,1024]{2,1,0:T(2,128)S(1)}, u32[]{:S(2)}, u32[]{:S(2)}) collective-permute-start(f32[2,2,1024]{2,1,0:T(2,128)S(1)} %slice.77), channel_id=1, source_target_pairs={{0,4},{4,8},{8,12},{12,16},{16,20},{20,24},{24,28},{1,5},{5,9},{9,... | collective-permute-start | bytes 49160 | tf_op jit(solution)/shard_map/ppermute | solution.py:36
  132.0 4.4 copy-start.3
  132.0 5.3 copy-start.7
  136.4 3.6 copy-start.10
  140.0 3.2 copy-start.5
  143.2 42.9 %collective-permute-start.1 = (f32[1024,1024]{0,1:T(8,128)}, f32[1024,1024]{0,1:T(8,128)}, u32[]{:S(2)}, u32[]{:S(2)}) collective-permute-start(f32[1024,1024]{0,1:T(8,128)} %broadcast_multiply_fusion), channel_id=1, source_target_pairs={{0,1},{1,0},{2,3},{3,2},{4,5},{5,4},{6,7},{7,6},{8,9},{9,8},{10,11... | collective-permute-start | bytes 12582920 | tf_op jit(solution)/shard_map/ppermute | solution.py:40
  143.7 11.6 %copy-start.11 = (f32[1,4,4,128]{3,1,2,0:T(4,128)}, f32[1,4,4,128]{3,1,2,0:T(4,128)S(1)}, u32[]{:S(2)}) copy-start(f32[1,4,4,128]{3,1,2,0:T(4,128)S(1)} %copy.55) | copy-start | bytes 24580
  166.6 3.2 copy-start.9
  169.9 4.4 copy-start.8
  181.4 4.7 copy-start.6
  186.1 3.8 copy-start.14
  615.2 10.6 %copy-start.12 = (f32[1,4,4,128]{3,1,2,0:T(4,128)S(1)}, f32[1,4,4,128]{3,1,2,0:T(4,128)}, u32[]{:S(2)}) copy-start(f32[1,4,4,128]{3,1,2,0:T(4,128)} %copy-done.11) | copy-start | bytes 24580

commit v6 on v5

--- a/solution.py
+++ b/solution.py
@@ -28,16 +28,6 @@
     return lax.dot_general(
         left, right, (((1,), (1,)), ((), ())), preferred_element_type=jnp.float32
     )
-
-
-def shift_seq(block, distance):
-    count = lax.axis_size("seq")
-    route = [(i - distance, i) for i in range(count) if 0 <= i - distance < count]
-    return lax.ppermute(block, "seq", route)
-
-
-def swap_tp(block, bit):
-    return lax.ppermute(block, "tp", [(i, i ^ bit) for i in range(lax.axis_size("tp"))])
 
 
 def greet_seq(places, others=(), more=0):
@@ -307,6 +297,8 @@
     return [half] * 4 + [wide] * 4 + [pltpu.SemaphoreType.DMA((20, SLOTS_IN_FLIGHT))]
 
 
+SUB_ROWS = 64
+SUB_COLS = 256
 FFN_PIECES = 36
 FFN_PANELS = 27
 FFN_PARTS = 3
@@ -323,11 +315,11 @@
 
 
 def ffn_kernel(places, *refs):
-    (mid_hbm, mid_t_hbm, cot_hbm, cot_t_hbm, w_gu_hbm, w_d_hbm) = refs[0:6]
+    (mid_hbm, cot_hbm, w_gate_hbm, w_up_hbm, w_d_hbm, valid) = refs[0:6]
     (sums, rest, mid_chip, mid_far, ffn_chip, mid_land, ffn_land) = refs[6:13]
-    (mid, mid_t, cot, cot_t, w_gu, w_d, act, ggu, own, staged, fetched) = refs[13:24]
-    load_sems, near_sems, far_sems, keep_sem, fetch_sem = refs[24:29]
-    summer = SeqSum(places, own, sums, panel_in_sums, refs[29:])
+    (mid, cot, w_gu, w_d, act, ggu, own, staged, fetched) = refs[13:22]
+    load_sems, near_sems, far_sems, keep_sem, fetch_sem = refs[22:27]
+    summer = SeqSum(places, own, sums, panel_in_sums, refs[27:])
     tp_at = lax.axis_index("tp")
     core = lax.rem(tp_at, 2)
     sibling = tp_at + 1 - 2 * core
@@ -337,24 +329,23 @@
     hidden = wide // 2
     panels = 3 * hidden // LANES
 
+    moves = [(mid_hbm, mid), (cot_hbm, cot), (w_d_hbm, w_d)]
+    for c in range(parts):
+        for i, source in enumerate((w_gate_hbm, w_up_hbm)):
+            moves.append(
+                (
+                    source.at[:, c * hidden : (c + 1) * hidden],
+                    w_gu.at[c, :, i * hidden : (i + 1) * hidden],
+                )
+            )
     loads = [
-        pltpu.make_async_copy(src, dst, load_sems.at[i])
-        for i, (src, dst) in enumerate(
-            (
-                (mid_hbm, mid),
-                (w_gu_hbm, w_gu),
-                (cot_hbm, cot),
-                (w_d_hbm, w_d),
-                (mid_t_hbm, mid_t),
-                (cot_t_hbm, cot_t),
-            )
-        )
+        pltpu.make_async_copy(src, dst, load_sems.at[i]) for i, (src, dst) in enumerate(moves)
     ]
     for load in loads:
         load.start()
     greet_seq(places, ({"tp": sibling}, {"tp": across}))
     count = FFN_PIECES
-    for load in loads[:4]:
+    for load in loads:
         load.wait()
 
     def part_cols(c):
@@ -365,6 +356,11 @@
         @pl.loop(0, rows // ROW_BLOCK)
         def _(r):
             at = pl.ds(pl.multiple_of(r * ROW_BLOCK, ROW_BLOCK), ROW_BLOCK)
+
+            @pl.when(c == 0)
+            def _():
+                cot[at, :] = (valid[at, :] * cot[at, :].astype(jnp.float32)).astype(jnp.bfloat16)
+
             both = jnp.dot(mid[at, :], w_gu[c], preferred_element_type=jnp.float32)
             gate, up = both[:, :hidden], both[:, hidden:]
             grad_act = dot_cols(cot[at, :], w_d[c])
@@ -375,11 +371,6 @@
             ggu[c, at, :hidden] = (grad_act * up * slope).astype(jnp.bfloat16)
             ggu[c, at, hidden:] = (grad_act * silu).astype(jnp.bfloat16)
 
-        @pl.when(c == 0)
-        def _():
-            for load in loads[4:]:
-                load.wait()
-
         @pl.loop(0, width // OUT_BLOCK)
         def _(m):
             first = pl.multiple_of(m * OUT_BLOCK, OUT_BLOCK)
@@ -391,11 +382,8 @@
                     to = pl.multiple_of(base + (panel + j) * width, OUT_BLOCK)
                     own[pl.ds(to, OUT_BLOCK), :] = block[:, j * LANES : (j + 1) * LANES]
 
-            put(jnp.dot(mid_t[at, :], ggu[c], preferred_element_type=jnp.float32), 0)
-            put(
-                jnp.dot(cot_t[at, :], act[:, part_cols(c)], preferred_element_type=jnp.float32),
-                wide // LANES,
-            )
+            put(dot_rows(mid[:, at], ggu[c]), 0)
+            put(dot_rows(cot[:, at], act[:, part_cols(c)]), wide // LANES)
 
             @pl.when(c > 0)
             def _():
@@ -486,15 +474,11 @@
         far(k).wait()
 
 
-def ffn_both_ways(normed_mid, grad_ffn, w_gate, w_up, w_down, sum_cols, collective_id):
+def ffn_both_ways(normed_mid, cotangent, w_gate, w_up, w_down, valid, sum_cols, collective_id):
     rows, width = normed_mid.shape
     local = w_gate.shape[1]
     hidden = local // FFN_PARTS
 
-    def in_parts(weights):
-        return weights.reshape(width, FFN_PARTS, hidden)
-
-    w_gu = jnp.concatenate([in_parts(w_gate), in_parts(w_up)], axis=2).transpose(1, 0, 2)
     w_d = w_down.reshape(FFN_PARTS, hidden, width)
     grad_rows = 3 * local * width // LANES
     summed = FFN_PIECES * 4 * HALF
@@ -508,21 +492,20 @@
             jax.ShapeDtypeStruct((grad_rows - summed, LANES), jnp.float32),
         ]
         + [half] * 5,
-        in_specs=[pl.BlockSpec(memory_space=pl.ANY)] * 6,
+        in_specs=[pl.BlockSpec(memory_space=pl.ANY)] * 5
+        + [pl.BlockSpec(memory_space=pltpu.VMEM)],
         out_specs=[pl.BlockSpec(memory_space=pl.ANY)] * 7,
         scratch_shapes=[
             pltpu.VMEM((rows, width), low),
-            pltpu.VMEM((width, rows), low),
             pltpu.VMEM((rows, width), low),
-            pltpu.VMEM((width, rows), low),
-            pltpu.VMEM(w_gu.shape, low),
+            pltpu.VMEM((FFN_PARTS, width, 2 * hidden), low),
             pltpu.VMEM(w_d.shape, low),
             pltpu.VMEM((rows, local), low),
             pltpu.VMEM((FFN_PARTS, rows, 2 * hidden), low),
             pltpu.VMEM((grad_rows, LANES), jnp.float32),
             pltpu.VMEM((2, OUT_BLOCK, width), jnp.float32),
             pltpu.VMEM((OUT_BLOCK, width), jnp.float32),
-            pltpu.SemaphoreType.DMA((6,)),
+            pltpu.SemaphoreType.DMA((3 + 2 * FFN_PARTS,)),
             pltpu.SemaphoreType.DMA((2, 2, blocks)),
             pltpu.SemaphoreType.DMA((2, blocks)),
             pltpu.SemaphoreType.DMA,
@@ -536,16 +519,22 @@
             flops=18 * rows * width * local, bytes_accessed=800 << 20, transcendentals=0
         ),
         name="ffn_both_ways",
-    )(normed_mid, normed_mid.T, grad_ffn, grad_ffn.T, w_gu, w_d)
-
-
-def gather_kernel(places, w_in, w_out, taps, full_in, full_out, full_taps, *scratch):
-    own_in, own_out, far_in, far_out, sib_in, sib_out, sibfar_in, sibfar_out = scratch[0:8]
-    own_taps, far_taps, sib_taps, sibfar_taps, share_in, share_out = scratch[8:14]
-    sends, recvs, once = scratch[14:17]
+    )(normed_mid, cotangent, w_gate, w_up, w_d, valid)
+
+
+def front_kernel(places, slots, *refs):
+    (w_in, w_out, taps, gain_mix, gain_ffn, valid, tokens_hbm) = refs[0:7]
+    (in_hbm, out_hbm, full_taps, mid_hbm, hidden_hbm, proj_hbm, gated_hbm) = refs[7:14]
+    (normed_hbm, mixed_hbm) = refs[14:16]
+    own_in, own_out, far_in, far_out, sib_in, sib_out, sibfar_in, sibfar_out = refs[16:24]
+    own_taps, far_taps, sib_taps, sibfar_taps, share_in, share_out = refs[24:30]
+    (full_in, full_out, tokens, normed, mixed, out_gate, gates, gated) = refs[30:38]
+    (unit_out, unit_in, hidden) = refs[38:41]
+    sends, recvs, once, halo_sems, gate_sems, unit_sems, keep_sems, mid_sems = refs[41:49]
     here = lax.axis_index("seq")
     place, side = here // 2, lax.rem(here, 2)
     last = places - 1
+    end = 2 * places - 1
     tp_at = lax.axis_index("tp")
     core = lax.rem(tp_at, 2)
     sibling = tp_at + 1 - 2 * core
@@ -554,9 +543,23 @@
     in_rows = w_in.shape[0] // (2 * places)
     out_rows = w_out.shape[0] // (2 * places)
     chans = w_in.shape[1] // 3
-    width = w_out.shape[1]
-
-    greet_seq(places, ({"tp": sibling}, {"tp": across}))
+    rows, width = tokens.shape
+    slot_len = rows // slots
+    low = jnp.bfloat16
+
+    load_tokens = pltpu.make_async_copy(
+        tokens_hbm.at[pl.ds(pl.multiple_of(core * rows, rows), rows)], tokens, keep_sems.at[0]
+    )
+    load_tokens.start()
+    barrier = pltpu.get_barrier_semaphore()
+
+    def signal(device):
+        pl.semaphore_signal(barrier, inc=1, device_id=device, device_id_type=pl.DeviceIdType.MESH)
+
+    pl.when(here > 0)(lambda: signal({"seq": here - 1}))
+    pl.when(here < end)(lambda: signal({"seq": here + 1}))
+    ends = jnp.where(here > 0, 1, 0) + jnp.where(here < end, 1, 0)
+    greet_seq(places, ({"tp": sibling}, {"tp": across}), ends)
 
     def shares(j):
         return (
@@ -564,15 +567,24 @@
             pl.ds(pl.multiple_of(j * out_rows, out_rows), out_rows),
         )
 
+    def remote(src, dst, send, recv, device):
+        return pltpu.make_async_remote_copy(
+            src_ref=src,
+            dst_ref=dst,
+            send_sem=send,
+            recv_sem=recv,
+            device_id=device,
+            device_id_type=pl.DeviceIdType.MESH,
+        )
+
     def copies(source, target, j, kind, device):
         for i, at in enumerate(shares(j)):
-            yield pltpu.make_async_remote_copy(
-                src_ref=source[i] if kind == 0 else source[i].at[at],
-                dst_ref=target[i].at[at],
-                send_sem=sends.at[kind, i, j],
-                recv_sem=recvs.at[0 if kind < 4 else 1, i, j],
-                device_id=device,
-                device_id_type=pl.DeviceIdType.MESH,
+            yield remote(
+                source[i] if kind == 0 else source[i].at[at],
+                target[i].at[at],
+                sends.at[kind, i, j],
+                recvs.at[0 if kind < 4 else 1, i, j],
+                device,
             )
 
     share, far, sibfar = (share_in, share_out), (far_in, far_out), (sibfar_in, sibfar_out)
@@ -605,14 +617,7 @@
             copy.wait_send()
 
     def single(i, src, dst, device):
-        return pltpu.make_async_remote_copy(
-            src_ref=src,
-            dst_ref=dst,
-            send_sem=once.at[0, i],
-            recv_sem=once.at[1, i],
-            device_id=device,
-            device_id_type=pl.DeviceIdType.MESH,
-        )
+        return remote(src, dst, once.at[0, i], once.at[1, i], device)
 
     for source, held, at in zip((w_in, w_out), share, shares(here)):
         held[...] = source[at, :].astype(jnp.float32)
@@ -628,22 +633,116 @@
     for copy in (taps_far, taps_sib, in_sib, out_sib):
         copy.start()
 
+    def gate_cols(g, index):
+        return pl.ds(pl.multiple_of(g * width + index * chans, LANES), chans)
+
+    def place_shard(shard_in, shard_out, shard_taps, index):
+        for g in range(3):
+            full_in[:, gate_cols(g, index)] = shard_in[:, g * chans : (g + 1) * chans].astype(low)
+        at = pl.ds(pl.multiple_of(index * chans, chans), chans)
+        full_out[at, :] = shard_out[...].astype(low)
+        full_taps[:, gate_cols(0, index)] = shard_taps[...]
+
+    def gate_out(turn, index, g):
+        if g == 1:
+            return pltpu.make_async_copy(
+                out_gate.at[:, gate_cols(0, index)],
+                proj_hbm.at[:, gate_cols(1, index)],
+                gate_sems.at[turn, 1],
+            )
+        return pltpu.make_async_copy(
+            gates.at[turn % 2, g // 2], proj_hbm.at[:, gate_cols(g, index)], gate_sems.at[turn, g]
+        )
+
+    def halo(turn, index, slot):
+        return remote(
+            gated.at[slot, pl.ds(slot_len, 8), gate_cols(0, index)],
+            gated.at[slot, pl.ds(0, 8), gate_cols(0, index)],
+            halo_sems.at[0, turn, slot],
+            halo_sems.at[1, turn, slot],
+            {"seq": here + 1},
+        )
+
+    order = (tp_at, sibling, across, far_sibling)
+
+    def project(turn):
+        index = order[turn]
+        cols = gate_cols(0, index)
+        if turn >= 2:
+            gate_out(turn - 2, order[turn - 2], 0).wait()
+            gate_out(turn - 2, order[turn - 2], 2).wait()
+
+        @pl.loop(0, slots)
+        def _(s):
+            at = pl.ds(pl.multiple_of(s * slot_len, slot_len), slot_len)
+
+            def gate(g):
+                return jnp.dot(
+                    normed[at, :], full_in[:, gate_cols(g, index)],
+                    preferred_element_type=jnp.float32,
+                )
+
+            in_gate, value = gate(0), gate(2)
+            gates[turn % 2, 0, at, :] = in_gate
+            gates[turn % 2, 1, at, :] = value
+            gated[s, pl.ds(8, slot_len), cols] = valid[at, :] * in_gate * value
+            out_gate[at, cols] = gate(1)
+
+        for g in range(3):
+            gate_out(turn, index, g).start()
+
+        @pl.when(here < end)
+        def _():
+            for slot in range(slots):
+                halo(turn, index, slot).start()
+
+    def convolve(turn):
+        index = order[turn]
+        cols = gate_cols(0, index)
+
+        @pl.when(here > 0)
+        def _():
+            for slot in range(slots):
+                halo(turn, index, slot).wait_recv()
+
+        @pl.loop(0, slots)
+        def _(s):
+            at = pl.ds(pl.multiple_of(s * slot_len, slot_len), slot_len)
+            seen = [gated[s, pl.ds(6 + j, slot_len), cols] for j in range(3)]
+            tap = [full_taps[j : j + 1, cols] for j in range(3)]
+            conv_sum = tap[0] * seen[0] + tap[1] * seen[1] + tap[2] * seen[2]
+            mixed[at, cols] = (out_gate[at, cols] * conv_sum).astype(low)
+
+    @pl.when(here == 0)
+    def _():
+        for slot in range(slots):
+            gated[slot, pl.ds(0, 8), :] = jnp.zeros((8, width), jnp.float32)
+
+    load_tokens.wait()
+
+    @pl.loop(0, rows // SUB_ROWS)
+    def _(r):
+        at = pl.ds(pl.multiple_of(r * SUB_ROWS, SUB_ROWS), SUB_ROWS)
+        inputs = tokens[at, :].astype(jnp.float32)
+        normed[at, :] = (gain_mix[...] * (inputs * rms_scale(inputs))).astype(low)
+
+    keep_normed = pltpu.make_async_copy(normed, normed_hbm, keep_sems.at[0])
+    keep_normed.start()
+    place_shard(own_in, own_out, own_taps, tp_at)
+    project(0)
+
     arrived(across_share())
-    start(to_side(here))
     pl.when(place < last)(lambda: start(to_right(here)))
     pl.when(place > 0)(lambda: start(to_left(here)))
+    start(to_side(here))
     start(to_sibling(here))
     taps_far.wait_recv()
     taps_sibfar.start()
-
-    def place_shard(shard_in, shard_out, shard_taps, index):
-        for g in range(3):
-            cols = pl.ds(pl.multiple_of(g * width + index * chans, LANES), chans)
-            full_in[:, cols] = shard_in[:, g * chans : (g + 1) * chans].astype(jnp.bfloat16)
-        rows = pl.ds(pl.multiple_of(index * chans, chans), chans)
-        full_out[rows, :] = shard_out[...].astype(jnp.bfloat16)
-        cols = pl.ds(pl.multiple_of(index * chans, LANES), chans)
-        full_taps[:, cols] = shard_taps[...]
+    in_sib.wait_recv()
+    out_sib.wait_recv()
+    taps_sib.wait_recv()
+    place_shard(sib_in, sib_out, sib_taps, sibling)
+    project(1)
 
     def from_side(q):
         j = 2 * q + 1 - side
@@ -671,16 +770,14 @@
         @pl.when(d == 1)
         def _():
             from_side(place)
-            place_shard(own_in, own_out, own_taps, tp_at)
-            in_sib.wait_recv()
-            out_sib.wait_recv()
-            taps_sib.wait_recv()
-            place_shard(sib_in, sib_out, sib_taps, sibling)
+            convolve(0)
+            convolve(1)
 
         pl.when(place - d >= 0)(lambda: from_side(place - d))
         pl.when(place + d <= last)(lambda: from_side(place + d))
 
     place_shard(far_in, far_out, far_taps, across)
+    project(2)
     taps_sibfar.wait_recv()
 
     @pl.loop(0, 2 * places)
@@ -688,6 +785,95 @@
         arrived(to_sibling(j))
 
     place_shard(sibfar_in, sibfar_out, sibfar_taps, far_sibling)
+    project(3)
+    keep_in = pltpu.make_async_copy(full_in, in_hbm, keep_sems.at[1])
+    keep_out = pltpu.make_async_copy(full_out, out_hbm, keep_sems.at[2])
+    keep_in.start()
+    keep_out.start()
+    convolve(2)
+    convolve(3)
+    keep_gated = pltpu.make_async_copy(gated, gated_hbm, keep_sems.at[3])
+    keep_mixed = pltpu.make_async_copy(mixed, mixed_hbm, keep_sems.at[4])
+    keep_gated.start()
+    keep_mixed.start()
+    keep_normed.wait()
+
+    blocks = rows // OUT_BLOCK
+
+    def block_at(k, first=0):
+        return pl.ds(pl.multiple_of(first + k * OUT_BLOCK, OUT_BLOCK), OUT_BLOCK)
+
+    def unit_copy(k):
+        return remote(
+            unit_out.at[block_at(k)], unit_in.at[block_at(k)],
+            unit_sems.at[0, k], unit_sems.at[1, k], {"tp": sibling},
+        )
+
+    def hidden_copy(k):
+        return pltpu.make_async_copy(
+            hidden.at[lax.rem(k, 2)], hidden_hbm.at[block_at(k)], mid_sems.at[0, lax.rem(k, 2)]
+        )
+
+    def mid_copy(half, held, whose, k):
+        return pltpu.make_async_copy(
+            held.at[block_at(k)], mid_hbm.at[block_at(k, whose * rows)], mid_sems.at[half, k]
+        )
+
+    @pl.loop(0, blocks)
+    def _(k):
+        slot = lax.rem(k, 2)
+        at = block_at(k)
+        pl.when(k >= 2)(lambda: hidden_copy(k - 2).wait())
+        hidden[slot] = jnp.dot(mixed[at, :], full_out[...], preferred_element_type=jnp.float32)
+
+        @pl.loop(0, OUT_BLOCK // SUB_ROWS)
+        def _(r):
+            sub = pl.ds(pl.multiple_of(r * SUB_ROWS, SUB_ROWS), SUB_ROWS)
+            whole = pl.ds(pl.multiple_of(k * OUT_BLOCK + r * SUB_ROWS, SUB_ROWS), SUB_ROWS)
+            hidden_rows = tokens[whole, :].astype(jnp.float32) + hidden[slot, sub, :]
+            hidden[slot, sub, :] = hidden_rows
+            unit = hidden_rows * rms_scale(hidden_rows)
+            unit_out[whole, :] = unit
+            normed[whole, :] = (gain_ffn[...] * unit).astype(low)
+
+        unit_copy(k).start()
+        hidden_copy(k).start()
+        mid_copy(1, normed, core, k).start()
+
+    keep_mixed.wait()
+
+    @pl.loop(0, blocks)
+    def _(k):
+        unit_copy(k).wait_recv()
+
+        @pl.loop(0, OUT_BLOCK // SUB_ROWS)
+        def _(r):
+            whole = pl.ds(pl.multiple_of(k * OUT_BLOCK + r * SUB_ROWS, SUB_ROWS), SUB_ROWS)
+            mixed[whole, :] = (gain_ffn[...] * unit_in[whole, :]).astype(low)
+
+        mid_copy(2, mixed, 1 - core, k).start()
+
+    @pl.loop(0, blocks)
+    def _(k):
+        unit_copy(k).wait_send()
+        mid_copy(1, normed, core, k).wait()
+        mid_copy(2, mixed, 1 - core, k).wait()
+
+    for k in range(max(blocks - 2, 0), blocks):
+        hidden_copy(k).wait()
+    keep_in.wait()
+    keep_out.wait()
+    keep_gated.wait()
+    for turn in range(4):
+        for g in range(3):
+            if turn >= 2 or g == 1:
+                gate_out(turn, order[turn], g).wait()
+
+    @pl.when(here < end)
+    def _():
+        for turn in range(4):
+            for slot in range(slots):
+                halo(turn, order[turn], slot).wait_send()
 
     left_source(across_share())
     for copy in (taps_far, taps_sib, taps_sibfar, in_sib, out_sib):
@@ -703,42 +889,70 @@
         left_source(to_sibling(2 * q + 1 - side))
 
 
-def gather_mixer(w_in, w_out, taps, collective_id):
+def mixer_front(w_in, w_out, taps, gain_mix, gain_ffn, valid, tokens, slots, collective_id):
     width, _, chans = w_in.shape
+    rows = valid.shape[0]
     count = lax.axis_size("seq")
     group = lax.axis_size("tp")
-    f32 = jnp.float32
+    f32, low = jnp.float32, jnp.bfloat16
+    blocks = rows // OUT_BLOCK
     pair = [pltpu.VMEM((width, 3 * chans), f32), pltpu.VMEM((chans, width), f32)]
     whole = pl.BlockSpec(memory_space=pltpu.VMEM)
+    anywhere = pl.BlockSpec(memory_space=pl.ANY)
+    padded = (slots, rows // slots + 8, width)
     return pl.pallas_call(
-        functools.partial(gather_kernel, count // 2),
+        functools.partial(front_kernel, count // 2, slots),
         out_shape=[
-            jax.ShapeDtypeStruct((width, 3 * chans * group), jnp.bfloat16),
-            jax.ShapeDtypeStruct((chans * group, width), jnp.bfloat16),
+            jax.ShapeDtypeStruct((width, 3 * chans * group), low),
+            jax.ShapeDtypeStruct((chans * group, width), low),
             jax.ShapeDtypeStruct((8, chans * group), f32),
+            jax.ShapeDtypeStruct((2 * rows, width), low),
+            jax.ShapeDtypeStruct((rows, width), f32),
+            jax.ShapeDtypeStruct((rows, 3 * width), f32),
+            jax.ShapeDtypeStruct(padded, f32),
+            jax.ShapeDtypeStruct((rows, width), low),
+            jax.ShapeDtypeStruct((rows, width), low),
         ],
-        in_specs=[whole] * 3,
-        out_specs=[whole] * 3,
+        in_specs=[whole] * 6 + [anywhere],
+        out_specs=[anywhere] * 2 + [whole] + [anywhere] * 6,
         scratch_shapes=pair * 4
         + [pltpu.VMEM((8, chans), f32)] * 4
         + [
             pltpu.VMEM((width // count, 3 * chans), f32),
             pltpu.VMEM((chans // count, width), f32),
-        ]
-        + [
+            pltpu.VMEM((width, 3 * chans * group), low),
+            pltpu.VMEM((chans * group, width), low),
+            pltpu.VMEM((rows, width), low),
+            pltpu.VMEM((rows, width), low),
+            pltpu.VMEM((rows, width), low),
+            pltpu.VMEM((rows, width), f32),
+            pltpu.VMEM((2, 2, rows, chans), f32),
+            pltpu.VMEM(padded, f32),
+            pltpu.VMEM((rows, width), f32),
+            pltpu.VMEM((rows, width), f32),
+            pltpu.VMEM((2, OUT_BLOCK, width), f32),
             pltpu.SemaphoreType.DMA((5, 2, count)),
             pltpu.SemaphoreType.DMA((2, 2, count)),
             pltpu.SemaphoreType.DMA((2, 5)),
+            pltpu.SemaphoreType.DMA((2, 4, slots)),
+            pltpu.SemaphoreType.DMA((4, 3)),
+            pltpu.SemaphoreType.DMA((2, blocks)),
+            pltpu.SemaphoreType.DMA((5,)),
+            pltpu.SemaphoreType.DMA((3, blocks)),
         ],
         compiler_params=pltpu.CompilerParams(
-            collective_id=collective_id, has_side_effects=True, vmem_limit_bytes=48 << 20
+            collective_id=collective_id, has_side_effects=True, vmem_limit_bytes=VMEM_LIMIT
         ),
-        name="gather_mixer",
-    )(w_in.reshape(width, 3 * chans), w_out, jnp.pad(taps, ((0, 5), (0, 0))))
-
-
-SUB_ROWS = 64
-SUB_COLS = 256
+        name="mixer_front",
+    )(
+        w_in.reshape(width, 3 * chans),
+        w_out,
+        jnp.pad(taps, ((0, 5), (0, 0))),
+        gain_mix,
+        gain_ffn,
+        valid,
+        tokens,
+    )
 
 
 def norm_back(grad, gain, unit, scale):
@@ -748,10 +962,10 @@
 
 def mixer_kernel(places, *refs):
     (rest_hbm, mid_chip, mid_far, ffn_chip, hidden_hbm, proj_hbm, gated_hbm) = refs[0:7]
-    (normed_t_hbm, mixed_t_hbm, w_in_hbm, w_out_hbm, cot_hbm, tokens_hbm) = refs[7:13]
+    (normed_hbm, mixed_hbm, w_in_hbm, w_out_hbm, cot_hbm, tokens_hbm) = refs[7:13]
     (valid, taps, gain_mix, gain_ffn) = refs[13:17]
     (sums, tokens_out, block_out, ffn_far, land_in, land_out, land_small) = refs[18:25]
-    (own, normed_t, mixed_t, w_in, w_out, cot, tokens, grad_mixer, grad_proj) = refs[25:34]
+    (own, normed, mixed, w_in, w_out, cot, tokens, grad_mixer, grad_proj) = refs[25:34]
     (chip, far, hidden, proj, gated, mixed_buf, conv_in, grad_hid, grad_tok) = refs[34:43]
     (halo_out, halo_in, halo_keep, small, small_stage, small_fetch) = refs[43:49]
     (stage_in, fetch_in, stage_out, fetch_out) = refs[49:53]
@@ -777,18 +991,19 @@
     chans = w_out.shape[0] // 4
     count = own.shape[0] // (4 * HALF)
     early_rows = rest_hbm.shape[0]
+    own_half = pl.ds(pl.multiple_of(core * rows, rows), rows)
 
     loads = [
         pltpu.make_async_copy(src, dst, load_sems.at[i])
         for i, (src, dst) in enumerate(
             (
                 (rest_hbm, own.at[pl.ds(0, early_rows)]),
-                (cot_hbm, cot),
+                (cot_hbm.at[own_half], cot),
                 (w_out_hbm, w_out),
-                (tokens_hbm, tokens),
+                (tokens_hbm.at[own_half], tokens),
                 (w_in_hbm, w_in),
-                (normed_t_hbm, normed_t),
-                (mixed_t_hbm, mixed_t),
+                (normed_hbm, normed),
+                (mixed_hbm, mixed),
             )
         )
     ]
@@ -859,11 +1074,11 @@
     small[...] = jnp.zeros_like(small)
     wait(loads[:3])
 
-    def hidden_grad(chip_rows, far_rows, hidden_rows, cot_rows):
+    def hidden_grad(chip_rows, far_rows, hidden_rows, cot_rows, mask):
         grad_mid = chip_rows + far_rows
         scale = rms_scale(hidden_rows)
         unit = hidden_rows * scale
-        grad = cot_rows.astype(jnp.float32) + norm_back(grad_mid, gain_ffn[...], unit, scale)
+        grad = mask * cot_rows.astype(jnp.float32) + norm_back(grad_mid, gain_ffn[...], unit, scale)
         return grad, grad_mid * unit
 
     def halo_copy(slot, device):
@@ -886,7 +1101,9 @@
         ]
         start(copies)
         wait(copies)
-        grad, _ = hidden_grad(chip[top, :], far[top, :], hidden[top, :], cot[at, :])
+        grad, _ = hidden_grad(
+            chip[top, :], far[top, :], hidden[top, :], cot[at, :], valid[at, :]
+        )
         grad_mixed = dot_cols(grad.astype(jnp.bfloat16), w_out[...])
         halo_out[slot] = (grad_mixed * proj[top, width : 2 * width])[:8]
         pl.when(here > 0)(lambda slot=slot: halo_copy(slot, here - 1).start())
@@ -926,7 +1143,9 @@
         def _(r):
             sub = pl.ds(pl.multiple_of(r * SUB_ROWS, SUB_ROWS), SUB_ROWS)
             whole = pl.ds(pl.multiple_of(first + r * SUB_ROWS, SUB_ROWS), SUB_ROWS)
-            grad, for_gain = hidden_grad(chip[sub, :], far[sub, :], hidden[sub, :], cot[whole, :])
+            grad, for_gain = hidden_grad(
+                chip[sub, :], far[sub, :], hidden[sub, :], cot[whole, :], valid[whole, :]
+            )
             grad_hid[sub, :] = grad
             grad_mixer[whole, :] = grad.astype(jnp.bfloat16)
             small[1:2, :] += jnp.sum(for_gain, axis=0, keepdims=True)
@@ -1016,11 +1235,11 @@
     def in_part(m, g, shard):
         at = pl.ds(pl.multiple_of(m * OUT_BLOCK, OUT_BLOCK), OUT_BLOCK)
         cols = pl.ds(pl.multiple_of(g * width + shard * chans, LANES), chans)
-        return jnp.dot(normed_t[at, :], grad_proj[:, cols], preferred_element_type=jnp.float32)
+        return dot_rows(normed[:, at], grad_proj[:, cols])
 
     def out_part(shard):
-        at = pl.ds(pl.multiple_of(shard * chans, chans), chans)
-        return jnp.dot(mixed_t[at, :], grad_mixer[...], preferred_element_type=jnp.float32)
+        at = pl.ds(pl.multiple_of(shard * chans, LANES), chans)
+        return dot_rows(mixed[:, at], grad_mixer[...])
 
     for p in range(width // LANES):
         small_stage[8 * p : 8 * p + 8, :] = small[:, p * LANES : (p + 1) * LANES]
@@ -1139,8 +1358,8 @@
 
 
 def mixer_back(hbm, vmem, sums, slots, collective_id):
-    rest, _, _, _, hidden, _, gated, normed_t, mixed_t, w_in, w_out, _, tokens = hbm
-    rows, width = tokens.shape
+    rest, _, _, _, hidden, _, gated, normed, mixed, w_in, w_out, _, _ = hbm
+    rows, width = normed.shape
     chans = w_out.shape[0] // 4
     blocks = rows // OUT_BLOCK
     in_blocks = width // OUT_BLOCK
@@ -1169,8 +1388,8 @@
         out_specs=[anywhere] * 7,
         scratch_shapes=[
             pltpu.VMEM((grad_rows, LANES), f32),
-            pltpu.VMEM(normed_t.shape, low),
-            pltpu.VMEM(mixed_t.shape, low),
+            pltpu.VMEM(normed.shape, low),
+            pltpu.VMEM(mixed.shape, low),
             pltpu.VMEM(w_in.shape, low),
             pltpu.VMEM(w_out.shape, low),
             pltpu.VMEM((rows, width), low),
@@ -1219,68 +1438,27 @@
 ):
     slot_count, local_len, width = tokens.shape
     chans = w_in.shape[2]
-    group = lax.axis_size("tp")
-    seq_count = lax.axis_size("seq")
     tp_at, seq_at = lax.axis_index("tp"), lax.axis_index("seq")
-    core, chip = tp_at % 2, tp_at // 2
+    core = tp_at % 2
     half_slots = slot_count // 2
     half_rows = half_slots * local_len
     row_count = slot_count * local_len
 
-    def pick(is_first, first, second):
-        return jnp.where(is_first, first, second)
-
-    def both_cores(own, other):
-        return jnp.concatenate(
-            [pick(core == 0, own, other), pick(core == 0, other, own)], axis=0
-        )
-
-    w_in_all, w_out_all, taps = gather_mixer(w_in, w_out, conv_weight, 3)
-
-    first_pos = seq_at * local_len
-    positions = first_pos + jnp.arange(local_len, dtype=jnp.int32)
-    valid = (positions[None, :] < lengths[:, None]).astype(jnp.float32)[:, :, None]
+    positions = seq_at * local_len + jnp.arange(local_len, dtype=jnp.int32)
+    valid = (positions[None, :] < lengths[:, None]).astype(jnp.float32)
     valid_all = valid.reshape(row_count, 1)
-    valid_own = lax.dynamic_slice(valid, (core * half_slots, 0, 0), (half_slots, local_len, 1))
-    valid_rows = valid_own.reshape(half_rows, 1)
-    tokens_own = lax.dynamic_slice(
-        tokens, (core * half_slots, 0, 0), (half_slots, local_len, width)
+    valid_rows = lax.dynamic_slice(valid_all, (core * half_rows, 0), (half_rows, 1))
+    token_rows = tokens.reshape(row_count, width)
+    cot_rows = cotangent.reshape(row_count, width)
+    gains = gain_mix.reshape(1, width), gain_ffn.reshape(1, width)
+    w_in_all, w_out_all, taps, normed_mid, hidden_res, projected, gated_rows, normed_in, mixed = (
+        mixer_front(w_in, w_out, conv_weight, *gains, valid_rows, token_rows, half_slots, 3)
     )
-    inputs_f = tokens_own.astype(jnp.float32).reshape(half_rows, width)
-    scale_mix = rms_scale(inputs_f)
-    unit_mix = inputs_f * scale_mix
-    normed_in = (gain_mix * unit_mix).astype(jnp.bfloat16)
-    projected = jnp.dot(normed_in, w_in_all, preferred_element_type=jnp.float32)
-    in_gate = projected[:, :width]
-    out_gate = projected[:, width : 2 * width]
-    conv_value = projected[:, 2 * width :]
-    seq_shape = (half_slots, local_len, width)
-    gated_seq = (valid_rows * in_gate * conv_value).reshape(seq_shape)
-    carried = shift_seq(gated_seq[:, local_len - 2 :], 1)
-    padded_seq = jnp.concatenate([carried, gated_seq], axis=1)
-    conv_sum = (
-        taps[0] * padded_seq[:, 0:local_len]
-        + taps[1] * padded_seq[:, 1 : local_len + 1]
-        + taps[2] * padded_seq[:, 2 : local_len + 2]
-    ).reshape(half_rows, width)
-    mixed_seq = (out_gate * conv_sum).astype(jnp.bfloat16)
-    mixer_out = jnp.dot(mixed_seq, w_out_all, preferred_element_type=jnp.float32)
-    hidden_res = inputs_f + mixer_out
-    scale_ffn = rms_scale(hidden_res)
-    unit_ffn = hidden_res * scale_ffn
-    unit_all = both_cores(unit_ffn, swap_tp(unit_ffn, 1))
-    normed_mid = (gain_ffn * unit_all).astype(jnp.bfloat16)
-
-    grad_out = valid_all * cotangent.astype(jnp.float32).reshape(row_count, width)
-    grad_ffn = grad_out.astype(jnp.bfloat16)
     mixer_cols = 4 * chans
     sum_cols = FFN_PANELS * LANES + mixer_cols + LANES
     ffn_sums, rest, mid_chip, mid_far, ffn_chip = ffn_both_ways(
-        normed_mid, grad_ffn, w_gate, w_up, w_down, sum_cols, 1
+        normed_mid, cot_rows, w_gate, w_up, w_down, valid_all, sum_cols, 1
     )[:5]
-    cot_own = lax.dynamic_slice(grad_ffn, (core * half_rows, 0), (half_rows, width))
-    lead = jnp.zeros((half_slots, 6, width), jnp.float32)
-    gated_rows = jnp.concatenate([lead, padded_seq], axis=1)
     sums, grad_tokens, block_sum = mixer_back(
         (
             rest,
@@ -1290,14 +1468,14 @@
             hidden_res,
             projected,
             gated_rows,
-            normed_in.T,
-            mixed_seq.T,
+            normed_in,
+            mixed,
             w_in_all,
             w_out_all,
-            cot_own,
-            tokens_own.reshape(half_rows, width),
+            cot_rows,
+            token_rows,
         ),
-        (valid_rows, taps, gain_mix.reshape(1, width), gain_ffn.reshape(1, width)),
+        (valid_rows, taps, *gains),
         ffn_sums,
         half_slots,
         2,

time: 669 us -> 566 us (0.85)
  local copies, waits for them, and re-layouts: 97.3 us -> 46.3 us
  other arithmetic: 53.8 us -> 6.64 us
  Pallas kernels: 490 us -> 511 us
  matrix products: 16.4 us -> 0 us
    dot_general x2 -> x0, matrix products: 16.4 us -> none  [the longest x1 13.7 us: per_device(): projected = jnp.dot(normed_in, w_in_all, preferred_element_type=jnp.float32)]
    pallas_call x1, Pallas kernels: 78.3 us -> 94.5 us  [mixer_front(): pl.pallas_call(functools.partial(front_kernel, count // 2, slots), out_sh...]
    reshape x5 -> x1, local copies, waits for them, and re-layouts: 15.1 us -> 1.57 us  [mixer_front(): w_in.reshape(width, 3 * chans)]
    convert_element_type x3 -> x0, other arithmetic: 11.7 us -> none  [the longest x1 4.86 us: per_device(): grad_ffn = grad_out.astype(jnp.bfloat16)]
    unnamed x45 -> x9, local copies, waits for them, and re-layouts: 33.2 us -> 21.7 us
    mul x2 -> x0, other arithmetic: 10.5 us -> none  [the longest x1 7.75 us: per_device(): gated_seq = (valid_rows * in_gate * conv_value).reshape(seq_shape)]
    add x2 -> x1, other arithmetic: 6.95 us -> 0.01 us  [per_device(): positions = seq_at * local_len + jnp.arange(local_len, dtype=jnp.int32)]
  transfers between devices with their start and end apart: 2 -> 0, of which waited for: 0 -> 0; matrix products, arithmetic and copies ran while one was open for 7% -> 0% of each run, Pallas kernels for 0% -> 0%
where the time goes in v6:
time: 566 us; the launch traced here: 565 us
  Pallas kernels  511 us (90%)
  local copies, waits for them, and re-layouts  46.3 us (8%)
  other arithmetic  6.64 us (1%)
    pallas_call x1, Pallas kernels, ffn_both_ways(): pl.pallas_call(functools.partial(ffn_kernel, lax.axis_size('seq') // 2),...  227 us
    pallas_call x1, Pallas kernels, mixer_back(): pl.pallas_call(functools.partial(mixer_kernel, lax.axis_size('seq') // 2)...  190 us
    pallas_call x1, Pallas kernels, mixer_front(): pl.pallas_call(functools.partial(front_kernel, count // 2, slots), out_sh...  94.5 us
    unnamed x9, local copies, waits for them, and re-layouts  21.7 us

profile of v6, /device:TPU:0, one launch (start us, length us, event | category | flops | bytes accessed | tf_op | source)
XLA Modules:
  0.0 565.1 jit_solution(4731702074756711999)
XLA Ops:
  0.7 1.3 pad.4.refs_2_
  2.0 0.7 convert_bitcast_fusion.1
  2.7 0.6 copy.34
  3.7 1.0 copy-done
  4.7 0.8 constant_dynamic-slice_fusion.1.refs_5_.refs_13_
  5.5 1.7 copy.26
  7.2 1.6 copy.28.refs_0_
  8.8 94.5 %mixer_front.1 = (bf16[1024,3072]{1,0:T(8,128)(2,1)}, bf16[1024,1024]{1,0:T(8,128)(2,1)}, f32[8,1024]{1,0:T(8,128)}, bf16[2048,1024]{1,0:T(8,128)(2,1)}, f32[102...) custom-call(bf16[1024,768]{1,0:T(8,128)(2,1)} %copy.28.refs_0_, ...), custom_call_target="tpu_custom_call" | custom-call | tf_op jit(solution)/shard_map/mixer_front/pallas_call | solution.py:903
  103.3 226.6 %ffn_both_ways.1 = (f32[1024,4608]{1,0:T(8,128)}, f32[9216,128]{1,0:T(8,128)}, f32[1024,1024]{1,0:T(8,128)}, f32[1024,1024]{1,0:T(8,128)}, f32[1024,1024]{1,0:T(...) custom-call(bf16[2048,1024]{1,0:T(8,128)(2,1)} %get-tuple-element.27.refs_0_, bf16[2048,1024]{1,0:T(8,128)(2,1)} %bitcast.46, ...), custom_call_target="tpu_custom_call" | custom-call | flops 43486543872 | bytes 838860800 | tf_op jit(solution)/shard_map/ffn_both_ways/pallas_call | solution.py:488
  329.9 190.3 %mixer_back.1 = (f32[1024,4608]{1,0:T(8,128)}, f32[2048,1024]{1,0:T(8,128)}, f32[2048,1024]{1,0:T(8,128)}, f32[1024,1024]{1,0:T(8,128)}, f32[4,6,256,128]{3,2,1,...) custom-call(f32[9216,128]{1,0:T(8,128)} %get-tuple-element.28.refs_0_, ...), custom_call_target="tpu_custom_call", output_to_operand_aliasing={{0}: (17, {})} | custom-call | flops 27917287424 | bytes 419430400 | tf_op jit(solution)/shard_map/mixer_back/pallas_call | solution.py:1373
  520.2 5.9 %multiply_convert_fusion = bf16[2048,1024]{1,0:T(8,128)(2,1)} fusion(f32[2048,1024]{1,0:T(8,128)} %get-tuple-element.41, f32[2048]{0:T(1024)} %bitcast.39), kind=kLoop, calls=%fused_computation | loop fusion | flops 4194304 | bytes 12591104 | tf_op jit(solution)/shard_map/convert_element_type | solution.py:1484
  526.1 0.8 slice_bitcast_fusion.1
  526.9 0.7 constant_dynamic-slice_fusion
  527.5 0.6 fusion
  528.2 1.3 slice.33
  529.4 0.5 reshape.112
  530.0 0.7 copy.31
  530.7 1.4 reshape.113
  532.1 2.1 slice.32
  534.2 10.6 %slice_bitcast_fusion = (f32[1152,1024]{0,1:T(8,128)}, f32[1024,1152]{1,0:T(8,128)}, f32[1024,1152]{1,0:T(8,128)}) fusion(f32[1024,4608]{1,0:T(8,128)} %get-tuple-element.43), kind=kLoop, calls=%fused_computation.1 | loop fusion | bytes 28311552 | tf_op jit(solution)/shard_map/transpose | solution.py:1490
  544.8 6.0 %copy.33 = f32[1152,1024]{1,0:T(8,128)} copy(f32[1152,1024]{0,1:T(8,128)} %get-tuple-element.64) | data formatting | bytes 9437184
  550.8 2.4 copy.30
  553.1 3.5 copy.32
  556.7 8.4 %copy.39 = f32[4,512,1024]{2,1,0:T(8,128)} copy(f32[4,512,1024]{2,1,0:T(8,128)} %bitcast.30) | data formatting | bytes 16777216
  (4 shorter events, 0.4 us)
Async XLA Ops:
  3.7 1.0 copy-start

commit v7 on v6

--- a/solution.py
+++ b/solution.py
@@ -76,6 +76,10 @@
         from_right = (self.place >= root) & (self.place < last)
         return left, right, from_left, from_right
 
+    def own_base(self, k):
+        held = self.own.shape[0] // (4 * HALF)
+        return pl.multiple_of(lax.rem(k, held) * 4 * HALF, 4 * HALF)
+
     def out_at(self, k, first, size):
         per_panel = self.out.shape[0] // (4 * HALF)
         panel = self.panel_of(k // per_panel)
@@ -88,7 +92,7 @@
         place, side = self.place, self.side
         own = self.own
         slot = lax.rem(k, SLOTS_IN_FLIGHT)
-        base = pl.multiple_of(k * 4 * HALF, 4 * HALF)
+        base = self.own_base(k)
         mine = pl.ds(pl.multiple_of(base + side * HALF, HALF), HALF)
         theirs = pl.ds(pl.multiple_of(base + (1 - side) * HALF, HALF), HALF)
         out_mine = self.out_at(k, side * HALF, HALF)
@@ -180,7 +184,7 @@
         place, side = self.place, self.side
         own = self.own
         slot = lax.rem(k, SLOTS_IN_FLIGHT)
-        base = pl.multiple_of(k * 4 * HALF, 4 * HALF)
+        base = self.own_base(k)
         wide = pl.ds(pl.multiple_of(base + 2 * HALF, 2 * HALF), 2 * HALF)
         out_wide = self.out_at(k, 2 * HALF, 2 * HALF)
         root = self.places // 2 - lax.rem(k, 2)
@@ -298,11 +302,12 @@
 
 
 SUB_ROWS = 64
-SUB_COLS = 256
-FFN_PIECES = 36
+FIRST_MIXER_TICK = 36
+BLOCK_TICK = 56
 FFN_PANELS = 27
 FFN_PARTS = 3
-ROW_BLOCK = 512
+ROW_BLOCK = 256
+ROW_TICK = 2
 OUT_BLOCK = 256
 
 
@@ -314,18 +319,37 @@
     return kind * (FFN_PANELS // 3) + panel // per_part * third + lax.rem(inside, third)
 
 
-def ffn_kernel(places, *refs):
-    (mid_hbm, cot_hbm, w_gate_hbm, w_up_hbm, w_d_hbm, valid) = refs[0:6]
-    (sums, rest, mid_chip, mid_far, ffn_chip, mid_land, ffn_land) = refs[6:13]
-    (mid, cot, w_gu, w_d, act, ggu, own, staged, fetched) = refs[13:22]
-    load_sems, near_sems, far_sems, keep_sem, fetch_sem = refs[22:27]
-    summer = SeqSum(places, own, sums, panel_in_sums, refs[27:])
+def norm_back(grad, gain, unit, scale):
+    scaled = gain * grad
+    return scale * (scaled - unit * jnp.mean(scaled * unit, axis=-1, keepdims=True))
+
+
+def back_kernel(places, slots, *refs):
+    (mid_hbm, cot_hbm, w_gate_hbm, w_up_hbm, w_d_hbm, hidden_hbm, proj_hbm) = refs[0:7]
+    (gated_hbm, normed_hbm, mixed_hbm, w_in_hbm, w_out_hbm, tokens_hbm) = refs[7:13]
+    (lengths, taps, gain_mix, gain_ffn) = refs[13:17]
+    (sums, tokens_out, block_out, mid_chip, mid_far, ffn_chip, ffn_far) = refs[17:24]
+    (mid_land, ffn_land, land_in, land_out, land_small) = refs[24:29]
+    (mid, cot, w_gu, w_d, act, ggu, own, staged, fetched) = refs[29:38]
+    (proj, gated, mixed_buf, conv_in, grad_hid, grad_tok) = refs[38:44]
+    (halo_out, halo_in, halo_keep, small, small_in) = refs[44:49]
+    load_sems, near_sems, far_sems, keep_sem, fetch_sem = refs[49:54]
+    (later_sems, row_sems, halo_sems, weight_sems, out_sems) = refs[54:59]
+
+    def panel_of(panel):
+        return jnp.where(panel < FFN_PANELS, panel_in_sums(panel), panel)
+
+    summer = SeqSum(places, own, sums, panel_of, refs[59:])
+    here = lax.axis_index("seq")
+    last = 2 * places - 1
     tp_at = lax.axis_index("tp")
     core = lax.rem(tp_at, 2)
     sibling = tp_at + 1 - 2 * core
     across = lax.rem(tp_at + 2, 4)
     rows, width = mid.shape
     parts, _, wide = w_gu.shape
+    half_rows = rows // 2
+    chans = wide // 3
     hidden = wide // 2
     panels = 3 * hidden // LANES
 
@@ -343,10 +367,29 @@
     ]
     for load in loads:
         load.start()
-    greet_seq(places, ({"tp": sibling}, {"tp": across}))
-    count = FFN_PIECES
+
+    barrier = pltpu.get_barrier_semaphore()
+
+    def signal(device):
+        pl.semaphore_signal(barrier, inc=1, device_id=device, device_id_type=pl.DeviceIdType.MESH)
+
+    pl.when(here > 0)(lambda: signal({"seq": here - 1}))
+    pl.when(here < last)(lambda: signal({"seq": here + 1}))
+    ends = jnp.where(here > 0, 1, 0) + jnp.where(here < last, 1, 0)
+    greet_seq(places, ({"tp": sibling}, {"tp": across}), ends)
+    ffn_pieces = own.shape[0] // (4 * HALF)
+    mixer_pieces = 4 * chans * width // LANES // (4 * HALF) + 1
+    count = ffn_pieces + mixer_pieces
     for load in loads:
         load.wait()
+
+    slot_len = rows // 2 // slots
+
+    def valid_rows(slot, first, size):
+        at = lax.broadcasted_iota(jnp.int32, (size, 1), 0) + (here * slot_len + first)
+        return (at < lengths[slot]).astype(jnp.float32)
+
+    part_ticks = rows // ROW_BLOCK // ROW_TICK + width // OUT_BLOCK
 
     def part_cols(c):
         return pl.ds(pl.multiple_of(c * hidden, LANES), hidden)
@@ -359,11 +402,13 @@
 
             @pl.when(c == 0)
             def _():
-                cot[at, :] = (valid[at, :] * cot[at, :].astype(jnp.float32)).astype(jnp.bfloat16)
+                per_slot = slot_len // ROW_BLOCK
+                mask = valid_rows(r // per_slot, lax.rem(r, per_slot) * ROW_BLOCK, ROW_BLOCK)
+                cot[at, :] = (mask * cot[at, :].astype(jnp.float32)).astype(jnp.bfloat16)
 
             both = jnp.dot(mid[at, :], w_gu[c], preferred_element_type=jnp.float32)
             gate, up = both[:, :hidden], both[:, hidden:]
-            grad_act = dot_cols(cot[at, :], w_d[c])
+            grad_act = dot_cols(cot[at, :], w_d[part_cols(c), :])
             sigmoid = 1.0 / (1.0 + jnp.exp(-gate))
             silu = gate * sigmoid
             act[at, part_cols(c)] = (silu * up).astype(jnp.bfloat16)
@@ -371,6 +416,10 @@
             ggu[c, at, :hidden] = (grad_act * up * slope).astype(jnp.bfloat16)
             ggu[c, at, hidden:] = (grad_act * silu).astype(jnp.bfloat16)
 
+            @pl.when((c > 0) & (lax.rem(r, ROW_TICK) == ROW_TICK - 1))
+            def _():
+                summer.tick((c - 1) * part_ticks + r // ROW_TICK, count)
+
         @pl.loop(0, width // OUT_BLOCK)
         def _(m):
             first = pl.multiple_of(m * OUT_BLOCK, OUT_BLOCK)
@@ -387,15 +436,10 @@
 
             @pl.when(c > 0)
             def _():
-                summer.tick((c - 1) * (width // OUT_BLOCK) + m, count)
-
-    early = (parts - 1) * (width // OUT_BLOCK)
+                summer.tick((c - 1) * part_ticks + rows // ROW_BLOCK // ROW_TICK + m, count)
+
+    early = (parts - 1) * part_ticks
     blocks = rows // 2 // OUT_BLOCK
-    for_later = pltpu.make_async_copy(
-        own.at[pl.ds(count * 4 * HALF, rest.shape[0])], rest, load_sems.at[0]
-    )
-    for_later.start()
-
     def row_block(half, k):
         return pl.ds(pl.multiple_of((half * blocks + k) * OUT_BLOCK, OUT_BLOCK), OUT_BLOCK)
 
@@ -406,7 +450,7 @@
         return sum(
             jnp.dot(
                 act[at, c * hidden : (c + 1) * hidden],
-                w_d[c],
+                w_d[c * hidden : (c + 1) * hidden, :],
                 preferred_element_type=jnp.float32,
             )
             for c in range(parts)
@@ -422,15 +466,18 @@
             device_id_type=pl.DeviceIdType.MESH,
         )
 
-    def far(k):
+    def far(which, chip, there, k):
         return pltpu.make_async_remote_copy(
-            src_ref=mid_chip.at[row_block(0, k)],
-            dst_ref=mid_far.at[row_block(0, k)],
-            send_sem=far_sems.at[0, k],
-            recv_sem=far_sems.at[1, k],
+            src_ref=chip.at[row_block(0, k)],
+            dst_ref=there.at[row_block(0, k)],
+            send_sem=far_sems.at[which, 0, k],
+            recv_sem=far_sems.at[which, 1, k],
             device_id={"tp": across},
             device_id_type=pl.DeviceIdType.MESH,
         )
+
+    def ffn_across(k):
+        return far(1, ffn_chip, ffn_far, k)
 
     def tp_sum(which, part, land, chip, first_tick):
         @pl.loop(0, blocks)
@@ -458,43 +505,410 @@
             summer.tick(first_tick + k, count)
             keep.wait()
             if which == 0:
-                far(k).start()
+                far(0, mid_chip, mid_far, k).start()
 
     tp_sum(0, mid_part, mid_land, mid_chip, early)
     tp_sum(1, ffn_part, ffn_land, ffn_chip, early + blocks)
 
-    @pl.loop(early + 2 * blocks, count + summer.P_LAGS[-1][1])
+    own_half = pl.ds(pl.multiple_of(core * half_rows, half_rows), half_rows)
+    low_half, high_half = pl.ds(0, half_rows), pl.ds(half_rows, half_rows)
+    w_out, grad_mixer = mid.at[low_half], mid.at[high_half]
+    normed, mixed = act.at[low_half, pl.ds(0, width)], act.at[high_half, pl.ds(0, width)]
+    tokens = w_d.at[low_half]
+    w_in = (ggu.at[2, low_half], ggu.at[2, high_half], w_gu.at[0], w_gu.at[1])
+    moves = [
+        (w_out_hbm, w_out),
+        (tokens_hbm.at[own_half], tokens),
+        (normed_hbm, normed),
+        (mixed_hbm, mixed),
+    ]
+    for j in range(4):
+        for g in range(3):
+            first = g * width + j * chans
+            moves.append(
+                (w_in_hbm.at[:, first : first + chans], w_in[j].at[:, g * chans : (g + 1) * chans])
+            )
+    loads = [
+        pltpu.make_async_copy(src, dst, later_sems.at[i]) for i, (src, dst) in enumerate(moves)
+    ]
+    for load in loads:
+        load.start()
+    chip, far_rows, hidden_rows = staged.at[0], staged.at[1], fetched
+    per_slot = slot_len // OUT_BLOCK
+    small[...] = jnp.zeros_like(small)
+    ticked = early + 2 * blocks
+
+    @pl.loop(ticked, FIRST_MIXER_TICK)
     def _(t):
         summer.tick(t, count)
 
-    for_later.wait()
-
     @pl.loop(0, blocks)
     def _(k):
-        far(k).wait()
-
-
-def ffn_both_ways(normed_mid, cotangent, w_gate, w_up, w_down, valid, sum_cols, collective_id):
+        far(0, mid_chip, mid_far, k).wait()
+        ffn_across(k).start()
+
+    for load in loads:
+        load.wait()
+
+    def shard_rows(shard, first, size):
+        at = lax.rem(shard, 2) * half_rows + first
+        return shard // 2, pl.ds(pl.multiple_of(at, size), size)
+
+    def place_of(n):
+        slot = n // per_slot
+        block = per_slot - 1 - lax.rem(n, per_slot)
+        return slot, block, pl.multiple_of(slot * slot_len + block * OUT_BLOCK, OUT_BLOCK)
+
+    def mid_loads(first):
+        at = pl.ds(first, OUT_BLOCK)
+        return [
+            pltpu.make_async_copy(src.at[at], dst, row_sems.at[i])
+            for i, (src, dst) in enumerate(((mid_chip, chip), (mid_far, far_rows), (hidden_hbm, hidden_rows)))
+        ]
+
+    def proj_loads(slot, block, first):
+        return [
+            pltpu.make_async_copy(proj_hbm.at[pl.ds(first, OUT_BLOCK)], proj, row_sems.at[3]),
+            pltpu.make_async_copy(
+                gated_hbm.at[slot, pl.ds(pl.multiple_of(block * OUT_BLOCK, 8), OUT_BLOCK + 8)],
+                gated,
+                row_sems.at[4],
+            ),
+        ]
+
+    def start(copies):
+        for copy in copies:
+            copy.start()
+
+    def wait(copies):
+        for copy in copies:
+            copy.wait()
+
+    def remote(src, dst, sems, i, device):
+        return pltpu.make_async_remote_copy(
+            src_ref=src,
+            dst_ref=dst,
+            send_sem=sems.at[0, i],
+            recv_sem=sems.at[1, i],
+            device_id=device,
+            device_id_type=pl.DeviceIdType.MESH,
+        )
+
+    def block_at(k):
+        return pl.ds(pl.multiple_of(k * OUT_BLOCK, OUT_BLOCK), OUT_BLOCK)
+
+    def own_rows(first, size):
+        return pl.ds(pl.multiple_of(core * half_rows + first, size), size)
+
+    def hidden_grad(chip_part, far_part, hidden_part, cot_part):
+        grad_mid = chip_part + far_part
+        scale = rms_scale(hidden_part)
+        unit = hidden_part * scale
+        grad = cot_part.astype(jnp.float32) + norm_back(grad_mid, gain_ffn[...], unit, scale)
+        return grad, grad_mid * unit
+
+    def halo_copy(slot, device):
+        return remote(halo_out.at[slot], halo_in.at[slot], halo_sems, slot, {"seq": device})
+
+    head = 16
+    for slot in range(slots):
+        at = pl.ds(slot * slot_len, head)
+        top = pl.ds(0, head)
+        copies = [
+            pltpu.make_async_copy(src.at[at], dst, row_sems.at[i])
+            for i, (src, dst) in enumerate(
+                (
+                    (mid_chip, chip.at[top]),
+                    (mid_far, far_rows.at[top]),
+                    (hidden_hbm, hidden_rows.at[top]),
+                    (proj_hbm, proj.at[top]),
+                )
+            )
+        ]
+        start(copies)
+        wait(copies)
+        grad, _ = hidden_grad(
+            chip[top, :], far_rows[top, :], hidden_rows[top, :], cot[own_rows(slot * slot_len, head), :]
+        )
+        grad_mixed = dot_cols(grad.astype(jnp.bfloat16), w_out[...])
+        halo_out[slot] = (grad_mixed * proj[top, width : 2 * width])[:8]
+        pl.when(here > 0)(lambda slot=slot: halo_copy(slot, here - 1).start())
+
+    slot, block, first = place_of(0)
+    start(mid_loads(first))
+    start(proj_loads(slot, block, first))
+
+    @pl.when(here == last)
+    def _():
+        halo_in[...] = jnp.zeros_like(halo_in)
+
+    @pl.when(here < last)
+    def _():
+        for slot in range(slots):
+            halo_copy(slot, here + 1).wait_recv()
+
+    def out_rows(first):
+        return own_rows(first, OUT_BLOCK)
+
+    def hand_out(target, first, i):
+        at = out_rows(first)
+        return (
+            pltpu.make_async_copy(grad_tok, target.at[at], out_sems.at[0, 2 * blocks]),
+            remote(grad_tok, target.at[at], out_sems, i, {"tp": sibling}),
+        )
+
+    @pl.loop(0, blocks)
+    def _(n):
+        slot, block, first = place_of(n)
+        at = pl.ds(first, OUT_BLOCK)
+        wait(mid_loads(first))
+
+        @pl.loop(0, OUT_BLOCK // SUB_ROWS)
+        def _(r):
+            sub = pl.ds(pl.multiple_of(r * SUB_ROWS, SUB_ROWS), SUB_ROWS)
+            whole = pl.ds(pl.multiple_of(first + r * SUB_ROWS, SUB_ROWS), SUB_ROWS)
+            grad, for_gain = hidden_grad(
+                chip[sub, :],
+                far_rows[sub, :],
+                hidden_rows[sub, :],
+                cot[own_rows(first + r * SUB_ROWS, SUB_ROWS), :],
+            )
+            grad_hid[sub, :] = grad
+            grad_mixer[whole, :] = grad.astype(jnp.bfloat16)
+            small[1:2, :] += jnp.sum(for_gain, axis=0, keepdims=True)
+
+        @pl.when(n < blocks - 1)
+        def _():
+            start(mid_loads(place_of(n + 1)[2]))
+
+        mixed_buf[...] = dot_cols(grad_mixer[at, :], w_out[...])
+        wait(proj_loads(slot, block, first))
+
+        @pl.when(block == per_slot - 1)
+        def _():
+            conv_in[pl.ds(OUT_BLOCK, 8), :] = halo_in[slot]
+
+        @pl.when(block < per_slot - 1)
+        def _():
+            conv_in[pl.ds(OUT_BLOCK, 8), :] = halo_keep[...]
+
+        summer.tick(FIRST_MIXER_TICK + 2 * n, count)
+        mask = valid_rows(core * slots + slot, block * OUT_BLOCK, OUT_BLOCK)
+
+        @pl.loop(0, width // chans)
+        def _(c):
+            def cols(gate):
+                return pl.ds(pl.multiple_of(gate * width + c * chans, chans), chans)
+
+            here_cols = cols(0)
+            pair, shard_at = shard_rows(c, first, OUT_BLOCK)
+            in_gate, out_gate, conv_value = (proj[:, cols(g)] for g in range(3))
+            grad_mixed = mixed_buf[:, here_cols]
+            now = grad_mixed * out_gate
+            conv_in[pl.ds(0, OUT_BLOCK), here_cols] = now
+            seen = [gated[pl.ds(6 + j, OUT_BLOCK), here_cols] for j in range(3)]
+            tap = [taps[j : j + 1, here_cols] for j in range(3)]
+            conv_sum = tap[0] * seen[0] + tap[1] * seen[1] + tap[2] * seen[2]
+            for j in range(3):
+                small[2 + j : 3 + j, here_cols] += jnp.sum(now * seen[j], axis=0, keepdims=True)
+            ggu[pair, shard_at, chans : 2 * chans] = (grad_mixed * conv_sum).astype(jnp.bfloat16)
+            grad_gated = mask * (
+                tap[2] * now
+                + tap[1] * conv_in[pl.ds(1, OUT_BLOCK), here_cols]
+                + tap[0] * conv_in[pl.ds(2, OUT_BLOCK), here_cols]
+            )
+            ggu[pair, shard_at, :chans] = (grad_gated * conv_value).astype(jnp.bfloat16)
+            ggu[pair, shard_at, 2 * chans : 3 * chans] = (grad_gated * in_gate).astype(jnp.bfloat16)
+
+        halo_keep[...] = conv_in[pl.ds(0, 8), :]
+
+        @pl.when(n < blocks - 1)
+        def _():
+            start(proj_loads(*place_of(n + 1)))
+
+        def shard_grad(j):
+            pair, shard_at = shard_rows(j, first, OUT_BLOCK)
+            return dot_cols(ggu[pair, shard_at, :], w_in[j][...])
+
+        mixed_buf[...] = sum(shard_grad(j) for j in range(4))
+
+        @pl.when(n > 0)
+        def _():
+            local, there = hand_out(tokens_out, place_of(n - 1)[2], n - 1)
+            local.wait()
+            there.wait_send()
+
+        @pl.loop(0, OUT_BLOCK // SUB_ROWS)
+        def _(r):
+            sub = pl.ds(pl.multiple_of(r * SUB_ROWS, SUB_ROWS), SUB_ROWS)
+            whole = pl.ds(pl.multiple_of(first + r * SUB_ROWS, SUB_ROWS), SUB_ROWS)
+            inputs = tokens[whole, :].astype(jnp.float32)
+            scale = rms_scale(inputs)
+            unit = inputs * scale
+            grad_in = mixed_buf[sub, :]
+            grad_tok[sub, :] = grad_hid[sub, :] + norm_back(grad_in, gain_mix[...], unit, scale)
+            small[0:1, :] += jnp.sum(grad_in * unit, axis=0, keepdims=True)
+
+        start(hand_out(tokens_out, first, n))
+        summer.tick(FIRST_MIXER_TICK + 2 * n + 1, count)
+
+    in_blocks = width // OUT_BLOCK
+    stages = [proj.at[:, i * wide : (i + 1) * wide] for i in range(3)]
+
+    def to_near(src, dst, i):
+        return remote(src, dst, weight_sems, i, {"tp": sibling})
+
+    def near_in(m):
+        cols = pl.ds(pl.multiple_of(lax.rem(m, 2) * wide, LANES), wide)
+        return to_near(proj.at[:, cols], land_in.at[m], m)
+
+    near_out = to_near(grad_hid, land_out, in_blocks)
+    near_small = to_near(small, land_small, in_blocks + 1)
+
+    def in_part(m, shard):
+        pair, shard_at = shard_rows(shard, 0, half_rows)
+        return dot_rows(normed[:, block_at(m)], ggu[pair, shard_at, :])
+
+    def out_part(shard):
+        at = pl.ds(pl.multiple_of(shard * chans, LANES), chans)
+        return dot_rows(mixed[:, at], grad_mixer[...])
+
+    near_small.start()
+    first_tick = FIRST_MIXER_TICK + 2 * blocks
+
+    @pl.loop(0, in_blocks)
+    def _(m):
+        @pl.when(m >= 2)
+        def _():
+            near_in(m - 2).wait_send()
+
+        cols = pl.ds(pl.multiple_of(lax.rem(m, 2) * wide, LANES), wide)
+        proj[:, cols] = in_part(m, sibling)
+        near_in(m).start()
+        summer.tick(first_tick + m, count)
+
+    grad_hid[...] = out_part(sibling)
+    near_out.start()
+
+    @pl.loop(0, in_blocks)
+    def _(m):
+        near_in(m).wait_recv()
+        fetch = pltpu.make_async_copy(land_in.at[m], stages[2], row_sems.at[0])
+        fetch.start()
+        part = in_part(m, tp_at)
+        fetch.wait()
+        for i in range(wide // LANES):
+            to = pl.multiple_of(i * width + m * OUT_BLOCK, OUT_BLOCK)
+            own[pl.ds(to, OUT_BLOCK), :] = (
+                part[:, i * LANES : (i + 1) * LANES]
+                + proj[:, 2 * wide + i * LANES : 2 * wide + (i + 1) * LANES]
+            )
+
+        summer.tick(first_tick + in_blocks + m, count)
+
+    near_out.wait_recv()
+    near_small.wait_recv()
+    fetches = [
+        pltpu.make_async_copy(land_out, mixed_buf, row_sems.at[0]),
+        pltpu.make_async_copy(land_small, small_in, row_sems.at[1]),
+    ]
+    start(fetches)
+    part = out_part(tp_at)
+    wait(fetches)
+    out_first = wide // LANES * width
+    small_first = out_first + width // LANES * chans
+    for p in range(width // LANES):
+        cols = slice(p * LANES, (p + 1) * LANES)
+        own[pl.ds(out_first + p * chans, chans), :] = part[:, cols] + mixed_buf[:, cols]
+        own[pl.ds(small_first + 8 * p, 8), :] = small[:, cols] + small_in[:, cols]
+    unused = 4 * HALF - 8 * (width // LANES)
+    own[pl.ds(small_first + 4 * HALF - unused, unused), :] = jnp.zeros((unused, LANES), jnp.float32)
+
+    local, there = hand_out(tokens_out, place_of(blocks - 1)[2], blocks - 1)
+    local.wait()
+    there.wait_send()
+    done = first_tick + 2 * in_blocks
+    pause = BLOCK_TICK
+
+    @pl.loop(done, pause)
+    def _(t):
+        summer.tick(t, count)
+
+    @pl.loop(0, blocks)
+    def _(k):
+        ffn_across(k).wait_recv()
+        at = block_at(k)
+        copies = [
+            pltpu.make_async_copy(src.at[at], dst, row_sems.at[i])
+            for i, (src, dst) in enumerate(((ffn_chip, chip), (ffn_far, far_rows), (hidden_hbm, hidden_rows)))
+        ]
+        start(copies)
+
+        @pl.when(k > 0)
+        def _():
+            local, there = hand_out(block_out, (k - 1) * OUT_BLOCK, blocks + k - 1)
+            local.wait()
+            there.wait_send()
+
+        wait(copies)
+        grad_tok[...] = hidden_rows[...] + (chip[...] + far_rows[...])
+        start(hand_out(block_out, k * OUT_BLOCK, blocks + k))
+        summer.tick(pause + k, count)
+
+    @pl.loop(pause + blocks, count + summer.P_LAGS[-1][1])
+    def _(t):
+        summer.tick(t, count)
+
+    local, there = hand_out(block_out, (blocks - 1) * OUT_BLOCK, 2 * blocks - 1)
+    local.wait()
+    there.wait_send()
+
+    @pl.loop(0, blocks)
+    def _(k):
+        ffn_across(k).wait_send()
+        hand_out(tokens_out, place_of(k)[2], k)[1].wait_recv()
+        hand_out(block_out, k * OUT_BLOCK, blocks + k)[1].wait_recv()
+
+    for m in range(max(in_blocks - 2, 0), in_blocks):
+        near_in(m).wait_send()
+    near_out.wait_send()
+    near_small.wait_send()
+
+    @pl.when(here > 0)
+    def _():
+        for slot in range(slots):
+            halo_copy(slot, here - 1).wait_send()
+
+
+def back_both(hbm, vmem, slots, sum_cols, collective_id):
+    normed_mid, _, w_gate, _, w_d, _, _, gated, _, _, _, _, _ = hbm
     rows, width = normed_mid.shape
+    half_rows = rows // 2
     local = w_gate.shape[1]
     hidden = local // FFN_PARTS
-
-    w_d = w_down.reshape(FFN_PARTS, hidden, width)
-    grad_rows = 3 * local * width // LANES
-    summed = FFN_PIECES * 4 * HALF
-    half = jax.ShapeDtypeStruct((rows // 2, width), jnp.float32)
-    low = jnp.bfloat16
-    blocks = rows // 2 // OUT_BLOCK
+    chans = 2 * hidden // 3
+    blocks = half_rows // OUT_BLOCK
+    in_blocks = width // OUT_BLOCK
+    f32, low = jnp.float32, jnp.bfloat16
+    half = jax.ShapeDtypeStruct((half_rows, width), f32)
+    full = jax.ShapeDtypeStruct((rows, width), f32)
+    block = pltpu.VMEM((OUT_BLOCK, width), f32)
+    row8 = pltpu.VMEM((8, width), f32)
+    anywhere = pl.BlockSpec(memory_space=pl.ANY)
     return pl.pallas_call(
-        functools.partial(ffn_kernel, lax.axis_size("seq") // 2),
-        out_shape=[
-            jax.ShapeDtypeStruct((width, sum_cols), jnp.float32),
-            jax.ShapeDtypeStruct((grad_rows - summed, LANES), jnp.float32),
-        ]
-        + [half] * 5,
-        in_specs=[pl.BlockSpec(memory_space=pl.ANY)] * 5
-        + [pl.BlockSpec(memory_space=pltpu.VMEM)],
-        out_specs=[pl.BlockSpec(memory_space=pl.ANY)] * 7,
+        functools.partial(back_kernel, lax.axis_size("seq") // 2, slots),
+        out_shape=[jax.ShapeDtypeStruct((width, sum_cols), f32)]
+        + [full] * 2
+        + [half] * 6
+        + [
+            jax.ShapeDtypeStruct((in_blocks, OUT_BLOCK, 2 * hidden), f32),
+            jax.ShapeDtypeStruct((chans, width), f32),
+            jax.ShapeDtypeStruct((8, width), f32),
+        ],
+        in_specs=[anywhere] * len(hbm)
+        + [pl.BlockSpec(memory_space=pltpu.SMEM)]
+        + [pl.BlockSpec(memory_space=pltpu.VMEM)] * (len(vmem) - 1),
+        out_specs=[anywhere] * 12,
         scratch_shapes=[
             pltpu.VMEM((rows, width), low),
             pltpu.VMEM((rows, width), low),
@@ -502,14 +916,30 @@
             pltpu.VMEM(w_d.shape, low),
             pltpu.VMEM((rows, local), low),
             pltpu.VMEM((FFN_PARTS, rows, 2 * hidden), low),
-            pltpu.VMEM((grad_rows, LANES), jnp.float32),
-            pltpu.VMEM((2, OUT_BLOCK, width), jnp.float32),
-            pltpu.VMEM((OUT_BLOCK, width), jnp.float32),
+            pltpu.VMEM((3 * local * width // LANES, LANES), f32),
+            pltpu.VMEM((2, OUT_BLOCK, width), f32),
+            block,
+            pltpu.VMEM((OUT_BLOCK, 3 * width), f32),
+            pltpu.VMEM((OUT_BLOCK + 8, width), f32),
+            block,
+            pltpu.VMEM((OUT_BLOCK + 8, width), f32),
+            block,
+            block,
+            pltpu.VMEM((slots, 8, width), f32),
+            pltpu.VMEM((slots, 8, width), f32),
+            row8,
+            row8,
+            row8,
             pltpu.SemaphoreType.DMA((3 + 2 * FFN_PARTS,)),
             pltpu.SemaphoreType.DMA((2, 2, blocks)),
-            pltpu.SemaphoreType.DMA((2, blocks)),
+            pltpu.SemaphoreType.DMA((2, 2, blocks)),
             pltpu.SemaphoreType.DMA,
             pltpu.SemaphoreType.DMA,
+            pltpu.SemaphoreType.DMA((16,)),
+            pltpu.SemaphoreType.DMA((5,)),
+            pltpu.SemaphoreType.DMA((2, slots)),
+            pltpu.SemaphoreType.DMA((2, in_blocks + 2)),
+            pltpu.SemaphoreType.DMA((2, 2 * blocks + 1)),
         ]
         + seq_sum_scratch(),
         compiler_params=pltpu.CompilerParams(
@@ -518,8 +948,8 @@
         cost_estimate=pl.CostEstimate(
             flops=18 * rows * width * local, bytes_accessed=800 << 20, transcendentals=0
         ),
-        name="ffn_both_ways",
-    )(normed_mid, cotangent, w_gate, w_up, w_d, valid)
+        name="back_both",
+    )(*hbm, *vmem)
 
 
 def front_kernel(places, slots, *refs):
@@ -955,484 +1385,6 @@
     )
 
 
-def norm_back(grad, gain, unit, scale):
-    scaled = gain * grad
-    return scale * (scaled - unit * jnp.mean(scaled * unit, axis=-1, keepdims=True))
-
-
-def mixer_kernel(places, *refs):
-    (rest_hbm, mid_chip, mid_far, ffn_chip, hidden_hbm, proj_hbm, gated_hbm) = refs[0:7]
-    (normed_hbm, mixed_hbm, w_in_hbm, w_out_hbm, cot_hbm, tokens_hbm) = refs[7:13]
-    (valid, taps, gain_mix, gain_ffn) = refs[13:17]
-    (sums, tokens_out, block_out, ffn_far, land_in, land_out, land_small) = refs[18:25]
-    (own, normed, mixed, w_in, w_out, cot, tokens, grad_mixer, grad_proj) = refs[25:34]
-    (chip, far, hidden, proj, gated, mixed_buf, conv_in, grad_hid, grad_tok) = refs[34:43]
-    (halo_out, halo_in, halo_keep, small, small_stage, small_fetch) = refs[43:49]
-    (stage_in, fetch_in, stage_out, fetch_out) = refs[49:53]
-    (load_sems, row_sems, halo_sems, near_sems, far_sems, out_sems) = refs[53:59]
-    first_panel = FFN_PIECES * 4 * HALF // LANES // 8
-
-    def panel_of(panel):
-        panel = first_panel + panel
-        return jnp.where(panel < FFN_PANELS, panel_in_sums(panel), panel)
-
-    summer = SeqSum(places, own, sums, panel_of, refs[59:])
-    here = lax.axis_index("seq")
-    last = 2 * places - 1
-    tp_at = lax.axis_index("tp")
-    core = lax.rem(tp_at, 2)
-    sibling = tp_at + 1 - 2 * core
-    across = lax.rem(tp_at + 2, 4)
-    rows, width = tokens.shape
-    slots = halo_in.shape[0]
-    slot_len = rows // slots
-    per_slot = slot_len // OUT_BLOCK
-    blocks = rows // OUT_BLOCK
-    chans = w_out.shape[0] // 4
-    count = own.shape[0] // (4 * HALF)
-    early_rows = rest_hbm.shape[0]
-    own_half = pl.ds(pl.multiple_of(core * rows, rows), rows)
-
-    loads = [
-        pltpu.make_async_copy(src, dst, load_sems.at[i])
-        for i, (src, dst) in enumerate(
-            (
-                (rest_hbm, own.at[pl.ds(0, early_rows)]),
-                (cot_hbm.at[own_half], cot),
-                (w_out_hbm, w_out),
-                (tokens_hbm.at[own_half], tokens),
-                (w_in_hbm, w_in),
-                (normed_hbm, normed),
-                (mixed_hbm, mixed),
-            )
-        )
-    ]
-    for load in loads:
-        load.start()
-
-    def place_of(n):
-        slot = n // per_slot
-        block = per_slot - 1 - lax.rem(n, per_slot)
-        return slot, block, pl.multiple_of(slot * slot_len + block * OUT_BLOCK, OUT_BLOCK)
-
-    def mid_loads(first):
-        at = pl.ds(first, OUT_BLOCK)
-        return [
-            pltpu.make_async_copy(src.at[at], dst, row_sems.at[i])
-            for i, (src, dst) in enumerate(((mid_chip, chip), (mid_far, far), (hidden_hbm, hidden)))
-        ]
-
-    def proj_loads(slot, block, first):
-        return [
-            pltpu.make_async_copy(proj_hbm.at[pl.ds(first, OUT_BLOCK)], proj, row_sems.at[3]),
-            pltpu.make_async_copy(
-                gated_hbm.at[slot, pl.ds(pl.multiple_of(block * OUT_BLOCK, 8), OUT_BLOCK + 8)],
-                gated,
-                row_sems.at[4],
-            ),
-        ]
-
-    def start(copies):
-        for copy in copies:
-            copy.start()
-
-    def wait(copies):
-        for copy in copies:
-            copy.wait()
-
-    def remote(src, dst, sems, i, device):
-        return pltpu.make_async_remote_copy(
-            src_ref=src,
-            dst_ref=dst,
-            send_sem=sems.at[0, i],
-            recv_sem=sems.at[1, i],
-            device_id=device,
-            device_id_type=pl.DeviceIdType.MESH,
-        )
-
-    barrier = pltpu.get_barrier_semaphore()
-
-    def signal(device):
-        pl.semaphore_signal(barrier, inc=1, device_id=device, device_id_type=pl.DeviceIdType.MESH)
-
-    pl.when(here > 0)(lambda: signal({"seq": here - 1}))
-    pl.when(here < last)(lambda: signal({"seq": here + 1}))
-    ends = jnp.where(here > 0, 1, 0) + jnp.where(here < last, 1, 0)
-    greet_seq(places, ({"tp": sibling}, {"tp": across}), ends)
-
-    def block_at(k):
-        return pl.ds(pl.multiple_of(k * OUT_BLOCK, OUT_BLOCK), OUT_BLOCK)
-
-    def ffn_across(k):
-        at = block_at(k)
-        return remote(ffn_chip.at[at], ffn_far.at[at], far_sems, k, {"tp": across})
-
-    @pl.loop(0, blocks)
-    def _(k):
-        ffn_across(k).start()
-
-    small[...] = jnp.zeros_like(small)
-    wait(loads[:3])
-
-    def hidden_grad(chip_rows, far_rows, hidden_rows, cot_rows, mask):
-        grad_mid = chip_rows + far_rows
-        scale = rms_scale(hidden_rows)
-        unit = hidden_rows * scale
-        grad = mask * cot_rows.astype(jnp.float32) + norm_back(grad_mid, gain_ffn[...], unit, scale)
-        return grad, grad_mid * unit
-
-    def halo_copy(slot, device):
-        return remote(halo_out.at[slot], halo_in.at[slot], halo_sems, slot, {"seq": device})
-
-    head = 16
-    for slot in range(slots):
-        at = pl.ds(slot * slot_len, head)
-        top = pl.ds(0, head)
-        copies = [
-            pltpu.make_async_copy(src.at[at], dst, row_sems.at[i])
-            for i, (src, dst) in enumerate(
-                (
-                    (mid_chip, chip.at[top]),
-                    (mid_far, far.at[top]),
-                    (hidden_hbm, hidden.at[top]),
-                    (proj_hbm, proj.at[top]),
-                )
-            )
-        ]
-        start(copies)
-        wait(copies)
-        grad, _ = hidden_grad(
-            chip[top, :], far[top, :], hidden[top, :], cot[at, :], valid[at, :]
-        )
-        grad_mixed = dot_cols(grad.astype(jnp.bfloat16), w_out[...])
-        halo_out[slot] = (grad_mixed * proj[top, width : 2 * width])[:8]
-        pl.when(here > 0)(lambda slot=slot: halo_copy(slot, here - 1).start())
-
-    slot, block, first = place_of(0)
-    start(mid_loads(first))
-    start(proj_loads(slot, block, first))
-
-    @pl.when(here == last)
-    def _():
-        halo_in[...] = jnp.zeros_like(halo_in)
-
-    @pl.when(here < last)
-    def _():
-        for slot in range(slots):
-            halo_copy(slot, here + 1).wait_recv()
-
-    wait(loads[3:])
-
-    def out_rows(first):
-        return pl.ds(pl.multiple_of(core * rows + first, OUT_BLOCK), OUT_BLOCK)
-
-    def hand_out(target, first, i):
-        at = out_rows(first)
-        return (
-            pltpu.make_async_copy(grad_tok, target.at[at], out_sems.at[0, 2 * blocks]),
-            remote(grad_tok, target.at[at], out_sems, i, {"tp": sibling}),
-        )
-
-    @pl.loop(0, blocks)
-    def _(n):
-        slot, block, first = place_of(n)
-        at = pl.ds(first, OUT_BLOCK)
-        wait(mid_loads(first))
-
-        @pl.loop(0, OUT_BLOCK // SUB_ROWS)
-        def _(r):
-            sub = pl.ds(pl.multiple_of(r * SUB_ROWS, SUB_ROWS), SUB_ROWS)
-            whole = pl.ds(pl.multiple_of(first + r * SUB_ROWS, SUB_ROWS), SUB_ROWS)
-            grad, for_gain = hidden_grad(
-                chip[sub, :], far[sub, :], hidden[sub, :], cot[whole, :], valid[whole, :]
-            )
-            grad_hid[sub, :] = grad
-            grad_mixer[whole, :] = grad.astype(jnp.bfloat16)
-            small[1:2, :] += jnp.sum(for_gain, axis=0, keepdims=True)
-
-        @pl.when(n < blocks - 1)
-        def _():
-            start(mid_loads(place_of(n + 1)[2]))
-
-        mixed_buf[...] = dot_cols(grad_mixer[at, :], w_out[...])
-        wait(proj_loads(slot, block, first))
-
-        @pl.when(block == per_slot - 1)
-        def _():
-            conv_in[pl.ds(OUT_BLOCK, 8), :] = halo_in[slot]
-
-        @pl.when(block < per_slot - 1)
-        def _():
-            conv_in[pl.ds(OUT_BLOCK, 8), :] = halo_keep[...]
-
-        summer.tick(2 * n, count)
-        mask = valid[at, :]
-
-        @pl.loop(0, width // SUB_COLS)
-        def _(c):
-            def cols(gate):
-                return pl.ds(pl.multiple_of(gate * width + c * SUB_COLS, SUB_COLS), SUB_COLS)
-
-            here_cols = cols(0)
-            in_gate, out_gate, conv_value = (proj[:, cols(g)] for g in range(3))
-            grad_mixed = mixed_buf[:, here_cols]
-            now = grad_mixed * out_gate
-            conv_in[pl.ds(0, OUT_BLOCK), here_cols] = now
-            seen = [gated[pl.ds(6 + j, OUT_BLOCK), here_cols] for j in range(3)]
-            tap = [taps[j : j + 1, here_cols] for j in range(3)]
-            conv_sum = tap[0] * seen[0] + tap[1] * seen[1] + tap[2] * seen[2]
-            for j in range(3):
-                small[2 + j : 3 + j, here_cols] += jnp.sum(now * seen[j], axis=0, keepdims=True)
-            grad_proj[at, cols(1)] = (grad_mixed * conv_sum).astype(jnp.bfloat16)
-            grad_gated = mask * (
-                tap[2] * now
-                + tap[1] * conv_in[pl.ds(1, OUT_BLOCK), here_cols]
-                + tap[0] * conv_in[pl.ds(2, OUT_BLOCK), here_cols]
-            )
-            grad_proj[at, cols(0)] = (grad_gated * conv_value).astype(jnp.bfloat16)
-            grad_proj[at, cols(2)] = (grad_gated * in_gate).astype(jnp.bfloat16)
-
-        halo_keep[...] = conv_in[pl.ds(0, 8), :]
-
-        @pl.when(n < blocks - 1)
-        def _():
-            start(proj_loads(*place_of(n + 1)))
-
-        mixed_buf[...] = dot_cols(grad_proj[at, :], w_in[...])
-
-        @pl.when(n > 0)
-        def _():
-            local, there = hand_out(tokens_out, place_of(n - 1)[2], n - 1)
-            local.wait()
-            there.wait_send()
-
-        @pl.loop(0, OUT_BLOCK // SUB_ROWS)
-        def _(r):
-            sub = pl.ds(pl.multiple_of(r * SUB_ROWS, SUB_ROWS), SUB_ROWS)
-            whole = pl.ds(pl.multiple_of(first + r * SUB_ROWS, SUB_ROWS), SUB_ROWS)
-            inputs = tokens[whole, :].astype(jnp.float32)
-            scale = rms_scale(inputs)
-            unit = inputs * scale
-            grad_in = mixed_buf[sub, :]
-            grad_tok[sub, :] = grad_hid[sub, :] + norm_back(grad_in, gain_mix[...], unit, scale)
-            small[0:1, :] += jnp.sum(grad_in * unit, axis=0, keepdims=True)
-
-        start(hand_out(tokens_out, first, n))
-        summer.tick(2 * n + 1, count)
-
-    def near(src, dst, i):
-        return remote(src, dst, near_sems, i, {"tp": sibling})
-
-    in_blocks = width // OUT_BLOCK
-    panels_in = 3 * chans // LANES
-
-    def near_in(m):
-        return near(stage_in.at[lax.rem(m, 2)], land_in.at[m], m)
-
-    near_out = near(stage_out, land_out, in_blocks)
-    near_small = near(small_stage, land_small, in_blocks + 1)
-
-    def in_part(m, g, shard):
-        at = pl.ds(pl.multiple_of(m * OUT_BLOCK, OUT_BLOCK), OUT_BLOCK)
-        cols = pl.ds(pl.multiple_of(g * width + shard * chans, LANES), chans)
-        return dot_rows(normed[:, at], grad_proj[:, cols])
-
-    def out_part(shard):
-        at = pl.ds(pl.multiple_of(shard * chans, LANES), chans)
-        return dot_rows(mixed[:, at], grad_mixer[...])
-
-    for p in range(width // LANES):
-        small_stage[8 * p : 8 * p + 8, :] = small[:, p * LANES : (p + 1) * LANES]
-    near_small.start()
-    halves = chans // LANES
-
-    @pl.loop(0, in_blocks)
-    def _(m):
-        @pl.when(m >= 2)
-        def _():
-            near_in(m - 2).wait_send()
-
-        for g in range(3):
-            part = in_part(m, g, sibling)
-            for h in range(halves):
-                stage_in[lax.rem(m, 2), g * halves + h] = part[:, h * LANES : (h + 1) * LANES]
-        near_in(m).start()
-        summer.tick(2 * blocks + m, count)
-
-    part = out_part(sibling)
-    for p in range(width // LANES):
-        stage_out[p] = part[:, p * LANES : (p + 1) * LANES]
-    near_out.start()
-
-    @pl.loop(0, in_blocks)
-    def _(m):
-        near_in(m).wait_recv()
-        fetch = pltpu.make_async_copy(land_in.at[m], fetch_in, row_sems.at[0])
-        fetch.start()
-        parts = [in_part(m, g, tp_at) for g in range(3)]
-        fetch.wait()
-        for g in range(3):
-            for h in range(halves):
-                i = g * halves + h
-                to = pl.multiple_of(early_rows + i * width + m * OUT_BLOCK, OUT_BLOCK)
-                own[pl.ds(to, OUT_BLOCK), :] = (
-                    parts[g][:, h * LANES : (h + 1) * LANES] + fetch_in[i]
-                )
-
-        summer.tick(2 * blocks + in_blocks + m, count)
-
-    near_out.wait_recv()
-    near_small.wait_recv()
-    fetches = [
-        pltpu.make_async_copy(land_out, fetch_out, row_sems.at[0]),
-        pltpu.make_async_copy(land_small, small_fetch, row_sems.at[1]),
-    ]
-    start(fetches)
-    part = out_part(tp_at)
-    wait(fetches)
-    out_first = early_rows + panels_in * width
-    for p in range(width // LANES):
-        own[pl.ds(out_first + p * chans, chans), :] = (
-            part[:, p * LANES : (p + 1) * LANES] + fetch_out[p]
-        )
-    small_first = out_first + width // LANES * chans
-    small_rows = small_stage.shape[0]
-    own[pl.ds(small_first, small_rows), :] = small_stage[...] + small_fetch[...]
-    unused = own.shape[0] - small_first - small_rows
-    own[pl.ds(small_first + small_rows, unused), :] = jnp.zeros((unused, LANES), jnp.float32)
-
-    local, there = hand_out(tokens_out, place_of(blocks - 1)[2], blocks - 1)
-    local.wait()
-    there.wait_send()
-    done = 2 * blocks + 2 * in_blocks
-    pause = min(done + 10, count)
-
-    @pl.loop(done, pause)
-    def _(t):
-        summer.tick(t, count)
-
-    @pl.loop(0, blocks)
-    def _(k):
-        ffn_across(k).wait_recv()
-        at = block_at(k)
-        copies = [
-            pltpu.make_async_copy(src.at[at], dst, row_sems.at[i])
-            for i, (src, dst) in enumerate(((ffn_chip, chip), (ffn_far, far), (hidden_hbm, hidden)))
-        ]
-        start(copies)
-
-        @pl.when(k > 0)
-        def _():
-            local, there = hand_out(block_out, (k - 1) * OUT_BLOCK, blocks + k - 1)
-            local.wait()
-            there.wait_send()
-
-        wait(copies)
-        grad_tok[...] = hidden[...] + (chip[...] + far[...])
-        start(hand_out(block_out, k * OUT_BLOCK, blocks + k))
-        summer.tick(pause + k, count)
-
-    @pl.loop(pause + blocks, count + summer.P_LAGS[-1][1])
-    def _(t):
-        summer.tick(t, count)
-
-    local, there = hand_out(block_out, (blocks - 1) * OUT_BLOCK, 2 * blocks - 1)
-    local.wait()
-    there.wait_send()
-
-    @pl.loop(0, blocks)
-    def _(k):
-        ffn_across(k).wait_send()
-        hand_out(tokens_out, place_of(k)[2], k)[1].wait_recv()
-        hand_out(block_out, k * OUT_BLOCK, blocks + k)[1].wait_recv()
-
-    for m in range(max(in_blocks - 2, 0), in_blocks):
-        near_in(m).wait_send()
-    near_out.wait_send()
-    near_small.wait_send()
-
-    @pl.when(here > 0)
-    def _():
-        for slot in range(slots):
-            halo_copy(slot, here - 1).wait_send()
-
-
-def mixer_back(hbm, vmem, sums, slots, collective_id):
-    rest, _, _, _, hidden, _, gated, normed, mixed, w_in, w_out, _, _ = hbm
-    rows, width = normed.shape
-    chans = w_out.shape[0] // 4
-    blocks = rows // OUT_BLOCK
-    in_blocks = width // OUT_BLOCK
-    f32, low = jnp.float32, jnp.bfloat16
-    panels_in = 3 * chans // LANES
-    grad_rows = rest.shape[0] + panels_in * width + width // LANES * chans + 4 * HALF
-    small_rows = 8 * width // LANES
-    block = pltpu.VMEM((OUT_BLOCK, width), f32)
-    full = jax.ShapeDtypeStruct((2 * rows, width), f32)
-    anywhere = pl.BlockSpec(memory_space=pl.ANY)
-    return pl.pallas_call(
-        functools.partial(mixer_kernel, lax.axis_size("seq") // 2),
-        out_shape=[
-            jax.ShapeDtypeStruct(sums.shape, f32),
-            full,
-            full,
-            jax.ShapeDtypeStruct((rows, width), f32),
-            jax.ShapeDtypeStruct((in_blocks, panels_in, OUT_BLOCK, LANES), f32),
-            jax.ShapeDtypeStruct((width // LANES, chans, LANES), f32),
-            jax.ShapeDtypeStruct((small_rows, LANES), f32),
-        ],
-        in_specs=[anywhere] * len(hbm)
-        + [pl.BlockSpec(memory_space=pltpu.VMEM)] * len(vmem)
-        + [anywhere],
-        input_output_aliases={len(hbm) + len(vmem): 0},
-        out_specs=[anywhere] * 7,
-        scratch_shapes=[
-            pltpu.VMEM((grad_rows, LANES), f32),
-            pltpu.VMEM(normed.shape, low),
-            pltpu.VMEM(mixed.shape, low),
-            pltpu.VMEM(w_in.shape, low),
-            pltpu.VMEM(w_out.shape, low),
-            pltpu.VMEM((rows, width), low),
-            pltpu.VMEM((rows, width), low),
-            pltpu.VMEM((rows, width), low),
-            pltpu.VMEM((rows, 3 * width), low),
-            block,
-            block,
-            block,
-            pltpu.VMEM((OUT_BLOCK, 3 * width), f32),
-            pltpu.VMEM((OUT_BLOCK + 8, width), f32),
-            block,
-            pltpu.VMEM((OUT_BLOCK + 8, width), f32),
-            block,
-            block,
-            pltpu.VMEM((slots, 8, width), f32),
-            pltpu.VMEM((slots, 8, width), f32),
-            pltpu.VMEM((8, width), f32),
-            pltpu.VMEM((8, width), f32),
-            pltpu.VMEM((small_rows, LANES), f32),
-            pltpu.VMEM((small_rows, LANES), f32),
-            pltpu.VMEM((2, panels_in, OUT_BLOCK, LANES), f32),
-            pltpu.VMEM((panels_in, OUT_BLOCK, LANES), f32),
-            pltpu.VMEM((width // LANES, chans, LANES), f32),
-            pltpu.VMEM((width // LANES, chans, LANES), f32),
-            pltpu.SemaphoreType.DMA((7,)),
-            pltpu.SemaphoreType.DMA((5,)),
-            pltpu.SemaphoreType.DMA((2, slots)),
-            pltpu.SemaphoreType.DMA((2, in_blocks + 2)),
-            pltpu.SemaphoreType.DMA((2, blocks)),
-            pltpu.SemaphoreType.DMA((2, 2 * blocks + 1)),
-        ]
-        + seq_sum_scratch(),
-        compiler_params=pltpu.CompilerParams(
-            collective_id=collective_id, has_side_effects=True, vmem_limit_bytes=VMEM_LIMIT
-        ),
-        cost_estimate=pl.CostEstimate(
-            flops=26 * rows * width * width, bytes_accessed=400 << 20, transcendentals=0
-        ),
-        name="mixer_back",
-    )(*hbm, *vmem, sums)
-
-
 def per_device(
     tokens, lengths, gain_mix, w_in, conv_weight, w_out, gain_ffn, w_gate, w_up, w_down, cotangent
 ):
@@ -1456,15 +1408,13 @@
     )
     mixer_cols = 4 * chans
     sum_cols = FFN_PANELS * LANES + mixer_cols + LANES
-    ffn_sums, rest, mid_chip, mid_far, ffn_chip = ffn_both_ways(
-        normed_mid, cot_rows, w_gate, w_up, w_down, valid_all, sum_cols, 1
-    )[:5]
-    sums, grad_tokens, block_sum = mixer_back(
+    sums, grad_tokens, block_sum = back_both(
         (
-            rest,
-            mid_chip,
-            mid_far,
-            ffn_chip,
+            normed_mid,
+            cot_rows,
+            w_gate,
+            w_up,
+            w_down,
             hidden_res,
             projected,
             gated_rows,
@@ -1472,13 +1422,12 @@
             mixed,
             w_in_all,
             w_out_all,
-            cot_rows,
             token_rows,
         ),
-        (valid_rows, taps, *gains),
-        ffn_sums,
+        (lengths, taps, *gains),
         half_slots,
-        2,
+        sum_cols,
+        1,
     )[:3]
     grad_tokens = grad_tokens.reshape(slot_count, local_len, width)
     block_out = (valid_all * block_sum).astype(jnp.bfloat16)

time: 566 us -> 529 us (0.935)
  Pallas kernels: 511 us -> 475 us
    pallas_call x2 -> x1, Pallas kernels: 417 us -> 381 us  [back_both(): pl.pallas_call(functools.partial(back_kernel, lax.axis_size('seq') // 2,...]
    unnamed x9 -> x7, local copies, waits for them, and re-layouts: 21.7 us -> 20.7 us
where the time goes in v7:
time: 529 us; the launch traced here: 528 us
  Pallas kernels  475 us (90%)
  local copies, waits for them, and re-layouts  45.4 us (9%)
  other arithmetic  6.64 us (1%)
    pallas_call x1, Pallas kernels, back_both(): pl.pallas_call(functools.partial(back_kernel, lax.axis_size('seq') // 2,...  381 us
    pallas_call x1, Pallas kernels, mixer_front(): pl.pallas_call(functools.partial(front_kernel, count // 2, slots), out_sh...  94.4 us
    unnamed x7, local copies, waits for them, and re-layouts  20.7 us
    transpose x1, local copies, waits for them, and re-layouts, per_device(): total_w_down = sums[:, 2 * hidden:3 * hidden].T  10.6 us

profile of v7, /device:TPU:0, one launch (start us, length us, event | category | flops | bytes accessed | tf_op | source)
XLA Modules:
  0.0 528.2 jit_solution(3963905860610744044)
XLA Ops:
  0.7 1.3 pad.4.refs_2_
  2.0 0.7 convert_bitcast_fusion.1
  2.7 0.6 copy.32
  3.3 0.4 copy.34
  3.7 0.8 constant_dynamic-slice_fusion.1.refs_5_
  4.5 1.7 copy.25
  6.2 1.6 copy.27.refs_0_
  7.8 94.4 %mixer_front.1 = (bf16[1024,3072]{1,0:T(8,128)(2,1)}, bf16[1024,1024]{1,0:T(8,128)(2,1)}, f32[8,1024]{1,0:T(8,128)}, bf16[2048,1024]{1,0:T(8,128)(2,1)}, f32[102...) custom-call(bf16[1024,768]{1,0:T(8,128)(2,1)} %copy.27.refs_0_, ...), custom_call_target="tpu_custom_call" | custom-call | tf_op jit(solution)/shard_map/mixer_front/pallas_call | solution.py:1333
  102.2 381.1 %back_both.1 = (f32[1024,4608]{1,0:T(8,128)}, f32[2048,1024]{1,0:T(8,128)}, f32[2048,1024]{1,0:T(8,128)}, f32[1024,1024]{1,0:T(8,128)}, f32[1024,1024]{1,0:T(8,1...) custom-call(bf16[2048,1024]{1,0:T(8,128)(2,1)} %get-tuple-element.22, ...), custom_call_target="tpu_custom_call" | custom-call | flops 43486543872 | bytes 838860800 | tf_op jit(solution)/shard_map/back_both/pallas_call | solution.py:898
  483.3 5.9 %multiply_convert_fusion = bf16[2048,1024]{1,0:T(8,128)(2,1)} fusion(f32[2048,1024]{1,0:T(8,128)} %get-tuple-element.31, f32[2048]{0:T(1024)} %bitcast.37), kind=kLoop, calls=%fused_computation | loop fusion | flops 4194304 | bytes 12591104 | tf_op jit(solution)/shard_map/convert_element_type | solution.py:1433
  489.2 0.8 slice_bitcast_fusion.1
  490.0 0.7 constant_dynamic-slice_fusion
  490.6 0.6 fusion
  491.2 1.3 slice.33
  492.5 0.5 reshape.108
  493.1 0.7 copy.29
  493.8 1.4 reshape.109
  495.2 2.1 slice.32
  497.2 10.6 %slice_bitcast_fusion = (f32[1152,1024]{0,1:T(8,128)}, f32[1024,1152]{1,0:T(8,128)}, f32[1024,1152]{1,0:T(8,128)}) fusion(f32[1024,4608]{1,0:T(8,128)} %get-tuple-element.33), kind=kLoop, calls=%fused_computation.1 | loop fusion | bytes 28311552 | tf_op jit(solution)/shard_map/transpose | solution.py:1439
  507.8 6.0 %copy.31 = f32[1152,1024]{1,0:T(8,128)} copy(f32[1152,1024]{0,1:T(8,128)} %get-tuple-element.54) | data formatting | bytes 9437184
  513.9 2.4 copy.28
  516.2 3.5 copy.30
  519.8 8.4 %copy.36 = f32[4,512,1024]{2,1,0:T(8,128)} copy(f32[4,512,1024]{2,1,0:T(8,128)} %bitcast.29) | data formatting | bytes 16777216
  (2 shorter events, 0.0 us)

commit v8 on v7

--- a/solution.py
+++ b/solution.py
@@ -953,7 +953,7 @@
 
 
 def front_kernel(places, slots, *refs):
-    (w_in, w_out, taps, gain_mix, gain_ffn, valid, tokens_hbm) = refs[0:7]
+    (w_in, w_out, taps, gain_mix, gain_ffn, lengths, tokens_hbm) = refs[0:7]
     (in_hbm, out_hbm, full_taps, mid_hbm, hidden_hbm, proj_hbm, gated_hbm) = refs[7:14]
     (normed_hbm, mixed_hbm) = refs[14:16]
     own_in, own_out, far_in, far_out, sib_in, sib_out, sibfar_in, sibfar_out = refs[16:24]
@@ -970,9 +970,9 @@
     sibling = tp_at + 1 - 2 * core
     across = lax.rem(tp_at + 2, 4)
     far_sibling = sibling + across - tp_at
-    in_rows = w_in.shape[0] // (2 * places)
+    in_rows = w_in.shape[1] // (2 * places)
     out_rows = w_out.shape[0] // (2 * places)
-    chans = w_in.shape[1] // 3
+    chans = w_in.shape[2]
     rows, width = tokens.shape
     slot_len = rows // slots
     low = jnp.bfloat16
@@ -1049,14 +1049,17 @@
     def single(i, src, dst, device):
         return remote(src, dst, once.at[0, i], once.at[1, i], device)
 
-    for source, held, at in zip((w_in, w_out), share, shares(here)):
-        held[...] = source[at, :].astype(jnp.float32)
+    in_at, out_at = shares(here)
+    for g in range(3):
+        share_in[:, g * chans : (g + 1) * chans] = w_in[g, in_at, :].astype(jnp.float32)
+    share_out[...] = w_out[out_at, :].astype(jnp.float32)
     start(across_share())
     own_taps[...] = taps[...]
     taps_far = single(0, own_taps, far_taps, {"tp": across})
     taps_sib = single(1, own_taps, sib_taps, {"tp": sibling})
     taps_sibfar = single(2, far_taps, sibfar_taps, {"tp": sibling})
-    own_in[...] = w_in[...].astype(jnp.float32)
+    for g in range(3):
+        own_in[:, g * chans : (g + 1) * chans] = w_in[g].astype(jnp.float32)
     own_out[...] = w_out[...].astype(jnp.float32)
     in_sib = single(3, own_in, sib_in, {"tp": sibling})
     out_sib = single(4, own_out, sib_out, {"tp": sibling})
@@ -1112,10 +1115,12 @@
                     preferred_element_type=jnp.float32,
                 )
 
+            at_pos = lax.broadcasted_iota(jnp.int32, (slot_len, 1), 0) + here * slot_len
+            mask = (at_pos < lengths[core * slots + s]).astype(jnp.float32)
             in_gate, value = gate(0), gate(2)
             gates[turn % 2, 0, at, :] = in_gate
             gates[turn % 2, 1, at, :] = value
-            gated[s, pl.ds(8, slot_len), cols] = valid[at, :] * in_gate * value
+            gated[s, pl.ds(8, slot_len), cols] = mask * in_gate * value
             out_gate[at, cols] = gate(1)
 
         for g in range(3):
@@ -1319,9 +1324,9 @@
         left_source(to_sibling(2 * q + 1 - side))
 
 
-def mixer_front(w_in, w_out, taps, gain_mix, gain_ffn, valid, tokens, slots, collective_id):
+def mixer_front(w_in, w_out, taps, gain_mix, gain_ffn, lengths, tokens, slots, collective_id):
     width, _, chans = w_in.shape
-    rows = valid.shape[0]
+    rows = tokens.shape[0] // 2
     count = lax.axis_size("seq")
     group = lax.axis_size("tp")
     f32, low = jnp.float32, jnp.bfloat16
@@ -1343,7 +1348,7 @@
             jax.ShapeDtypeStruct((rows, width), low),
             jax.ShapeDtypeStruct((rows, width), low),
         ],
-        in_specs=[whole] * 6 + [anywhere],
+        in_specs=[whole] * 5 + [pl.BlockSpec(memory_space=pltpu.SMEM), anywhere],
         out_specs=[anywhere] * 2 + [whole] + [anywhere] * 6,
         scratch_shapes=pair * 4
         + [pltpu.VMEM((8, chans), f32)] * 4
@@ -1375,14 +1380,162 @@
         ),
         name="mixer_front",
     )(
-        w_in.reshape(width, 3 * chans),
+        w_in.transpose(1, 0, 2),
         w_out,
         jnp.pad(taps, ((0, 5), (0, 0))),
         gain_mix,
         gain_ffn,
-        valid,
+        lengths,
         tokens,
     )
+
+
+def finish_kernel(slots, chans, hidden, *refs):
+    (sums, tokens_in, block_in, lengths) = refs[0:4]
+    (block_out, tokens_out, gains, g_in, g_conv, g_out, g_gate, g_up, g_down) = refs[4:13]
+    (held, tokens, block, rounded, turned, in_sems, block_sems, turn_sems, out_sems) = refs[13:22]
+    rows, width = block_in.shape
+    slot_len = rows // slots
+    here = lax.axis_index("seq")
+    tp_at = lax.axis_index("tp")
+    first = 3 * hidden
+    out_first = first + 3 * chans
+    small_first = out_first + chans
+    blocks = rows // OUT_BLOCK
+    turns = hidden // LANES
+    half_rows = rows // 2
+
+    def cols(start, size):
+        return (slice(None), slice(start, start + size))
+
+    parts = [cols(i * hidden, hidden) for i in range(3)] + [cols(first, held.shape[1] - first)]
+    halves = [slice(0, half_rows), slice(half_rows, rows)]
+    part_loads = [
+        pltpu.make_async_copy(sums.at[at], held.at[at], in_sems.at[i]) for i, at in enumerate(parts)
+    ]
+    token_loads = [
+        pltpu.make_async_copy(tokens_in.at[at], tokens.at[at], in_sems.at[4 + i])
+        for i, at in enumerate(halves)
+    ]
+
+    def block_at(k):
+        return pl.ds(pl.multiple_of(k * OUT_BLOCK, OUT_BLOCK), OUT_BLOCK)
+
+    def block_load(k):
+        return pltpu.make_async_copy(
+            block_in.at[block_at(k)], block.at[block_at(k)], block_sems.at[0, k]
+        )
+
+    def block_store(k):
+        return pltpu.make_async_copy(
+            rounded.at[block_at(k)], block_out.at[block_at(k)], block_sems.at[1, k]
+        )
+
+    def panel_at(k):
+        return pl.ds(pl.multiple_of(k * LANES, LANES), LANES)
+
+    def turn_store(k):
+        at = panel_at(k)
+        return pltpu.make_async_copy(turned.at[at], g_down.at[at], turn_sems.at[k])
+
+    stores = []
+
+    def store(src, dst):
+        copy = pltpu.make_async_copy(src, dst, out_sems.at[len(stores)])
+        copy.start()
+        stores.append(copy)
+
+    part_loads[2].start()
+
+    @pl.loop(0, blocks)
+    def _(k):
+        block_load(k).start()
+
+    for load in (*token_loads, part_loads[0], part_loads[1], part_loads[3]):
+        load.start()
+
+    part_loads[2].wait()
+
+    @pl.loop(0, turns)
+    def _(k):
+        from_cols = pl.ds(pl.multiple_of(2 * hidden + k * LANES, LANES), LANES)
+        turned[panel_at(k), :] = held[:, from_cols].T
+        turn_store(k).start()
+
+    @pl.loop(0, blocks)
+    def _(k):
+        block_load(k).wait()
+        per_slot = slot_len // OUT_BLOCK
+        at = lax.broadcasted_iota(jnp.int32, (OUT_BLOCK, 1), 0)
+        at = at + (here * slot_len + lax.rem(k, per_slot) * OUT_BLOCK)
+        mask = (at < lengths[k // per_slot]).astype(jnp.float32)
+        rounded[block_at(k), :] = (mask * block[block_at(k), :]).astype(jnp.bfloat16)
+        block_store(k).start()
+
+    for load, at in zip(token_loads, halves):
+        load.wait()
+        store(tokens.at[at], tokens_out.at[at])
+    for i, target in ((0, g_gate), (1, g_up)):
+        part_loads[i].wait()
+        store(held.at[parts[i]], target)
+    part_loads[3].wait()
+    for g in range(3):
+        store(held.at[cols(first + g * chans, chans)], g_in.at[g])
+    per_col = width // chans
+    for p in range(width // LANES):
+        q, r = p // per_col, p % per_col
+        at = (slice(r * chans, (r + 1) * chans), slice(out_first + q * LANES, out_first + (q + 1) * LANES))
+        store(held.at[at], g_out.at[cols(p * LANES, LANES)])
+        gains[cols(p * LANES, LANES)] = held[8 * p : 8 * p + 8, small_first:]
+    own = pl.ds(pl.multiple_of(tp_at * chans, LANES), chans)
+    g_conv[...] = gains[2:5, own]
+    for copy in stores:
+        copy.wait()
+
+    @pl.loop(0, turns)
+    def _(k):
+        turn_store(k).wait()
+
+    @pl.loop(0, blocks)
+    def _(k):
+        block_store(k).wait()
+
+
+def finish(sums, tokens_grad, block_sum, lengths, chans, hidden):
+    rows, width = block_sum.shape
+    f32 = jnp.float32
+    anywhere = pl.BlockSpec(memory_space=pl.ANY)
+    whole = pl.BlockSpec(memory_space=pltpu.VMEM)
+    blocks = rows // OUT_BLOCK
+    return pl.pallas_call(
+        functools.partial(finish_kernel, lengths.shape[0], chans, hidden),
+        out_shape=[
+            jax.ShapeDtypeStruct((rows, width), jnp.bfloat16),
+            jax.ShapeDtypeStruct((rows, width), f32),
+            jax.ShapeDtypeStruct((8, width), f32),
+            jax.ShapeDtypeStruct((3, width, chans), f32),
+            jax.ShapeDtypeStruct((3, chans), f32),
+            jax.ShapeDtypeStruct((chans, width), f32),
+            jax.ShapeDtypeStruct((width, hidden), f32),
+            jax.ShapeDtypeStruct((width, hidden), f32),
+            jax.ShapeDtypeStruct((hidden, width), f32),
+        ],
+        in_specs=[anywhere] * 3 + [pl.BlockSpec(memory_space=pltpu.SMEM)],
+        out_specs=[anywhere] * 2 + [whole, anywhere, whole] + [anywhere] * 4,
+        scratch_shapes=[
+            pltpu.VMEM(sums.shape, f32),
+            pltpu.VMEM((rows, width), f32),
+            pltpu.VMEM((rows, width), f32),
+            pltpu.VMEM((rows, width), jnp.bfloat16),
+            pltpu.VMEM((hidden, width), f32),
+            pltpu.SemaphoreType.DMA((6,)),
+            pltpu.SemaphoreType.DMA((2, blocks)),
+            pltpu.SemaphoreType.DMA((hidden // LANES,)),
+            pltpu.SemaphoreType.DMA((7 + width // LANES,)),
+        ],
+        compiler_params=pltpu.CompilerParams(vmem_limit_bytes=VMEM_LIMIT),
+        name="finish",
+    )(sums, tokens_grad, block_sum, lengths)
 
 
 def per_device(
@@ -1390,21 +1543,14 @@
 ):
     slot_count, local_len, width = tokens.shape
     chans = w_in.shape[2]
-    tp_at, seq_at = lax.axis_index("tp"), lax.axis_index("seq")
-    core = tp_at % 2
     half_slots = slot_count // 2
-    half_rows = half_slots * local_len
     row_count = slot_count * local_len
 
-    positions = seq_at * local_len + jnp.arange(local_len, dtype=jnp.int32)
-    valid = (positions[None, :] < lengths[:, None]).astype(jnp.float32)
-    valid_all = valid.reshape(row_count, 1)
-    valid_rows = lax.dynamic_slice(valid_all, (core * half_rows, 0), (half_rows, 1))
     token_rows = tokens.reshape(row_count, width)
     cot_rows = cotangent.reshape(row_count, width)
     gains = gain_mix.reshape(1, width), gain_ffn.reshape(1, width)
     w_in_all, w_out_all, taps, normed_mid, hidden_res, projected, gated_rows, normed_in, mixed = (
-        mixer_front(w_in, w_out, conv_weight, *gains, valid_rows, token_rows, half_slots, 3)
+        mixer_front(w_in, w_out, conv_weight, *gains, lengths, token_rows, half_slots, 3)
     )
     mixer_cols = 4 * chans
     sum_cols = FFN_PANELS * LANES + mixer_cols + LANES
@@ -1429,34 +1575,20 @@
         sum_cols,
         1,
     )[:3]
-    grad_tokens = grad_tokens.reshape(slot_count, local_len, width)
-    block_out = (valid_all * block_sum).astype(jnp.bfloat16)
-    block_out = block_out.reshape(slot_count, local_len, width)
-
-    hidden = w_gate.shape[1]
-    total_w_gate = sums[:, :hidden]
-    total_w_up = sums[:, hidden : 2 * hidden]
-    total_w_down = sums[:, 2 * hidden : 3 * hidden].T
-    mixer_sums = sums[:, 3 * hidden :]
-    total_w_in = mixer_sums[:, : 3 * chans].reshape(width, 3, chans)
-    out_parts = mixer_sums[:, 3 * chans : 4 * chans]
-    out_parts = out_parts.reshape(width // chans, chans, chans // LANES, LANES)
-    total_w_out = out_parts.transpose(1, 2, 0, 3).reshape(chans, width)
-    small = mixer_sums[: 8 * width // LANES, 4 * chans :]
-    small = small.reshape(width // LANES, 8, LANES).transpose(1, 0, 2).reshape(8, width)
-    total_gain_mix, total_gain_ffn = small[0], small[1]
-    total_conv = lax.dynamic_slice(small, (2, tp_at * chans), (3, chans))
+    block_out, grad_tokens, small, g_in, g_conv, g_out, g_gate, g_up, g_down = finish(
+        sums, grad_tokens, block_sum, lengths, chans, w_gate.shape[1]
+    )
     return (
-        block_out,
-        grad_tokens,
-        total_gain_mix,
-        total_w_in,
-        total_conv,
-        total_w_out,
-        total_gain_ffn,
-        total_w_gate,
-        total_w_up,
-        total_w_down,
+        block_out.reshape(slot_count, local_len, width),
+        grad_tokens.reshape(slot_count, local_len, width),
+        small[0],
+        g_in.transpose(1, 0, 2),
+        g_conv,
+        g_out,
+        small[1],
+        g_gate,
+        g_up,
+        g_down,
     )
 
 

time: 529 us -> 505 us (0.955)
  local copies, waits for them, and re-layouts: 45.4 us -> 2.73 us
  Pallas kernels: 475 us -> 500 us
  other arithmetic: 6.64 us -> 0 us
    pallas_call x0 -> x1, Pallas kernels: none -> 24.3 us  [finish(): pl.pallas_call(functools.partial(finish_kernel, lengths.shape[0], chans,...]
    unnamed x7 -> x0, local copies, waits for them, and re-layouts: 20.7 us -> none
    transpose x2 -> x0, local copies, waits for them, and re-layouts: 11.3 us -> none  [the longest x1 10.6 us: per_device(): total_w_down = sums[:, 2 * hidden:3 * hidden].T]
    convert_element_type x1 -> x0, other arithmetic: 5.91 us -> none  [per_device(): block_out = (valid_all * block_sum).astype(jnp.bfloat16)]
where the time goes in v8:
time: 505 us; the launch traced here: 504 us
  Pallas kernels  500 us (99%)
    pallas_call x1, Pallas kernels, back_both(): pl.pallas_call(functools.partial(back_kernel, lax.axis_size('seq') // 2,...  382 us
    pallas_call x1, Pallas kernels, mixer_front(): pl.pallas_call(functools.partial(front_kernel, count // 2, slots), out_sh...  94.3 us
    pallas_call x1, Pallas kernels, finish(): pl.pallas_call(functools.partial(finish_kernel, lengths.shape[0], chans,...  24.3 us

profile of v8, /device:TPU:0, one launch (start us, length us, event | category | flops | bytes accessed | tf_op | source)
XLA Modules:
  0.0 503.9 jit_solution(992452334574168094)
XLA Ops:
  0.6 1.3 pad.4.refs_2_
  1.9 94.3 %mixer_front.1 = (bf16[1024,3072]{1,0:T(8,128)(2,1)}, bf16[1024,1024]{1,0:T(8,128)(2,1)}, f32[8,1024]{1,0:T(8,128)}, bf16[2048,1024]{1,0:T(8,128)(2,1)}, f32[102...) custom-call(bf16[3,1024,256]{2,1,0:T(8,128)(2,1)} %bitcast.12, ...), custom_call_target="tpu_custom_call" | custom-call | tf_op jit(solution)/shard_map/mixer_front/pallas_call | solution.py:1338
  96.3 381.9 %back_both.1 = (f32[1024,4608]{1,0:T(8,128)}, f32[2048,1024]{1,0:T(8,128)}, f32[2048,1024]{1,0:T(8,128)}, f32[1024,1024]{1,0:T(8,128)}, f32[1024,1024]{1,0:T(8,1...) custom-call(bf16[2048,1024]{1,0:T(8,128)(2,1)} %get-tuple-element.31, ...), custom_call_target="tpu_custom_call" | custom-call | flops 43486543872 | bytes 838860800 | tf_op jit(solution)/shard_map/back_both/pallas_call | solution.py:898
  478.2 24.3 %finish.1 = (bf16[2048,1024]{1,0:T(8,128)(2,1)}, f32[2048,1024]{1,0:T(8,128)}, f32[8,1024]{1,0:T(8,128)}, f32[3,1024,256]{2,1,0:T(8,128)}, f32[3,256]{1,0:T(4,12...) custom-call(f32[1024,4608]{1,0:T(8,128)} %get-tuple-element.40.refs_0_, ...), custom_call_target="tpu_custom_call" | custom-call | tf_op jit(solution)/shard_map/finish/pallas_call | solution.py:1510
  502.4 1.4 fusion

commit v9 on v8

--- a/solution.py
+++ b/solution.py
@@ -50,8 +50,8 @@
 
 
 class SeqSum:
-    def __init__(self, places, own, out, panel_of, scratch):
-        self.places, self.own, self.out, self.panel_of = places, own, out, panel_of
+    def __init__(self, places, own, out, scratch):
+        self.places, self.own, self.out = places, own, out
         self.y_in, self.p_left, self.p_right, self.p_acc = scratch[0:4]
         self.q_left, self.q_right, self.q_acc, self.q_in = scratch[4:8]
         self.sems = scratch[8]
@@ -82,8 +82,8 @@
 
     def out_at(self, k, first, size):
         per_panel = self.out.shape[0] // (4 * HALF)
-        panel = self.panel_of(k // per_panel)
-        row = lax.rem(k, per_panel) * 4 * HALF + first
+        panel, part = place_in_sums(k, per_panel)
+        row = part * 4 * HALF + first
         return self.out.at[
             pl.ds(pl.multiple_of(row, size), size), pl.ds(pl.multiple_of(panel * LANES, LANES), LANES)
         ]
@@ -302,6 +302,7 @@
 
 
 SUB_ROWS = 64
+STRAIGHT_COPIES = 4
 FIRST_MIXER_TICK = 36
 BLOCK_TICK = 56
 FFN_PANELS = 27
@@ -311,12 +312,17 @@
 OUT_BLOCK = 256
 
 
-def panel_in_sums(panel):
+def place_in_sums(piece, per_panel):
     per_part = FFN_PANELS // FFN_PARTS
     third = per_part // 3
-    inside = lax.rem(panel, per_part)
-    kind = inside // third
-    return kind * (FFN_PANELS // 3) + panel // per_part * third + lax.rem(inside, third)
+    part, inside = piece // (per_part * per_panel), lax.rem(piece, per_part * per_panel)
+    kind = lax.rem(inside, per_part)
+    panel = kind // third * (FFN_PANELS // 3) + part * third + lax.rem(kind, third)
+    of_ffn = piece < FFN_PANELS * per_panel
+    return (
+        jnp.where(of_ffn, panel, piece // per_panel),
+        jnp.where(of_ffn, inside // per_part, lax.rem(piece, per_panel)),
+    )
 
 
 def norm_back(grad, gain, unit, scale):
@@ -336,10 +342,7 @@
     load_sems, near_sems, far_sems, keep_sem, fetch_sem = refs[49:54]
     (later_sems, row_sems, halo_sems, weight_sems, out_sems) = refs[54:59]
 
-    def panel_of(panel):
-        return jnp.where(panel < FFN_PANELS, panel_in_sums(panel), panel)
-
-    summer = SeqSum(places, own, sums, panel_of, refs[59:])
+    summer = SeqSum(places, own, sums, refs[59:])
     here = lax.axis_index("seq")
     last = 2 * places - 1
     tp_at = lax.axis_index("tp")
@@ -356,12 +359,11 @@
     moves = [(mid_hbm, mid), (cot_hbm, cot), (w_d_hbm, w_d)]
     for c in range(parts):
         for i, source in enumerate((w_gate_hbm, w_up_hbm)):
-            moves.append(
-                (
-                    source.at[:, c * hidden : (c + 1) * hidden],
-                    w_gu.at[c, :, i * hidden : (i + 1) * hidden],
-                )
+            move = (
+                source.at[:, c * hidden : (c + 1) * hidden],
+                w_gu.at[c, :, i * hidden : (i + 1) * hidden],
             )
+            moves.insert(i if c == 0 else len(moves), move)
     loads = [
         pltpu.make_async_copy(src, dst, load_sems.at[i]) for i, (src, dst) in enumerate(moves)
     ]
@@ -380,7 +382,7 @@
     ffn_pieces = own.shape[0] // (4 * HALF)
     mixer_pieces = 4 * chans * width // LANES // (4 * HALF) + 1
     count = ffn_pieces + mixer_pieces
-    for load in loads:
+    for load in loads[:5]:
         load.wait()
 
     slot_len = rows // 2 // slots
@@ -390,12 +392,20 @@
         return (at < lengths[slot]).astype(jnp.float32)
 
     part_ticks = rows // ROW_BLOCK // ROW_TICK + width // OUT_BLOCK
+    first_ticks = width // OUT_BLOCK - 4 * HALF // OUT_BLOCK
 
     def part_cols(c):
         return pl.ds(pl.multiple_of(c * hidden, LANES), hidden)
 
     @pl.loop(0, parts)
     def _(c):
+        for i in range(1, parts):
+
+            @pl.when(c == i)
+            def _(i=i):
+                loads[3 + 2 * i].wait()
+                loads[4 + 2 * i].wait()
+
         @pl.loop(0, rows // ROW_BLOCK)
         def _(r):
             at = pl.ds(pl.multiple_of(r * ROW_BLOCK, ROW_BLOCK), ROW_BLOCK)
@@ -418,27 +428,32 @@
 
             @pl.when((c > 0) & (lax.rem(r, ROW_TICK) == ROW_TICK - 1))
             def _():
-                summer.tick((c - 1) * part_ticks + r // ROW_TICK, count)
+                summer.tick(first_ticks + (c - 1) * part_ticks + r // ROW_TICK, count)
 
         @pl.loop(0, width // OUT_BLOCK)
         def _(m):
             first = pl.multiple_of(m * OUT_BLOCK, OUT_BLOCK)
             at = pl.ds(first, OUT_BLOCK)
-            base = c * (panels * width) + first
+            per_piece = 4 * HALF // OUT_BLOCK
+            piece = (c * (width // OUT_BLOCK // per_piece) + m // per_piece) * panels
+            base = piece * 4 * HALF + lax.rem(m, per_piece) * OUT_BLOCK
 
             def put(block, panel):
                 for j in range(block.shape[1] // LANES):
-                    to = pl.multiple_of(base + (panel + j) * width, OUT_BLOCK)
+                    to = pl.multiple_of(base + (panel + j) * 4 * HALF, OUT_BLOCK)
                     own[pl.ds(to, OUT_BLOCK), :] = block[:, j * LANES : (j + 1) * LANES]
 
             put(dot_rows(mid[:, at], ggu[c]), 0)
             put(dot_rows(cot[:, at], act[:, part_cols(c)]), wide // LANES)
 
-            @pl.when(c > 0)
+            step = first_ticks + (c - 1) * part_ticks + rows // ROW_BLOCK // ROW_TICK + m
+            step = jnp.where(c > 0, step, m - (width // OUT_BLOCK - first_ticks))
+
+            @pl.when(step >= 0)
             def _():
-                summer.tick((c - 1) * part_ticks + rows // ROW_BLOCK // ROW_TICK + m, count)
-
-    early = (parts - 1) * part_ticks
+                summer.tick(step, count)
+
+    early = first_ticks + (parts - 1) * part_ticks
     blocks = rows // 2 // OUT_BLOCK
     def row_block(half, k):
         return pl.ds(pl.multiple_of((half * blocks + k) * OUT_BLOCK, OUT_BLOCK), OUT_BLOCK)
@@ -961,6 +976,7 @@
     (full_in, full_out, tokens, normed, mixed, out_gate, gates, gated) = refs[30:38]
     (unit_out, unit_in, hidden) = refs[38:41]
     sends, recvs, once, halo_sems, gate_sems, unit_sems, keep_sems, mid_sems = refs[41:49]
+    straight_sems = refs[49]
     here = lax.axis_index("seq")
     place, side = here // 2, lax.rem(here, 2)
     last = places - 1
@@ -970,7 +986,8 @@
     sibling = tp_at + 1 - 2 * core
     across = lax.rem(tp_at + 2, 4)
     far_sibling = sibling + across - tp_at
-    in_rows = w_in.shape[1] // (2 * places)
+    straight = w_in.shape[1] // 2
+    in_rows = (w_in.shape[1] - straight) // (2 * places)
     out_rows = w_out.shape[0] // (2 * places)
     chans = w_in.shape[2]
     rows, width = tokens.shape
@@ -1033,6 +1050,29 @@
 
     def to_sibling(j):
         return copies(far, sibfar, j, 4, {"tp": sibling})
+
+    def straight_rows(q):
+        size = straight // STRAIGHT_COPIES
+        first = w_in.shape[1] - straight + q * size
+        return pl.ds(pl.multiple_of(first, size), size)
+
+    def straight_across(q):
+        at = straight_rows(q)
+        return remote(
+            own_in.at[at], far_in.at[at], straight_sems.at[0, q], straight_sems.at[1, q],
+            {"tp": across},
+        )
+
+    def straight_sibling(q):
+        at = straight_rows(q)
+        return remote(
+            far_in.at[at], sibfar_in.at[at], straight_sems.at[2, q], straight_sems.at[3, q],
+            {"tp": sibling},
+        )
+
+    def pass_straight(q):
+        straight_across(q).wait_recv()
+        straight_sibling(q).start()
 
     def start(group):
         for copy in group:
@@ -1065,6 +1105,8 @@
     out_sib = single(4, own_out, sib_out, {"tp": sibling})
     for copy in (taps_far, taps_sib, in_sib, out_sib):
         copy.start()
+    for q in range(STRAIGHT_COPIES):
+        straight_across(q).start()
 
     def gate_cols(g, index):
         return pl.ds(pl.multiple_of(g * width + index * chans, LANES), chans)
@@ -1210,6 +1252,10 @@
 
         pl.when(place - d >= 0)(lambda: from_side(place - d))
         pl.when(place + d <= last)(lambda: from_side(place + d))
+        pl.when(d <= STRAIGHT_COPIES)(lambda: pass_straight(d - 1))
+
+    for q in range(min(last, STRAIGHT_COPIES), STRAIGHT_COPIES):
+        pass_straight(q)
 
     place_shard(far_in, far_out, far_taps, across)
     project(2)
@@ -1219,6 +1265,8 @@
     def _(j):
         arrived(to_sibling(j))
 
+    for q in range(STRAIGHT_COPIES):
+        straight_sibling(q).wait_recv()
     place_shard(sibfar_in, sibfar_out, sibfar_taps, far_sibling)
     project(3)
     keep_in = pltpu.make_async_copy(full_in, in_hbm, keep_sems.at[1])
@@ -1311,6 +1359,9 @@
                 halo(turn, order[turn], slot).wait_send()
 
     left_source(across_share())
+    for q in range(STRAIGHT_COPIES):
+        straight_across(q).wait_send()
+        straight_sibling(q).wait_send()
     for copy in (taps_far, taps_sib, taps_sibfar, in_sib, out_sib):
         copy.wait_send()
 
@@ -1353,7 +1404,7 @@
         scratch_shapes=pair * 4
         + [pltpu.VMEM((8, chans), f32)] * 4
         + [
-            pltpu.VMEM((width // count, 3 * chans), f32),
+            pltpu.VMEM((width // 2 // count, 3 * chans), f32),
             pltpu.VMEM((chans // count, width), f32),
             pltpu.VMEM((width, 3 * chans * group), low),
             pltpu.VMEM((chans * group, width), low),
@@ -1374,6 +1425,7 @@
             pltpu.SemaphoreType.DMA((2, blocks)),
             pltpu.SemaphoreType.DMA((5,)),
             pltpu.SemaphoreType.DMA((3, blocks)),
+            pltpu.SemaphoreType.DMA((4, STRAIGHT_COPIES)),
         ],
         compiler_params=pltpu.CompilerParams(
             collective_id=collective_id, has_side_effects=True, vmem_limit_bytes=VMEM_LIMIT

time: 505 us -> 484 us (0.958)
  Pallas kernels: 500 us -> 480 us
    pallas_call x1, Pallas kernels: 94.3 us -> 69.8 us  [mixer_front(): pl.pallas_call(functools.partial(front_kernel, count // 2, slots), out_sh...]
where the time goes in v9:
time: 484 us; the launch traced here: 483 us
  Pallas kernels  480 us (99%)
    pallas_call x1, Pallas kernels, back_both(): pl.pallas_call(functools.partial(back_kernel, lax.axis_size('seq') // 2,...  386 us
    pallas_call x1, Pallas kernels, mixer_front(): pl.pallas_call(functools.partial(front_kernel, count // 2, slots), out_sh...  69.8 us
    pallas_call x1, Pallas kernels, finish(): pl.pallas_call(functools.partial(finish_kernel, lengths.shape[0], chans,...  24.3 us

profile of v9, /device:TPU:0, one launch (start us, length us, event | category | flops | bytes accessed | tf_op | source)
XLA Modules:
  0.0 483.5 jit_solution(10622955139212389268)
XLA Ops:
  0.6 1.3 pad.4.refs_2_
  1.9 69.8 %mixer_front.1 = (bf16[1024,3072]{1,0:T(8,128)(2,1)}, bf16[1024,1024]{1,0:T(8,128)(2,1)}, f32[8,1024]{1,0:T(8,128)}, bf16[2048,1024]{1,0:T(8,128)(2,1)}, f32[102...) custom-call(bf16[3,1024,256]{2,1,0:T(8,128)(2,1)} %bitcast.12, ...), custom_call_target="tpu_custom_call" | custom-call | tf_op jit(solution)/shard_map/mixer_front/pallas_call | solution.py:1389
  71.8 386.0 %back_both.1 = (f32[1024,4608]{1,0:T(8,128)}, f32[2048,1024]{1,0:T(8,128)}, f32[2048,1024]{1,0:T(8,128)}, f32[1024,1024]{1,0:T(8,128)}, f32[1024,1024]{1,0:T(8,1...) custom-call(bf16[2048,1024]{1,0:T(8,128)(2,1)} %get-tuple-element.31, ...), custom_call_target="tpu_custom_call" | custom-call | flops 43486543872 | bytes 838860800 | tf_op jit(solution)/shard_map/back_both/pallas_call | solution.py:913
  457.7 24.3 %finish.1 = (bf16[2048,1024]{1,0:T(8,128)(2,1)}, f32[2048,1024]{1,0:T(8,128)}, f32[8,1024]{1,0:T(8,128)}, f32[3,1024,256]{2,1,0:T(8,128)}, f32[3,256]{1,0:T(4,12...) custom-call(f32[1024,4608]{1,0:T(8,128)} %get-tuple-element.40.refs_0_, ...), custom_call_target="tpu_custom_call" | custom-call | tf_op jit(solution)/shard_map/finish/pallas_call | solution.py:1562
  482.0 1.4 fusion

commit v10 on v9

--- a/solution.py
+++ b/solution.py
@@ -391,17 +391,21 @@
         at = lax.broadcasted_iota(jnp.int32, (size, 1), 0) + (here * slot_len + first)
         return (at < lengths[slot]).astype(jnp.float32)
 
-    part_ticks = rows // ROW_BLOCK // ROW_TICK + width // OUT_BLOCK
-    first_ticks = width // OUT_BLOCK - 4 * HALF // OUT_BLOCK
+    row_ticks = rows // ROW_BLOCK // ROW_TICK
+    grad_ticks = width // OUT_BLOCK
+    first_ticks = grad_ticks - 4 * HALF // OUT_BLOCK
+    blocks = rows // 2 // OUT_BLOCK
+    before_mid = first_ticks + (parts - 1) * row_ticks
+    after_mid = before_mid + blocks
+    before_ffn = after_mid + (parts - 1) * grad_ticks
 
     def part_cols(c):
         return pl.ds(pl.multiple_of(c * hidden, LANES), hidden)
 
-    @pl.loop(0, parts)
-    def _(c):
+    def row_phase(c):
         for i in range(1, parts):
 
-            @pl.when(c == i)
+            @pl.when(jnp.int32(c) == i)
             def _(i=i):
                 loads[3 + 2 * i].wait()
                 loads[4 + 2 * i].wait()
@@ -410,7 +414,7 @@
         def _(r):
             at = pl.ds(pl.multiple_of(r * ROW_BLOCK, ROW_BLOCK), ROW_BLOCK)
 
-            @pl.when(c == 0)
+            @pl.when(jnp.int32(c) == 0)
             def _():
                 per_slot = slot_len // ROW_BLOCK
                 mask = valid_rows(r // per_slot, lax.rem(r, per_slot) * ROW_BLOCK, ROW_BLOCK)
@@ -426,10 +430,11 @@
             ggu[c, at, :hidden] = (grad_act * up * slope).astype(jnp.bfloat16)
             ggu[c, at, hidden:] = (grad_act * silu).astype(jnp.bfloat16)
 
-            @pl.when((c > 0) & (lax.rem(r, ROW_TICK) == ROW_TICK - 1))
+            @pl.when((jnp.int32(c) > 0) & (lax.rem(r, ROW_TICK) == ROW_TICK - 1))
             def _():
-                summer.tick(first_ticks + (c - 1) * part_ticks + r // ROW_TICK, count)
-
+                summer.tick(first_ticks + (c - 1) * row_ticks + r // ROW_TICK, count)
+
+    def grad_phase(c):
         @pl.loop(0, width // OUT_BLOCK)
         def _(m):
             first = pl.multiple_of(m * OUT_BLOCK, OUT_BLOCK)
@@ -446,15 +451,12 @@
             put(dot_rows(mid[:, at], ggu[c]), 0)
             put(dot_rows(cot[:, at], act[:, part_cols(c)]), wide // LANES)
 
-            step = first_ticks + (c - 1) * part_ticks + rows // ROW_BLOCK // ROW_TICK + m
-            step = jnp.where(c > 0, step, m - (width // OUT_BLOCK - first_ticks))
+            step = jnp.where(jnp.int32(c) > 0, after_mid + (c - 1) * grad_ticks + m, m - grad_ticks + first_ticks)
 
             @pl.when(step >= 0)
             def _():
                 summer.tick(step, count)
 
-    early = first_ticks + (parts - 1) * part_ticks
-    blocks = rows // 2 // OUT_BLOCK
     def row_block(half, k):
         return pl.ds(pl.multiple_of((half * blocks + k) * OUT_BLOCK, OUT_BLOCK), OUT_BLOCK)
 
@@ -522,8 +524,12 @@
             if which == 0:
                 far(0, mid_chip, mid_far, k).start()
 
-    tp_sum(0, mid_part, mid_land, mid_chip, early)
-    tp_sum(1, ffn_part, ffn_land, ffn_chip, early + blocks)
+    row_phase(0)
+    grad_phase(0)
+    pl.loop(1, parts)(row_phase)
+    tp_sum(0, mid_part, mid_land, mid_chip, before_mid)
+    pl.loop(1, parts)(grad_phase)
+    tp_sum(1, ffn_part, ffn_land, ffn_chip, before_ffn)
 
     own_half = pl.ds(pl.multiple_of(core * half_rows, half_rows), half_rows)
     low_half, high_half = pl.ds(0, half_rows), pl.ds(half_rows, half_rows)
@@ -551,7 +557,7 @@
     chip, far_rows, hidden_rows = staged.at[0], staged.at[1], fetched
     per_slot = slot_len // OUT_BLOCK
     small[...] = jnp.zeros_like(small)
-    ticked = early + 2 * blocks
+    ticked = before_ffn + blocks
 
     @pl.loop(ticked, FIRST_MIXER_TICK)
     def _(t):

time: 484 us -> 471 us (0.973)
  Pallas kernels: 480 us -> 467 us
    pallas_call x1, Pallas kernels: 386 us -> 373 us  [back_both(): pl.pallas_call(functools.partial(back_kernel, lax.axis_size('seq') // 2,...]
where the time goes in v10:
time: 471 us; the launch traced here: 470 us
  Pallas kernels  467 us (99%)
    pallas_call x1, Pallas kernels, back_both(): pl.pallas_call(functools.partial(back_kernel, lax.axis_size('seq') // 2,...  373 us
    pallas_call x1, Pallas kernels, mixer_front(): pl.pallas_call(functools.partial(front_kernel, count // 2, slots), out_sh...  69.8 us
    pallas_call x1, Pallas kernels, finish(): pl.pallas_call(functools.partial(finish_kernel, lengths.shape[0], chans,...  24.3 us

profile of v10, /device:TPU:0, one launch (start us, length us, event | category | flops | bytes accessed | tf_op | source)
XLA Modules:
  0.0 470.4 jit_solution(8219003524853844579)
XLA Ops:
  0.6 1.3 pad.4.refs_2_
  1.9 69.8 %mixer_front.1 = (bf16[1024,3072]{1,0:T(8,128)(2,1)}, bf16[1024,1024]{1,0:T(8,128)(2,1)}, f32[8,1024]{1,0:T(8,128)}, bf16[2048,1024]{1,0:T(8,128)(2,1)}, f32[102...) custom-call(bf16[3,1024,256]{2,1,0:T(8,128)(2,1)} %bitcast.12, ...), custom_call_target="tpu_custom_call" | custom-call | tf_op jit(solution)/shard_map/mixer_front/pallas_call | solution.py:1395
  71.8 372.9 %back_both.1 = (f32[1024,4608]{1,0:T(8,128)}, f32[2048,1024]{1,0:T(8,128)}, f32[2048,1024]{1,0:T(8,128)}, f32[1024,1024]{1,0:T(8,128)}, f32[1024,1024]{1,0:T(8,1...) custom-call(bf16[2048,1024]{1,0:T(8,128)(2,1)} %get-tuple-element.31, ...), custom_call_target="tpu_custom_call" | custom-call | flops 43486543872 | bytes 838860800 | tf_op jit(solution)/shard_map/back_both/pallas_call | solution.py:919
  444.7 24.3 %finish.1 = (bf16[2048,1024]{1,0:T(8,128)(2,1)}, f32[2048,1024]{1,0:T(8,128)}, f32[8,1024]{1,0:T(8,128)}, f32[3,1024,256]{2,1,0:T(8,128)}, f32[3,256]{1,0:T(4,12...) custom-call(f32[1024,4608]{1,0:T(8,128)} %get-tuple-element.40.refs_0_, ...), custom_call_target="tpu_custom_call" | custom-call | tf_op jit(solution)/shard_map/finish/pallas_call | solution.py:1568
  469.0 1.4 fusion

commit v11 on v10

--- a/solution.py
+++ b/solution.py
@@ -992,8 +992,8 @@
     sibling = tp_at + 1 - 2 * core
     across = lax.rem(tp_at + 2, 4)
     far_sibling = sibling + across - tp_at
-    straight = w_in.shape[1] // 2
-    in_rows = (w_in.shape[1] - straight) // (2 * places)
+    in_rows = share_in.shape[0]
+    straight = w_in.shape[1] - in_rows * 2 * places
     out_rows = w_out.shape[0] // (2 * places)
     chans = w_in.shape[2]
     rows, width = tokens.shape
@@ -1016,7 +1016,7 @@
 
     def shares(j):
         return (
-            pl.ds(pl.multiple_of(j * in_rows, in_rows), in_rows),
+            pl.ds(pl.multiple_of(j * in_rows, 8), in_rows),
             pl.ds(pl.multiple_of(j * out_rows, out_rows), out_rows),
         )
 
@@ -1060,7 +1060,7 @@
     def straight_rows(q):
         size = straight // STRAIGHT_COPIES
         first = w_in.shape[1] - straight + q * size
-        return pl.ds(pl.multiple_of(first, size), size)
+        return pl.ds(pl.multiple_of(first, 8), size)
 
     def straight_across(q):
         at = straight_rows(q)
@@ -1092,6 +1092,17 @@
         for copy in group:
             copy.wait_send()
 
+    def relay(incoming, j, on_right, on_left):
+        onward = zip(incoming, to_right(j), to_left(j), to_side(j), to_sibling(j))
+        for copy, right, left, aside, near in onward:
+            copy.wait_recv()
+            if on_right:
+                pl.when(place < last)(right.start)
+            if on_left:
+                pl.when(place > 0)(left.start)
+            aside.start()
+            near.start()
+
     def single(i, src, dst, device):
         return remote(src, dst, once.at[0, i], once.at[1, i], device)
 
@@ -1100,7 +1111,8 @@
         share_in[:, g * chans : (g + 1) * chans] = w_in[g, in_at, :].astype(jnp.float32)
     share_out[...] = w_out[out_at, :].astype(jnp.float32)
     start(across_share())
-    own_taps[...] = taps[...]
+    own_taps[...] = jnp.zeros_like(own_taps)
+    own_taps[0:3, :] = taps[...]
     taps_far = single(0, own_taps, far_taps, {"tp": across})
     taps_sib = single(1, own_taps, sib_taps, {"tp": sibling})
     taps_sibfar = single(2, far_taps, sibfar_taps, {"tp": sibling})
@@ -1214,11 +1226,7 @@
     place_shard(own_in, own_out, own_taps, tp_at)
     project(0)
 
-    arrived(across_share())
-    pl.when(place < last)(lambda: start(to_right(here)))
-    pl.when(place > 0)(lambda: start(to_left(here)))
-    start(to_side(here))
-    start(to_sibling(here))
+    relay(across_share(), here, True, True)
     taps_far.wait_recv()
     taps_sibfar.start()
     in_sib.wait_recv()
@@ -1237,18 +1245,12 @@
         @pl.when(place - d >= 0)
         def _():
             j = here - 2 * d
-            arrived(to_right(j))
-            pl.when(place < last)(lambda: start(to_right(j)))
-            start(to_side(j))
-            start(to_sibling(j))
+            relay(to_right(j), j, True, False)
 
         @pl.when(place + d <= last)
         def _():
             j = here + 2 * d
-            arrived(to_left(j))
-            pl.when(place > 0)(lambda: start(to_left(j)))
-            start(to_side(j))
-            start(to_sibling(j))
+            relay(to_left(j), j, False, True)
 
         @pl.when(d == 1)
         def _():
@@ -1410,7 +1412,7 @@
         scratch_shapes=pair * 4
         + [pltpu.VMEM((8, chans), f32)] * 4
         + [
-            pltpu.VMEM((width // 2 // count, 3 * chans), f32),
+            pltpu.VMEM((width * 8 // 16 // count // 8 * 8, 3 * chans), f32),
             pltpu.VMEM((chans // count, width), f32),
             pltpu.VMEM((width, 3 * chans * group), low),
             pltpu.VMEM((chans * group, width), low),
@@ -1440,7 +1442,7 @@
     )(
         w_in.transpose(1, 0, 2),
         w_out,
-        jnp.pad(taps, ((0, 5), (0, 0))),
+        taps,
         gain_mix,
         gain_ffn,
         lengths,
@@ -1450,8 +1452,9 @@
 
 def finish_kernel(slots, chans, hidden, *refs):
     (sums, tokens_in, block_in, lengths) = refs[0:4]
-    (block_out, tokens_out, gains, g_in, g_conv, g_out, g_gate, g_up, g_down) = refs[4:13]
-    (held, tokens, block, rounded, turned, in_sems, block_sems, turn_sems, out_sems) = refs[13:22]
+    (block_out, tokens_out, gain_a, gain_b, g_in, g_conv, g_out, g_gate, g_up, g_down) = refs[4:14]
+    (held, tokens, block, rounded, turned, gains) = refs[14:20]
+    (in_sems, block_sems, turn_sems, out_sems) = refs[20:24]
     rows, width = block_in.shape
     slot_len = rows // slots
     here = lax.axis_index("seq")
@@ -1547,6 +1550,8 @@
         gains[cols(p * LANES, LANES)] = held[8 * p : 8 * p + 8, small_first:]
     own = pl.ds(pl.multiple_of(tp_at * chans, LANES), chans)
     g_conv[...] = gains[2:5, own]
+    gain_a[...] = gains[0:1, :]
+    gain_b[...] = gains[1:2, :]
     for copy in stores:
         copy.wait()
 
@@ -1570,7 +1575,8 @@
         out_shape=[
             jax.ShapeDtypeStruct((rows, width), jnp.bfloat16),
             jax.ShapeDtypeStruct((rows, width), f32),
-            jax.ShapeDtypeStruct((8, width), f32),
+            jax.ShapeDtypeStruct((1, width), f32),
+            jax.ShapeDtypeStruct((1, width), f32),
             jax.ShapeDtypeStruct((3, width, chans), f32),
             jax.ShapeDtypeStruct((3, chans), f32),
             jax.ShapeDtypeStruct((chans, width), f32),
@@ -1579,13 +1585,14 @@
             jax.ShapeDtypeStruct((hidden, width), f32),
         ],
         in_specs=[anywhere] * 3 + [pl.BlockSpec(memory_space=pltpu.SMEM)],
-        out_specs=[anywhere] * 2 + [whole, anywhere, whole] + [anywhere] * 4,
+        out_specs=[anywhere] * 2 + [whole, whole, anywhere, whole] + [anywhere] * 4,
         scratch_shapes=[
             pltpu.VMEM(sums.shape, f32),
             pltpu.VMEM((rows, width), f32),
             pltpu.VMEM((rows, width), f32),
             pltpu.VMEM((rows, width), jnp.bfloat16),
             pltpu.VMEM((hidden, width), f32),
+            pltpu.VMEM((8, width), f32),
             pltpu.SemaphoreType.DMA((6,)),
             pltpu.SemaphoreType.DMA((2, blocks)),
             pltpu.SemaphoreType.DMA((hidden // LANES,)),
@@ -1633,17 +1640,17 @@
         sum_cols,
         1,
     )[:3]
-    block_out, grad_tokens, small, g_in, g_conv, g_out, g_gate, g_up, g_down = finish(
+    block_out, grad_tokens, g_gain_mix, g_gain_ffn, g_in, g_conv, g_out, g_gate, g_up, g_down = finish(
         sums, grad_tokens, block_sum, lengths, chans, w_gate.shape[1]
     )
     return (
         block_out.reshape(slot_count, local_len, width),
         grad_tokens.reshape(slot_count, local_len, width),
-        small[0],
+        g_gain_mix.reshape(width),
         g_in.transpose(1, 0, 2),
         g_conv,
         g_out,
-        small[1],
+        g_gain_ffn.reshape(width),
         g_gate,
         g_up,
         g_down,

time: 471 us -> 465 us (0.987)
  no operation moved by 1% of the time
where the time goes in v11:
time: 465 us
  Pallas kernels  464 us (100%)
    pallas_call x1, Pallas kernels, back_both(): pl.pallas_call(functools.partial(back_kernel, lax.axis_size('seq') // 2,...  373 us
    pallas_call x1, Pallas kernels, mixer_front(): pl.pallas_call(functools.partial(front_kernel, count // 2, slots), out_sh...  66.1 us
    pallas_call x1, Pallas kernels, finish(): pl.pallas_call(functools.partial(finish_kernel, lengths.shape[0], chans,...  24.3 us

profile of v11, /device:TPU:0, one launch (start us, length us, event | category | flops | bytes accessed | tf_op | source)
XLA Modules:
  0.0 464.6 jit_solution(2066134283240394773)
XLA Ops:
  0.6 66.1 %mixer_front.1 = (bf16[1024,3072]{1,0:T(8,128)(2,1)}, bf16[1024,1024]{1,0:T(8,128)(2,1)}, f32[8,1024]{1,0:T(8,128)}, bf16[2048,1024]{1,0:T(8,128)(2,1)}, f32[102...) custom-call(bf16[3,1024,256]{2,1,0:T(8,128)(2,1)} %bitcast.12, ...), custom_call_target="tpu_custom_call" | custom-call | tf_op jit(solution)/shard_map/mixer_front/pallas_call | solution.py:1397
  66.8 373.4 %back_both.1 = (f32[1024,4608]{1,0:T(8,128)}, f32[2048,1024]{1,0:T(8,128)}, f32[2048,1024]{1,0:T(8,128)}, f32[1024,1024]{1,0:T(8,128)}, f32[1024,1024]{1,0:T(8,1...) custom-call(bf16[2048,1024]{1,0:T(8,128)(2,1)} %get-tuple-element.32, ...), custom_call_target="tpu_custom_call" | custom-call | flops 43486543872 | bytes 838860800 | tf_op jit(solution)/shard_map/back_both/pallas_call | solution.py:919
  440.2 24.3 %finish.1 = (bf16[2048,1024]{1,0:T(8,128)(2,1)}, f32[2048,1024]{1,0:T(8,128)}, f32[1,1024]{1,0:T(1,128)}, f32[1,1024]{1,0:T(1,128)}, f32[3,1024,256]{2,1,0:T(8,1...) custom-call(f32[1024,4608]{1,0:T(8,128)} %get-tuple-element.41.refs_, ...), custom_call_target="tpu_custom_call" | custom-call | tf_op jit(solution)/shard_map/finish/pallas_call | solution.py:1573

commit v12 on v11

--- a/solution.py
+++ b/solution.py
@@ -277,7 +277,7 @@
             pl.when(place != root)(lambda: up_left().wait_send())
 
     P_LAGS = (("split", 0, 0), ("up", 2, 1), ("root", 3, 3), ("down", 6, 7), ("end", 9, 9))
-    Q_LAGS = (("up", 1, 0), ("root", 2, 2), ("side", 4, 4), ("down", 6, 7), ("end", 9, 9))
+    Q_LAGS = (("up", 1, 0), ("root", 3, 3), ("side", 4, 4), ("down", 6, 7), ("end", 9, 9))
 
     def tick(self, t, count):
         middle = (self.place == self.places // 2) | (self.place == self.places // 2 - 1)
@@ -982,7 +982,7 @@
     (full_in, full_out, tokens, normed, mixed, out_gate, gates, gated) = refs[30:38]
     (unit_out, unit_in, hidden) = refs[38:41]
     sends, recvs, once, halo_sems, gate_sems, unit_sems, keep_sems, mid_sems = refs[41:49]
-    straight_sems = refs[49]
+    straight_sems, shard_sems = refs[49:51]
     here = lax.axis_index("seq")
     place, side = here // 2, lax.rem(here, 2)
     last = places - 1
@@ -1158,6 +1158,20 @@
 
     order = (tp_at, sibling, across, far_sibling)
 
+    def shard_out(turn, g):
+        at = gate_cols(g, order[turn])
+        return pltpu.make_async_copy(full_in.at[:, at], in_hbm.at[:, at], shard_sems.at[turn, g])
+
+    def gated_out(turn):
+        at = gate_cols(0, order[turn])
+        return pltpu.make_async_copy(
+            gated.at[:, :, at], gated_hbm.at[:, :, at], shard_sems.at[turn, 3]
+        )
+
+    def mixed_out(turn):
+        at = gate_cols(0, order[turn])
+        return pltpu.make_async_copy(mixed.at[:, at], mixed_hbm.at[:, at], shard_sems.at[turn, 4])
+
     def project(turn):
         index = order[turn]
         cols = gate_cols(0, index)
@@ -1185,6 +1199,7 @@
 
         for g in range(3):
             gate_out(turn, index, g).start()
+            shard_out(turn, g).start()
 
         @pl.when(here < end)
         def _():
@@ -1207,6 +1222,9 @@
             tap = [full_taps[j : j + 1, cols] for j in range(3)]
             conv_sum = tap[0] * seen[0] + tap[1] * seen[1] + tap[2] * seen[2]
             mixed[at, cols] = (out_gate[at, cols] * conv_sum).astype(low)
+
+        gated_out(turn).start()
+        mixed_out(turn).start()
 
     @pl.when(here == 0)
     def _():
@@ -1277,16 +1295,10 @@
         straight_sibling(q).wait_recv()
     place_shard(sibfar_in, sibfar_out, sibfar_taps, far_sibling)
     project(3)
-    keep_in = pltpu.make_async_copy(full_in, in_hbm, keep_sems.at[1])
     keep_out = pltpu.make_async_copy(full_out, out_hbm, keep_sems.at[2])
-    keep_in.start()
     keep_out.start()
     convolve(2)
     convolve(3)
-    keep_gated = pltpu.make_async_copy(gated, gated_hbm, keep_sems.at[3])
-    keep_mixed = pltpu.make_async_copy(mixed, mixed_hbm, keep_sems.at[4])
-    keep_gated.start()
-    keep_mixed.start()
     keep_normed.wait()
 
     blocks = rows // OUT_BLOCK
@@ -1331,7 +1343,8 @@
         hidden_copy(k).start()
         mid_copy(1, normed, core, k).start()
 
-    keep_mixed.wait()
+    for turn in range(4):
+        mixed_out(turn).wait()
 
     @pl.loop(0, blocks)
     def _(k):
@@ -1352,9 +1365,11 @@
 
     for k in range(max(blocks - 2, 0), blocks):
         hidden_copy(k).wait()
-    keep_in.wait()
     keep_out.wait()
-    keep_gated.wait()
+    for turn in range(4):
+        gated_out(turn).wait()
+        for g in range(3):
+            shard_out(turn, g).wait()
     for turn in range(4):
         for g in range(3):
             if turn >= 2 or g == 1:
@@ -1431,9 +1446,10 @@
             pltpu.SemaphoreType.DMA((2, 4, slots)),
             pltpu.SemaphoreType.DMA((4, 3)),
             pltpu.SemaphoreType.DMA((2, blocks)),
-            pltpu.SemaphoreType.DMA((5,)),
+            pltpu.SemaphoreType.DMA((3,)),
             pltpu.SemaphoreType.DMA((3, blocks)),
             pltpu.SemaphoreType.DMA((4, STRAIGHT_COPIES)),
+            pltpu.SemaphoreType.DMA((4, 5)),
         ],
         compiler_params=pltpu.CompilerParams(
             collective_id=collective_id, has_side_effects=True, vmem_limit_bytes=VMEM_LIMIT

time: 465 us -> 465 us (level)
  no operation moved by 1% of the time
where the time goes in v12:
time: 465 us; the launch traced here: 464 us
  Pallas kernels  464 us (100%)
    pallas_call x1, Pallas kernels, back_both(): pl.pallas_call(functools.partial(back_kernel, lax.axis_size('seq') // 2,...  375 us
    pallas_call x1, Pallas kernels, mixer_front(): pl.pallas_call(functools.partial(front_kernel, count // 2, slots), out_sh...  64.1 us
    pallas_call x1, Pallas kernels, finish(): pl.pallas_call(functools.partial(finish_kernel, lengths.shape[0], chans,...  24.3 us

profile of v12, /device:TPU:0, one launch (start us, length us, event | category | flops | bytes accessed | tf_op | source)
XLA Modules:
  0.0 464.4 jit_solution(11135758179234675063)
XLA Ops:
  0.6 64.1 %mixer_front.1 = (bf16[1024,3072]{1,0:T(8,128)(2,1)}, bf16[1024,1024]{1,0:T(8,128)(2,1)}, f32[8,1024]{1,0:T(8,128)}, bf16[2048,1024]{1,0:T(8,128)(2,1)}, f32[102...) custom-call(bf16[3,1024,256]{2,1,0:T(8,128)(2,1)} %bitcast.12, ...), custom_call_target="tpu_custom_call" | custom-call | tf_op jit(solution)/shard_map/mixer_front/pallas_call | solution.py:1412
  64.7 375.2 %back_both.1 = (f32[1024,4608]{1,0:T(8,128)}, f32[2048,1024]{1,0:T(8,128)}, f32[2048,1024]{1,0:T(8,128)}, f32[1024,1024]{1,0:T(8,128)}, f32[1024,1024]{1,0:T(8,1...) custom-call(bf16[2048,1024]{1,0:T(8,128)(2,1)} %get-tuple-element.32, ...), custom_call_target="tpu_custom_call" | custom-call | flops 43486543872 | bytes 838860800 | tf_op jit(solution)/shard_map/back_both/pallas_call | solution.py:919
  440.0 24.3 %finish.1 = (bf16[2048,1024]{1,0:T(8,128)(2,1)}, f32[2048,1024]{1,0:T(8,128)}, f32[1,1024]{1,0:T(1,128)}, f32[1,1024]{1,0:T(1,128)}, f32[3,1024,256]{2,1,0:T(8,1...) custom-call(f32[1024,4608]{1,0:T(8,128)} %get-tuple-element.41.refs_, ...), custom_call_target="tpu_custom_call" | custom-call | tf_op jit(solution)/shard_map/finish/pallas_call | solution.py:1589

commit v13 on v11

--- a/solution.py
+++ b/solution.py
@@ -277,11 +277,16 @@
             pl.when(place != root)(lambda: up_left().wait_send())
 
     P_LAGS = (("split", 0, 0), ("up", 2, 1), ("root", 3, 3), ("down", 6, 7), ("end", 9, 9))
-    Q_LAGS = (("up", 1, 0), ("root", 2, 2), ("side", 4, 4), ("down", 6, 7), ("end", 9, 9))
+    Q_LAGS = (("up", 1, 0), ("root", 3, 3), ("side", 4, 4), ("down", 6, 7), ("end", 9, 9))
 
     def tick(self, t, count):
         middle = (self.place == self.places // 2) | (self.place == self.places // 2 - 1)
-        for stage, lags in ((self.p_stage, self.P_LAGS), (self.q_stage, self.Q_LAGS)):
+        for stage, lags in (
+            (self.p_stage, self.P_LAGS[:-1]),
+            (self.q_stage, self.Q_LAGS[:-1]),
+            (self.p_stage, self.P_LAGS[-1:]),
+            (self.q_stage, self.Q_LAGS[-1:]),
+        ):
             for which, mid_lag, outer_lag in lags:
                 k = t - jnp.where(middle, mid_lag, outer_lag)
 

time: 465 us -> 466 us (level)
  no operation moved by 1% of the time
where the time goes in v13:
time: 466 us; the launch traced here: 465 us
  Pallas kernels  464 us (100%)
    pallas_call x1, Pallas kernels, back_both(): pl.pallas_call(functools.partial(back_kernel, lax.axis_size('seq') // 2,...  374 us
    pallas_call x1, Pallas kernels, mixer_front(): pl.pallas_call(functools.partial(front_kernel, count // 2, slots), out_sh...  66.1 us
    pallas_call x1, Pallas kernels, finish(): pl.pallas_call(functools.partial(finish_kernel, lengths.shape[0], chans,...  24.3 us

profile of v13, /device:TPU:0, one launch (start us, length us, event | category | flops | bytes accessed | tf_op | source)
XLA Modules:
  0.0 465.3 jit_solution(1531453011689142808)
XLA Ops:
  0.6 66.1 %mixer_front.1 = (bf16[1024,3072]{1,0:T(8,128)(2,1)}, bf16[1024,1024]{1,0:T(8,128)(2,1)}, f32[8,1024]{1,0:T(8,128)}, bf16[2048,1024]{1,0:T(8,128)(2,1)}, f32[102...) custom-call(bf16[3,1024,256]{2,1,0:T(8,128)(2,1)} %bitcast.12, ...), custom_call_target="tpu_custom_call" | custom-call | tf_op jit(solution)/shard_map/mixer_front/pallas_call | solution.py:1402
  66.8 374.1 %back_both.1 = (f32[1024,4608]{1,0:T(8,128)}, f32[2048,1024]{1,0:T(8,128)}, f32[2048,1024]{1,0:T(8,128)}, f32[1024,1024]{1,0:T(8,128)}, f32[1024,1024]{1,0:T(8,1...) custom-call(bf16[2048,1024]{1,0:T(8,128)(2,1)} %get-tuple-element.32, ...), custom_call_target="tpu_custom_call" | custom-call | flops 43486543872 | bytes 838860800 | tf_op jit(solution)/shard_map/back_both/pallas_call | solution.py:924
  440.9 24.3 %finish.1 = (bf16[2048,1024]{1,0:T(8,128)(2,1)}, f32[2048,1024]{1,0:T(8,128)}, f32[1,1024]{1,0:T(1,128)}, f32[1,1024]{1,0:T(1,128)}, f32[3,1024,256]{2,1,0:T(8,1...) custom-call(f32[1024,4608]{1,0:T(8,128)} %get-tuple-element.41.refs_, ...), custom_call_target="tpu_custom_call" | custom-call | tf_op jit(solution)/shard_map/finish/pallas_call | solution.py:1578
